TPU v7x, 32 devices: a whole 2x2x4 slice. The times are simulated.
32 devices in a mesh: fsdp: 16 (over z, y, x), ctx: 2 (over core).
Axes of the slice: x: 2, y: 2, z: 4, core: 2. Of those that a mesh axis runs over, the one named last changes fastest.
Arguments:
- hidden_states: bfloat16 [16, 768, 4096], P('fsdp', 'ctx'), may hold values from -20.4 to 20.4
- qkv_weight: bfloat16 [4096, 768], P('fsdp'), may hold values from -0.09375 to 0.09375
- doc_ids: int32 [16, 768], P('fsdp', 'ctx'), may hold values from 0 to 1, never falling along the last dimension, each value on 1 to 576 neighbouring positions
Outputs:
- context: bfloat16 [16, 768, 512], P('fsdp', 'ctx')
Inputs may be any that keep to these rules, and one draw needn't show every extreme that they name: `doc_ids`: each sequence holds two documents one after the other, numbered 0 then 1, never falling; the first has 192 to 576 tokens and the second the rest.
All inputs are finite; a program needn't handle non-finite values.
Results may differ from a plain program's by a relative error of at most 0.012.
The roundings to bfloat16 on the way count: a program that leaves them out, or rounds other values in their place, can miss the bound.
Values may be sent and summed in bfloat16 or wider, within the bound.
No kernel may reach another device: no remote copies, remote signals or barrier semaphores. Data moves between devices by JAX's collectives and lax.ppermute only.
A program may use at most 64 MiB of HBM per device.

v0:
```python
import math

import jax
import jax.numpy as jnp
from jax import lax
from jax.sharding import PartitionSpec as P

HEADS = 4
HD = 128


THETA = 1000000.0


def shifted(value, axis, steps):
    count = lax.axis_size(axis)
    first, last = (max(0, -steps), min(count, count - steps))
    return lax.ppermute(value, axis, [(source, source + steps) for source in range(first, last)])


def rotary(values_in, positions):
    half_width = values_in.shape[-1] // 2
    frequency = jnp.exp(
        jnp.arange(half_width, dtype=jnp.float32) * (-2.0 * math.log(THETA) / values_in.shape[-1])
    )
    angles = positions * frequency
    cosine = jnp.cos(angles)
    sine_part = jnp.sin(angles)
    lower_half = values_in[..., :half_width]
    upper_half = values_in[..., half_width:]
    return jnp.concatenate(
        [
            lower_half * cosine - upper_half * sine_part,
            upper_half * cosine + lower_half * sine_part,
        ],
        axis=-1,
    )


def body(hidden_states, qkv_weight, doc_ids):
    tokens = hidden_states[0]
    row_count = tokens.shape[0]
    projected = jnp.dot(
        tokens,
        lax.all_gather(qkv_weight, "fsdp", axis=0, tiled=True),
        preferred_element_type=jnp.float32,
    )
    ctx_count = lax.axis_size("ctx")
    ctx_index = lax.axis_index("ctx")
    row_start = ctx_index * row_count
    local_index = jnp.arange(row_count, dtype=jnp.int32)
    query_pos = row_start + local_index
    positions = query_pos.astype(jnp.float32)
    queries = rotary(
        projected[:, : HEADS * HD].reshape(row_count, HEADS, HD), positions[:, None, None]
    ).astype(jnp.bfloat16)
    keys_here = rotary(projected[:, HEADS * HD : (HEADS + 1) * HD], positions[:, None]).astype(
        jnp.bfloat16
    )
    values_here = projected[:, (HEADS + 1) * HD :].astype(jnp.bfloat16)
    docs_wire = doc_ids[0].astype(jnp.bfloat16)
    scale = 1.0 / math.sqrt(HD)

    def attend(state, key_block, value_block, doc_block, key_first):
        running_max, running_sum, running_acc = state
        scores = (
            jnp.einsum("qhd,kd->hqk", queries, key_block, preferred_element_type=jnp.float32)
            * scale
        )
        key_pos = key_first + jnp.arange(key_block.shape[0], dtype=jnp.int32)
        visible = (key_pos[None, :] <= query_pos[:, None]) & (
            doc_block[None, :] == docs_wire[:, None]
        )
        scores = jnp.where(visible[None], scores, -jnp.inf)
        new_max = jnp.maximum(running_max, jnp.max(scores, axis=-1))
        weights = jnp.exp(scores - new_max[..., None])
        factor = jnp.exp(running_max - new_max)
        new_sum = running_sum * factor + jnp.sum(weights, axis=-1)
        update = jnp.einsum(
            "hqk,kd->hqd",
            weights.astype(jnp.bfloat16),
            value_block,
            preferred_element_type=jnp.float32,
        )
        new_acc = running_acc * factor[..., None] + update
        return (new_max, new_sum, new_acc)

    state = (
        jnp.full((HEADS, row_count), -jnp.inf, jnp.float32),
        jnp.zeros((HEADS, row_count), jnp.float32),
        jnp.zeros((HEADS, row_count, HD), jnp.float32),
    )
    state = attend(state, keys_here, values_here, docs_wire, row_start)
    travelling = (keys_here, values_here, docs_wire)
    for rotation in range(1, ctx_count):
        travelling = shifted((travelling[0], travelling[1], travelling[2]), "ctx", 1)
        key_first = (ctx_index - rotation) * row_count
        arrived = travelling

        def take_block(current):
            return attend(current, arrived[0], arrived[1], arrived[2], key_first)

        def keep_block(current):
            return current

        state = lax.cond(rotation <= ctx_index, take_block, keep_block, state)
    context = state[2] / state[1][..., None]
    context = jnp.transpose(context.astype(jnp.bfloat16), (1, 0, 2)).reshape(row_count, HEADS * HD)
    return context[None]


def solution(mesh):
    in_specs = (P("fsdp", "ctx", None), P("fsdp", None), P("fsdp", "ctx"))
    out_specs = P("fsdp", "ctx", None)
    return jax.shard_map(body, mesh=mesh, in_specs=in_specs, out_specs=out_specs, check_vma=False)
```

profile of v0, /device:TPU:1, one launch (start us, length us, event | category | flops | bytes accessed | tf_op | source)
XLA Modules:
  0.0 142.6 jit_solution(9244264226109511525)
XLA Ops:
  6.5 0.7 all-gather.2.cloned.1.call-update
  7.3 1.4 %convert_reduce_fusion = bf16[384]{0:T(512)(128)(2,1)} fusion(s32[1,384]{1,0:T(1,128)} %param.7), kind=kLoop, calls=%fused_computation.49 | loop fusion | flops 384 | bytes 2304 | tf_op jit(solution)/shard_map/convert_element_type | solution.py:61
  8.7 1.3 collective-permute-start
  10.0 1.5 %compare_and_fusion.1 = pred[384,384]{0,1:T(8,128)(4,1)} fusion(s32[384]{0:T(512)S(1)} %iota_add_fusion.1, bf16[384]{0:T(512)(128)(2,1)} %convert_reduce_fusion), kind=kLoop, calls=%fused_computation.35 | loop fusion | flops 737280 | bytes 149760 | tf_op jit(solution)/shard_map/and | solution.py:71
  11.6 93.6 %all-gather.2.cloned.1.call-done = bf16[4096,768]{1,0:T(8,128)(2,1)} async-done(((bf16[256,768]{1,0:T(8,128)(2,1)}), bf16[4096,768]{1,0:T(8,128)(2,1)}) %all-gather.2.cloned.1.call-update) | async-done | bytes 6291472 | tf_op jit(solution)/shard_map/all_gather | solution.py:45
  105.2 5.4 %fusion.13 = f32[384,768]{1,0:T(8,128)S(1)} fusion(bf16[4096,768]{1,0:T(8,128)(2,1)} %all-gather.2.cloned.1.call-done, bf16[1,384,4096]{2,1,0:T(8,128)(2,1)S(1)} %copy-done), kind=kOutput, calls=%fused_computation.20 | convolution fusion | flops 2415919104 | bytes 10616832 | tf_op jit(solution)/shard_map/dot_general | solution.py:43
  110.6 0.7 slice.39
  111.3 1.0 slice.30
  112.3 1.3 collective-permute-start.2
  113.6 0.8 subtract_convert_fusion.1
  114.5 0.7 pad_maximum_fusion.1
  115.2 1.3 collective-permute-start.1
  116.5 2.3 %reshape.217 = f32[384,4,128]{2,1,0:T(4,128)} reshape(f32[384,512]{1,0:T(8,128)} %slice.30) | data formatting | bytes 1572864 | tf_op jit(solution)/shard_map/reshape | solution.py:55
  118.8 1.8 %fusion.31 = (f32[384,4,64]{2,1,0:T(4,128)S(1)}, f32[384,4,64]{2,1,0:T(4,128)S(1)}) fusion(f32[384,4,128]{2,1,0:T(4,128)} %reshape.217), kind=kLoop, calls=%fused_computation.55 | loop fusion | bytes 1572864 | tf_op jit(solution)/shard_map/slice | solution.py:29
  121.5 1.4 fusion.17
  123.5 2.7 %convolution_add_fusion.1 = f32[4,384,128]{2,1,0:T(8,128)} fusion(f32[384,384,4]{1,0,2:T(8,128)S(1)} %get-tuple-element.93, f32[4,384]{1,0:T(4,128)S(1)} %get-tuple-element.92, pred[384,384]{0,1:T(8,128)(4,1)S(1)} %copy-done.2, f32[4,384]{1,0:T(4,128)S(1)} %get-tuple-element.88, f32[384,768]{1,0:T(8,128)} %copy-done.1), kind=kOutput, calls=%fused_computation.27 | convolution fusion | flops 153550848 | bytes 3403776 | tf_op jit(solution)/shard_map/hqk,kd->hqd/dot_general | solution.py:79
  126.8 6.4 %conditional.1 = ((f32[4,384]{1,0:T(4,128)S(1)}, f32[4,384,128]{2,1,0:T(8,128)})) conditional(s32[]{:T(128)} %convert_element_type.38, (f32[4,384]{1,0:T(4,128)S(1)}, f32[4,384,128]{2,1,0:T(8,128)}) %tuple.15, (s32[]{:T(128)}, s32[]{:T(128)}, s32[384]{0:T(512)}, bf16[384]{0:T(512)(128)(2,1)}, bf16[384]{0:T(512)(128)(2,1)}, ...), branch_computations={%region_2.3_spmd, %region_3.6_spmd} | conditional | flops 309612288 | bytes 16217200 | solution.py:106
  126.8 0.7 iota_add_fusion
  127.4 0.9 compare_and_fusion
  128.3 1.5 %fusion.2 = (f32[4,384]{1,0:T(4,128)S(1)}, f32[384,384,4]{1,0,2:T(8,128)S(1)}) fusion(pred[384,384]{0,1:T(8,128)(4,1)S(1)} %compare_and_fusion, bf16[384,4,128]{2,0,1:T(8,128)(2,1)S(1)} %get-tuple-element.69, bf16[384,128]{1,0:T(8,128)(2,1)} %get-tuple-element.68), kind=kOutput, calls=%fused_computation.4 | convolution fusion | flops 152762880 | bytes 3004416 | tf_op jit(solution)/shard_map/cond/branch_1_fun/qhd,kd->hqk/dot_general | solution.py:67
  130.4 1.8 %convolution_add_fusion = f32[4,384,128]{2,1,0:T(8,128)S(1)} fusion(f32[384,384,4]{1,0,2:T(8,128)S(1)} %get-tuple-element.79, f32[4,384]{1,0:T(4,128)S(1)} %max.3, pred[384,384]{0,1:T(8,128)(4,1)S(1)} %compare_and_fusion, f32[4,384,128]{2,1,0:T(8,128)S(1)} %copy-done.3, f32[4,384]{1,0:T(4,128)S(1)} %get-tuple-element.77, bf16[384,128]{1,0:T(8,128)(2,1)} %get-tuple-element.71), kind=kOutput, calls=%fused_computation.5 | convolution fusion | flops 153747456 | bytes 4190208 | tf_op jit(solution)/shard_map/cond/branch_1_fun/hqk,kd->hqd/dot_general | solution.py:79
  132.2 0.9 copy-done.4
  133.2 1.4 fusion.23
  134.9 0.9 broadcast_in_dim_reshape.3
  (25 shorter events, 2.9 us)
Async XLA Ops:
  6.5 98.7 %copy-start = (bf16[1,384,4096]{2,1,0:T(8,128)(2,1)S(1)}, bf16[1,384,4096]{2,1,0:T(8,128)(2,1)}, u32[]{:S(2)}) copy-start(bf16[1,384,4096]{2,1,0:T(8,128)(2,1)} %param.5) | copy-start | bytes 9437188
  6.5 98.7 %all-gather.2.cloned.1.call-start = ((), (), s32[]{:S(2)}) async-start(), calls=%async_computation | async-start | bytes 6684672 | tf_op jit(solution)/shard_map/all_gather | solution.py:45
  8.7 117.5 %collective-permute-start = (bf16[384]{0:T(512)(128)(2,1)}, bf16[384]{0:T(512)(128)(2,1)}, u32[]{:S(2)}, u32[]{:S(2)}) collective-permute-start(bf16[384]{0:T(512)(128)(2,1)} %convert_reduce_fusion), channel_id=1, source_target_pairs={{0,1},{2,3},{4,5},{6,7},{8,9},{10,11},{12,13},{14,15},{16,17},{18,... | collective-permute-start | bytes 2312 | tf_op jit(solution)/shard_map/ppermute | solution.py:18
  110.6 3.0 %copy-start.1 = (f32[384,768]{1,0:T(8,128)}, f32[384,768]{1,0:T(8,128)S(1)}, u32[]{:S(2)}) copy-start(f32[384,768]{1,0:T(8,128)S(1)} %fusion.13) | copy-start | bytes 3538948
  112.3 13.8 %collective-permute-start.2 = (bf16[384,128]{1,0:T(8,128)(2,1)}, bf16[384,128]{1,0:T(8,128)(2,1)}, u32[]{:S(2)}, u32[]{:S(2)}) collective-permute-start(bf16[384,128]{1,0:T(8,128)(2,1)} %slice.39), channel_id=1, source_target_pairs={{0,1},{2,3},{4,5},{6,7},{8,9},{10,11},{12,13},{14,15},{16,17},{18,... | collective-permute-start | bytes 294920 | tf_op jit(solution)/shard_map/ppermute | solution.py:18
  115.2 11.0 %collective-permute-start.1 = (bf16[384,128]{1,0:T(8,128)(2,1)}, bf16[384,128]{1,0:T(8,128)(2,1)}, u32[]{:S(2)}, u32[]{:S(2)}) collective-permute-start(bf16[384,128]{1,0:T(8,128)(2,1)} %pad_maximum_fusion.1), channel_id=1, source_target_pairs={{0,1},{2,3},{4,5},{6,7},{8,9},{10,11},{12,13},{14,15},{16,17},{18,... | collective-permute-start | bytes 294920 | tf_op jit(solution)/shard_map/ppermute | solution.py:18
  120.6 0.9 copy-start.2
  128.3 2.1 %copy-start.3 = (f32[4,384,128]{2,1,0:T(8,128)S(1)}, f32[4,384,128]{2,1,0:T(8,128)}, u32[]{:S(2)}) copy-start(f32[4,384,128]{2,1,0:T(8,128)} %get-tuple-element.70) | copy-start | bytes 2359300 | tf_op jit(solution)/shard_map/cond
  132.2 0.9 copy-start.4
Sparse Core Ops, SparseCore 0:
  10.1 95.0 all-gather.1
where the time goes:
time: 143 us
  waiting for transfers between devices  94.4 us (66%)
  between operations  13.5 us (9%)
  matrix products  12.8 us (9%)
  local copies, waits for them, and re-layouts  9.06 us (6%)
  other arithmetic  9 us (6%)
  starting transfers between devices  3.84 us (3%)
    all_gather x1, waiting for transfers between devices, body(): lax.all_gather(qkv_weight, 'fsdp', axis=0, tiled=True)  93.6 us
    dot_general x1, matrix products, body(): jnp.dot(tokens, lax.all_gather(qkv_weight, 'fsdp', axis=0, tiled=True), p...  5.37 us
    dot_general x2, matrix products, attend(): jnp.einsum('hqk,kd->hqd', weights.astype(jnp.bfloat16), value_block, pref...  4.49 us
    ppermute x3, starting transfers between devices, shifted(): lax.ppermute(value, axis, [(source, source + steps) for source in range(f...  3.84 us
    dot_general x2, matrix products, attend(): jnp.einsum('qhd,kd->hqk', queries, key_block, preferred_element_type=jnp....  2.92 us
  transfers between devices with their start and end apart: 4, of which 1 were waited for; matrix products, arithmetic and copies ran while one was open for 15% of the time, Pallas kernels for 0%

commit v1 on v0

--- a/solution.py
+++ b/solution.py
@@ -1,8 +1,11 @@
+import functools
 import math
 
 import jax
 import jax.numpy as jnp
 from jax import lax
+from jax.experimental import pallas as pl
+from jax.experimental.pallas import tpu as pltpu
 from jax.sharding import PartitionSpec as P
 
 HEADS = 4
@@ -10,6 +13,8 @@
 
 
 THETA = 1000000.0
+
+VMEM_LIMIT = 40 * 1024 * 1024
 
 
 def shifted(value, axis, steps):
@@ -37,7 +42,7 @@
     )
 
 
-def body(hidden_states, qkv_weight, doc_ids):
+def ring_body(hidden_states, qkv_weight, doc_ids):
     tokens = hidden_states[0]
     row_count = tokens.shape[0]
     projected = jnp.dot(
@@ -58,7 +63,7 @@
         jnp.bfloat16
     )
     values_here = projected[:, (HEADS + 1) * HD :].astype(jnp.bfloat16)
-    docs_wire = doc_ids[0].astype(jnp.bfloat16)
+    docs_wire = doc_ids[0]
     scale = 1.0 / math.sqrt(HD)
 
     def attend(state, key_block, value_block, doc_block, key_first):
@@ -109,7 +114,245 @@
     return context[None]
 
 
+def flip(value, first_mask, second_mask):
+    count = lax.axis_size("fsdp")
+    pairs = []
+    for chip in range(count):
+        pairs.append((chip * 2, (chip ^ first_mask) * 2))
+        pairs.append((chip * 2 + 1, (chip ^ second_mask) * 2 + 1))
+    return lax.ppermute(value, ("fsdp", "ctx"), pairs)
+
+
+def swap(value):
+    return lax.ppermute(value, "ctx", [(0, 1), (1, 0)])
+
+
+def after(value, *others):
+    return lax.optimization_barrier((value,) + others)[0]
+
+
+def add_blocks(total, parts, masks, mine_ref, other_ref, held, sems):
+    rows = parts[0].shape[0]
+    chip = lax.axis_index("fsdp")
+    core = lax.axis_index("ctx")
+    copies = []
+    for place, (first_mask, second_mask) in enumerate(masks):
+        source = jnp.where(core == 0, chip ^ first_mask, chip ^ second_mask)
+        columns = pl.ds(pl.multiple_of(source * rows, rows), rows)
+        for side, ref in enumerate((mine_ref, other_ref)):
+            copy = pltpu.make_async_copy(
+                ref.at[:, columns], held.at[side, place], sems.at[side, place]
+            )
+            copy.start()
+            copies.append(copy)
+    sums = [None, None] if total is None else [total[0], total[1]]
+    for place, part in enumerate(parts):
+        weights = part[...]
+        for side in range(2):
+            copies[place * 2 + side].wait()
+            term = jnp.dot(held[side, place], weights, preferred_element_type=jnp.float32)
+            sums[side] = term if sums[side] is None else sums[side] + term
+    return sums
+
+
+def partial_kernel(masks, begun, *refs):
+    count = len(masks)
+    mine_ref, other_ref = refs[:2]
+    parts = refs[2 : 2 + count]
+    rest = refs[2 + count :]
+    total = None
+    if begun:
+        total, rest = rest[0], rest[1:]
+    out_ref, held, sems = rest
+    sums = add_blocks(total, parts, masks, mine_ref, other_ref, held, sems)
+    out_ref[0] = sums[0]
+    out_ref[1] = sums[1]
+
+
+def final_kernel(masks, *refs):
+    count = len(masks)
+    mine_ref, other_ref = refs[:2]
+    parts = refs[2 : 2 + count]
+    total, cos_ref, sin_ref, keep_ref, send_ref, held, sems = refs[2 + count :]
+    sums = add_blocks(total, parts, masks, mine_ref, other_ref, held, sems)
+    turned = lax.axis_index("ctx") == 0
+
+    def turn(block, cosine, sine):
+        swapped = jnp.concatenate([block[:, HD // 2 :], block[:, : HD // 2]], axis=1)
+        return (block * cosine + swapped * sine).astype(jnp.bfloat16)
+
+    ends = []
+    for side in range(2):
+        cosine, sine = cos_ref[side], sin_ref[side]
+        blocks = [
+            turn(sums[side][:, :HD], cosine, sine),
+            turn(sums[side][:, HD : 2 * HD], cosine, sine),
+            turn(
+                sums[side][:, 2 * HD :],
+                jnp.where(turned, cosine, 1.0),
+                jnp.where(turned, sine, 0.0),
+            ),
+        ]
+        ends.append(blocks)
+    for ref, here, there in ((keep_ref, ends[0], ends[1]), (send_ref, ends[1], ends[0])):
+        ref[:, :HD] = here[0]
+        ref[:, HD : 2 * HD] = here[1]
+        ref[:, 2 * HD : 3 * HD] = here[2]
+        ref[:, 3 * HD :] = there[2]
+
+
+def attention_kernel(keep_ref, recv_ref, docs_q_ref, docs_k_ref, out_ref):
+    core = lax.axis_index("ctx")
+    rows = keep_ref.shape[0]
+    tile = 128
+    kept = jnp.concatenate([keep_ref[:, 3 * HD :], keep_ref[:, 2 * HD : 3 * HD]], axis=0)
+    received = jnp.concatenate([recv_ref[:, 3 * HD :], recv_ref[:, 2 * HD : 3 * HD]], axis=0)
+    keys = jnp.where(core == 0, kept, received)
+    values = jnp.where(core == 0, received, kept)
+    factor = math.log2(math.e) / math.sqrt(HD)
+    kept_first = pl.multiple_of(core * 2 * HD, 2 * HD)
+    recv_first = pl.multiple_of((1 - core) * 2 * HD, 2 * HD)
+    for step in range(rows // tile):
+        here = slice(step * tile, (step + 1) * tile)
+        width = rows + (step + 1) * tile
+        queries = jnp.concatenate(
+            [
+                keep_ref[here, :HD],
+                keep_ref[here, HD : 2 * HD],
+                recv_ref[here, :HD],
+                recv_ref[here, HD : 2 * HD],
+            ],
+            axis=0,
+        )
+        scores = lax.dot_general(
+            queries, keys[:width], (((1,), (1,)), ((), ())), preferred_element_type=jnp.float32
+        )
+        column = lax.broadcasted_iota(jnp.int32, (tile, width), 1)
+        row = lax.broadcasted_iota(jnp.int32, (tile, width), 0) + (rows + step * tile)
+        first = jnp.where(core == 0, rows, 0)
+        visible = (
+            (column <= row) & (column >= first) & (docs_q_ref[here, :] == docs_k_ref[:, :width])
+        )
+        scores = jnp.where(visible[None], scores.reshape(HEADS, tile, width), -jnp.inf)
+        top = jnp.max(scores, axis=-1, keepdims=True)
+        weights = jnp.exp2((scores - top) * factor)
+        totals = jnp.sum(weights, axis=-1, keepdims=True)
+        context = jnp.dot(
+            weights.astype(jnp.bfloat16).reshape(HEADS * tile, width),
+            values[:width],
+            preferred_element_type=jnp.float32,
+        ).reshape(HEADS, tile, HD)
+        context = (context / totals).astype(jnp.bfloat16)
+        for head in range(HEADS // 2):
+            out_ref[here, pl.ds(pl.multiple_of(kept_first + head * HD, HD), HD)] = context[head]
+            out_ref[here, pl.ds(pl.multiple_of(recv_first + head * HD, HD), HD)] = context[
+                head + HEADS // 2
+            ]
+
+
+VMEM = pl.BlockSpec(memory_space=pltpu.VMEM)
+ANY = pl.BlockSpec(memory_space=pl.ANY)
+
+
+def partial(mine, other, parts, masks, total=None, tables=None):
+    rows, width = parts[0].shape
+    tokens = mine.shape[0]
+    count = len(parts)
+    begun = total is not None
+    scratch = [
+        pltpu.VMEM((2, count, tokens, rows), mine.dtype),
+        pltpu.SemaphoreType.DMA((2, count)),
+    ]
+    cost = pl.CostEstimate(
+        flops=4 * tokens * rows * width * count,
+        bytes_accessed=count * rows * (width + 2 * tokens) * 2 + 16 * tokens * width,
+        transcendentals=0,
+    )
+    params = pltpu.CompilerParams(vmem_limit_bytes=VMEM_LIMIT)
+    if tables is None:
+        return pl.pallas_call(
+            functools.partial(partial_kernel, masks, begun),
+            out_shape=jax.ShapeDtypeStruct((2, tokens, width), jnp.float32),
+            in_specs=[ANY, ANY] + [VMEM] * (count + begun),
+            out_specs=VMEM,
+            scratch_shapes=scratch,
+            compiler_params=params,
+            cost_estimate=cost,
+        )(mine, other, *parts, *([total] if begun else []))
+    out = jax.ShapeDtypeStruct((tokens, 4 * HD), jnp.bfloat16)
+    return pl.pallas_call(
+        functools.partial(final_kernel, masks),
+        out_shape=(out, out),
+        in_specs=[ANY, ANY] + [VMEM] * (count + 3),
+        out_specs=(VMEM, VMEM),
+        scratch_shapes=scratch,
+        compiler_params=params,
+        cost_estimate=cost,
+    )(mine, other, *parts, total, *tables)
+
+
+def paired_body(hidden_states, qkv_weight, doc_ids):
+    mine = hidden_states[0]
+    tokens = mine.shape[0]
+    core = lax.axis_index("ctx")
+    own = jnp.concatenate(
+        [
+            lax.dynamic_slice_in_dim(qkv_weight, core * 2 * HD, 2 * HD, 1),
+            lax.dynamic_slice_in_dim(qkv_weight, (HEADS + core) * HD, HD, 1),
+        ],
+        axis=1,
+    )
+
+    near = flip(own, 4, 4)
+    slots = [(own, 0), (near, 4), (flip(own, 8, 8), 8), (flip(after(own, near), 12, 12), 12)]
+    parts, masks = [], []
+    for block, base in slots:
+        one = flip(block, 1, 2)
+        two = flip(block, 2, 1)
+        both = flip(one, 2, 1)
+        parts += [block, one, two, both]
+        masks += [(base, base), (base ^ 1, base ^ 2), (base ^ 2, base ^ 1), (base ^ 3, base ^ 3)]
+
+    other = swap(mine)
+    docs_other = swap(doc_ids)
+    docs_q = doc_ids.reshape(tokens, 1)
+    docs_k = jnp.concatenate([docs_other, doc_ids], axis=1)
+
+    frequency = jnp.exp(
+        jnp.arange(HD // 2, dtype=jnp.float32) * (-2.0 * math.log(THETA) / HD)
+    )
+    starts = jnp.stack([core, 1 - core])[:, None] * tokens
+    positions = (starts + jnp.arange(tokens, dtype=jnp.int32)[None]).astype(jnp.float32)
+    angles = positions[..., None] * frequency
+    cosine, sine = jnp.cos(angles), jnp.sin(angles)
+    cosines = jnp.concatenate([cosine, cosine], axis=-1)
+    sines = jnp.concatenate([-sine, sine], axis=-1)
+
+    mine_in, cosines, sines, docs_q, docs_k = lax.optimization_barrier(
+        (mine, cosines, sines, docs_q, docs_k)
+    )
+    total = partial(mine_in, other, parts[:8], masks[:8])
+    total = partial(mine_in, other, parts[8:15], masks[8:15], total)
+    keep, send = partial(mine_in, other, parts[15:], masks[15:], total, (cosines, sines))
+    recv = swap(send)
+    context = pl.pallas_call(
+        attention_kernel,
+        out_shape=jax.ShapeDtypeStruct((tokens, HEADS * HD), jnp.bfloat16),
+        in_specs=[VMEM] * 4,
+        out_specs=VMEM,
+        compiler_params=pltpu.CompilerParams(vmem_limit_bytes=VMEM_LIMIT),
+        cost_estimate=pl.CostEstimate(
+            flops=8 * HEADS * tokens * tokens * HD,
+            bytes_accessed=tokens * HD * 32,
+            transcendentals=2 * HEADS * tokens * tokens,
+        ),
+    )(keep, recv, docs_q, docs_k)
+    return context[None]
+
+
 def solution(mesh):
     in_specs = (P("fsdp", "ctx", None), P("fsdp", None), P("fsdp", "ctx"))
     out_specs = P("fsdp", "ctx", None)
+    paired = mesh.shape["fsdp"] == 16 and mesh.shape["ctx"] == 2
+    body = paired_body if paired else ring_body
     return jax.shard_map(body, mesh=mesh, in_specs=in_specs, out_specs=out_specs, check_vma=False)

time: 143 us -> 56.9 us (0.40)
  waiting for transfers between devices: 94.4 us -> 16.9 us
  starting transfers between devices: 3.84 us -> 20.7 us
  between operations: 13.5 us -> 0.13 us
  Pallas kernels: 0 us -> 13.2 us
  matrix products: 12.8 us -> 0 us
  other arithmetic: 9 us -> 2.57 us
  local copies, waits for them, and re-layouts: 9.06 us -> 2.78 us
    all_gather x1 -> x0, waiting for transfers between devices: 93.6 us -> none  [body(): lax.all_gather(qkv_weight, 'fsdp', axis=0, tiled=True)]
    ppermute x3 -> x18, waiting for transfers between devices: 0.01 us -> 16.9 us  [the longest x15 14.5 us: flip(): return lax.ppermute(value, ('fsdp', 'ctx'), pairs)]
    ppermute x3 -> x18, starting transfers between devices: 3.84 us -> 20.7 us  [the longest x15 17.3 us: flip(): return lax.ppermute(value, ('fsdp', 'ctx'), pairs)]
    pallas_call x0 -> x4, Pallas kernels: none -> 13.2 us  [the longest x2 8.11 us: partial(): pl.pallas_call(functools.partial(partial_kernel, masks, begun), out_shape...]
    dot_general x5 -> x0, matrix products: 12.8 us -> none  [the longest x1 5.37 us: body(): jnp.dot(tokens, lax.all_gather(qkv_weight, 'fsdp', axis=0, tiled=True), p...]
    slice x3 -> x0, local copies, waits for them, and re-layouts: 3.57 us -> none  [the longest x1 1.84 us: rotary(): lower_half = values_in[..., :half_width]]
    and x2 -> x0, other arithmetic: 2.39 us -> none  [attend(): (key_pos[None, :] <= query_pos[:, None]) & (doc_block[None, :] == docs_wi...]
    reshape x1 -> x0, local copies, waits for them, and re-layouts: 2.3 us -> none  [body(): projected[:, :HEADS * HD].reshape(row_count, HEADS, HD)]
  transfers between devices with their start and end apart: 4 -> 18, of which waited for: 1 -> 9; matrix products, arithmetic and copies ran while one was open for 15% -> 5% of each run, Pallas kernels for 0% -> 14%
where the time goes in v1:
time: 56.9 us; the launch traced here: 56.3 us
  starting transfers between devices  20.7 us (36%)
  waiting for transfers between devices  16.9 us (30%)
  Pallas kernels  13.2 us (23%)
  local copies, waits for them, and re-layouts  2.78 us (5%)
  other arithmetic  2.57 us (5%)
    ppermute x15, starting transfers between devices, flip(): return lax.ppermute(value, ('fsdp', 'ctx'), pairs)  17.3 us
    ppermute x15, waiting for transfers between devices, flip(): return lax.ppermute(value, ('fsdp', 'ctx'), pairs)  14.5 us
    pallas_call x2, Pallas kernels, partial(): pl.pallas_call(functools.partial(partial_kernel, masks, begun), out_shape...  8.11 us
    ppermute x3, starting transfers between devices, swap(): return lax.ppermute(value, 'ctx', [(0, 1), (1, 0)])  3.47 us
    pallas_call x1, Pallas kernels, paired_body(): pl.pallas_call(attention_kernel, out_shape=jax.ShapeDtypeStruct((tokens,...  2.99 us
    unnamed x10, local copies, waits for them, and re-layouts  2.63 us
    ppermute x3, waiting for transfers between devices, swap(): return lax.ppermute(value, 'ctx', [(0, 1), (1, 0)])  2.36 us
    pallas_call x1, Pallas kernels, partial(): pl.pallas_call(functools.partial(final_kernel, masks), out_shape=(out, ou...  2.13 us
  transfers between devices with their start and end apart: 18, of which 9 were waited for; matrix products, arithmetic and copies ran while one was open for 5% of the time, Pallas kernels for 14%

profile of v1, /device:TPU:1, one launch (start us, length us, event | category | flops | bytes accessed | tf_op | source)
XLA Modules:
  0.0 56.3 jit_solution(13006824123393059376)
XLA Ops:
  0.1 0.9 %copy-done = bf16[256,768]{1,0:T(8,128)(2,1)S(1)} copy-done((bf16[256,768]{1,0:T(8,128)(2,1)S(1)}, bf16[256,768]{1,0:T(8,128)(2,1)}, u32[]{:S(2)}) %copy-start) | copy-done | bytes 393240
  1.0 0.7 %pad_maximum_fusion.2.refs_2_ = bf16[256,384]{1,0:T(8,128)(2,1)} fusion(bf16[256,128]{1,0:T(8,128)(2,1)S(1)} %constant_dynamic-slice_fusion, bf16[256,256]{1,0:T(8,128)(2,1)S(1)} %constant_dynamic-slice_fusion.1), kind=kLoop, calls=%fused_computation.4 | loop fusion | flops 393216 | bytes 393216 | tf_op jit(solution)/shard_map/concatenate | solution.py:298
  1.7 2.1 %collective-permute-start.2 = (bf16[256,384]{1,0:T(8,128)(2,1)}, bf16[256,384]{1,0:T(8,128)(2,1)}, u32[]{:S(2)}, u32[]{:S(2)}) collective-permute-start(bf16[256,384]{1,0:T(8,128)(2,1)} %pad_maximum_fusion.2.refs_2_), channel_id=1, source_target_pairs={{0,8},{1,9},{2,10},{3,11},{4,12},{5,13},{6,14},{7,15},{8,0},{9,1},... | collective-permute-start | bytes 589832 | tf_op jit(solution)/shard_map/ppermute | solution.py:123
  3.8 1.2 %collective-permute-start.11 = (bf16[256,384]{1,0:T(8,128)(2,1)}, bf16[256,384]{1,0:T(8,128)(2,1)}, u32[]{:S(2)}, u32[]{:S(2)}) collective-permute-start(bf16[256,384]{1,0:T(8,128)(2,1)} %pad_maximum_fusion.2.refs_2_), channel_id=1, source_target_pairs={{0,2},{1,5},{2,0},{3,7},{4,6},{5,1},{6,4},{7,3},{8,10},{9,13},{10,... | collective-permute-start | bytes 589832 | tf_op jit(solution)/shard_map/ppermute | solution.py:123
  5.1 1.2 %collective-permute-start.12 = (bf16[256,384]{1,0:T(8,128)(2,1)}, bf16[256,384]{1,0:T(8,128)(2,1)}, u32[]{:S(2)}, u32[]{:S(2)}) collective-permute-start(bf16[256,384]{1,0:T(8,128)(2,1)} %pad_maximum_fusion.2.refs_2_), channel_id=1, source_target_pairs={{0,4},{1,3},{2,6},{3,1},{4,0},{5,7},{6,2},{7,5},{8,12},{9,11},{10,... | collective-permute-start | bytes 589832 | tf_op jit(solution)/shard_map/ppermute | solution.py:123
  6.3 1.5 %collective-permute-start = (s32[1,384]{1,0:T(1,128)}, s32[1,384]{1,0:T(1,128)S(1)}, u32[]{:S(2)}, u32[]{:S(2)}) collective-permute-start(s32[1,384]{1,0:T(1,128)} %param.5), channel_id=1, source_target_pairs={{0,1},{1,0},{2,3},{3,2},{4,5},{5,4},{6,7},{7,6},{8,9},{9,8},{10,11... | collective-permute-start | bytes 4616 | tf_op jit(solution)/shard_map/ppermute | solution.py:127
  7.9 0.9 %collective-permute-done = s32[1,384]{1,0:T(1,128)S(1)} collective-permute-done((s32[1,384]{1,0:T(1,128)}, s32[1,384]{1,0:T(1,128)S(1)}, u32[]{:S(2)}, u32[]{:S(2)}) %collective-permute-start) | collective-permute-done | bytes 1568 | tf_op jit(solution)/shard_map/ppermute | solution.py:127
  8.8 2.3 %collective-permute-start.6 = (bf16[256,384]{1,0:T(8,128)(2,1)}, bf16[256,384]{1,0:T(8,128)(2,1)S(1)}, u32[]{:S(2)}, u32[]{:S(2)}) collective-permute-start(bf16[256,384]{1,0:T(8,128)(2,1)} %pad_maximum_fusion.2.refs_2_), channel_id=1, source_target_pairs={{0,16},{1,17},{2,18},{3,19},{4,20},{5,21},{6,22},{7,23},{8,24},{9,... | collective-permute-start | bytes 589832 | tf_op jit(solution)/shard_map/ppermute | solution.py:123
  12.1 2.3 %collective-permute-start.3 = (bf16[256,384]{1,0:T(8,128)(2,1)}, bf16[256,384]{1,0:T(8,128)(2,1)S(1)}, u32[]{:S(2)}, u32[]{:S(2)}) collective-permute-start(bf16[256,384]{1,0:T(8,128)(2,1)} %pad_maximum_fusion.2.refs_2_), channel_id=1, source_target_pairs={{0,24},{1,25},{2,26},{3,27},{4,28},{5,29},{6,30},{7,31},{8,16},{9,... | collective-permute-start | bytes 589832 | tf_op jit(solution)/shard_map/ppermute | solution.py:123
  14.5 10.6 %collective-permute-done.6.refs_2_ = bf16[256,384]{1,0:T(8,128)(2,1)S(1)} collective-permute-done((bf16[256,384]{1,0:T(8,128)(2,1)}, bf16[256,384]{1,0:T(8,128)(2,1)S(1)}, u32[]{:S(2)}, u32[]{:S(2)}) %collective-permute-start.6) | collective-permute-done | bytes 196640 | tf_op jit(solution)/shard_map/ppermute | solution.py:123
  25.3 1.4 %collective-permute-start.16 = (bf16[256,384]{1,0:T(8,128)(2,1)S(1)}, bf16[256,384]{1,0:T(8,128)(2,1)S(1)}, u32[]{:S(2)}, u32[]{:S(2)}) collective-permute-start(bf16[256,384]{1,0:T(8,128)(2,1)S(1)} %collective-permute-done.14.refs_7_), channel_id=1, source_target_pairs={{0,4},{1,3},{2,6},{3,1},{4,0},{5,7},{6,2},{7,5},{8,12},{9,11},{10,... | collective-permute-start | bytes 589832 | tf_op jit(solution)/shard_map/ppermute | solution.py:123
  26.7 1.4 %fusion = (f32[2,384,64]{2,1,0:T(8,128)S(1)}, f32[2,384,64]{2,1,0:T(8,128)S(1)}, f32[2,384,64]{2,1,0:T(8,128)S(1)}) fusion(f32[64]{0:T(128)S(1)} %multiply_exponential_fusion, f32[2,384]{1,0:T(2,128)S(1)} %add_convert_fusion), kind=kLoop, calls=%fused_computation.5 | loop fusion | flops 98304 | bytes 593152 | tf_op jit(solution)/shard_map/neg | solution.py:329
  28.1 1.5 %collective-permute-start.4 = (bf16[256,384]{1,0:T(8,128)(2,1)S(1)}, bf16[256,384]{1,0:T(8,128)(2,1)S(1)}, u32[]{:S(2)}, u32[]{:S(2)}) collective-permute-start(bf16[256,384]{1,0:T(8,128)(2,1)S(1)} %collective-permute-done.3.refs_6_), channel_id=1, source_target_pairs={{0,2},{1,5},{2,0},{3,7},{4,6},{5,1},{6,4},{7,3},{8,10},{9,13},{10,... | collective-permute-start | bytes 589832 | tf_op jit(solution)/shard_map/ppermute | solution.py:123
  31.1 2.2 %collective-permute-start.10 = (bf16[256,384]{1,0:T(8,128)(2,1)S(1)}, bf16[256,384]{1,0:T(8,128)(2,1)S(1)}, u32[]{:S(2)}, u32[]{:S(2)}) collective-permute-start(bf16[256,384]{1,0:T(8,128)(2,1)S(1)} %collective-permute-done.3.refs_6_), channel_id=1, source_target_pairs={{0,4},{1,3},{2,6},{3,1},{4,0},{5,7},{6,2},{7,5},{8,12},{9,11},{10,... | collective-permute-start | bytes 589832 | tf_op jit(solution)/shard_map/ppermute | solution.py:123
  33.2 1.5 %collective-permute-done.16.refs_9_ = bf16[256,384]{1,0:T(8,128)(2,1)S(1)} collective-permute-done((bf16[256,384]{1,0:T(8,128)(2,1)S(1)}, bf16[256,384]{1,0:T(8,128)(2,1)S(1)}, u32[]{:S(2)}, u32[]{:S(2)}) %collective-permute-start.16) | collective-permute-done | bytes 196640 | tf_op jit(solution)/shard_map/ppermute | solution.py:123
  35.3 2.2 %collective-permute-start.5 = (bf16[256,384]{1,0:T(8,128)(2,1)S(1)}, bf16[256,384]{1,0:T(8,128)(2,1)S(1)}, u32[]{:S(2)}, u32[]{:S(2)}) collective-permute-start(bf16[256,384]{1,0:T(8,128)(2,1)S(1)} %collective-permute-done.4.refs_7_), channel_id=1, source_target_pairs={{0,4},{1,3},{2,6},{3,1},{4,0},{5,7},{6,2},{7,5},{8,12},{9,11},{10,... | collective-permute-start | bytes 589832 | tf_op jit(solution)/shard_map/ppermute | solution.py:123
  37.5 4.9 %shard_map.37.refs_9_ = f32[2,384,384]{2,1,0:T(8,128)S(1)} custom-call(bf16[384,4096]{1,0:T(8,128)(2,1)S(1)} %bitcast.6, bf16[384,4096]{1,0:T(8,128)(2,1)} %collective-permute-done.1.refs_1_, bf16[256,384]{1,0:T(8,128)(2,1)} %pad_maximum_fusion.2.refs_2_, bf16[256,384]{1,0:T(8,128)(2,1)} %collective-permute-done.11.refs_3_, ...), custom_call_target="tpu_custom_call" | custom-call | flops 1207959552 | bytes 7077888 | tf_op jit(solution)/shard_map/pallas_call | solution.py:273
  42.8 3.2 %shard_map.38.refs_3_ = f32[2,384,384]{2,1,0:T(8,128)S(1)} custom-call(bf16[384,4096]{1,0:T(8,128)(2,1)S(1)} %bitcast.7, bf16[384,4096]{1,0:T(8,128)(2,1)} %collective-permute-done.1.refs_1_, bf16[256,384]{1,0:T(8,128)(2,1)S(1)} %collective-permute-done.6.refs_2_, bf16[256,384]{1,0:T(8,128)(2,1)S(1)} %collective-permute-done.7.refs_3_, ...), custom_call_target="tpu_custom_call" | custom-call | flops 1056964608 | bytes 6488064 | tf_op jit(solution)/shard_map/pallas_call | solution.py:273
  46.0 2.1 %shard_map.39 = (bf16[384,512]{1,0:T(8,128)(2,1)S(1)}, bf16[384,512]{1,0:T(8,128)(2,1)}) custom-call(bf16[384,4096]{1,0:T(8,128)(2,1)S(1)} %bitcast.8, bf16[384,4096]{1,0:T(8,128)(2,1)} %collective-permute-done.1.refs_1_, bf16[256,384]{1,0:T(8,128)(2,1)S(1)} %collective-permute-done.5.refs_2_, f32[2,384,384]{2,1,0:T(8,128)S(1)} %shard_map.38.refs_3_, ...), custom_call_target="tpu_custom_call" | custom-call | flops 150994944 | bytes 2949120 | tf_op jit(solution)/shard_map/pallas_call | solution.py:283
  48.2 0.7 %copy-done.2 = bf16[384,512]{1,0:T(8,128)(2,1)} copy-done((bf16[384,512]{1,0:T(8,128)(2,1)}, bf16[384,512]{1,0:T(8,128)(2,1)S(1)}, u32[]{:S(2)}) %copy-start.2) | copy-done | bytes 393240
  48.9 1.9 %collective-permute-start.17 = (bf16[384,512]{1,0:T(8,128)(2,1)}, bf16[384,512]{1,0:T(8,128)(2,1)S(1)}, u32[]{:S(2)}, u32[]{:S(2)}) collective-permute-start(bf16[384,512]{1,0:T(8,128)(2,1)} %get-tuple-element.18), channel_id=1, source_target_pairs={{0,1},{1,0},{2,3},{3,2},{4,5},{5,4},{6,7},{7,6},{8,9},{9,8},{10,11... | collective-permute-start | bytes 1179656 | tf_op jit(solution)/shard_map/ppermute | solution.py:127
  50.9 1.4 %collective-permute-done.17.recv_ref = bf16[384,512]{1,0:T(8,128)(2,1)S(1)} collective-permute-done((bf16[384,512]{1,0:T(8,128)(2,1)}, bf16[384,512]{1,0:T(8,128)(2,1)S(1)}, u32[]{:S(2)}, u32[]{:S(2)}) %collective-permute-start.17) | collective-permute-done | bytes 393248 | tf_op jit(solution)/shard_map/ppermute | solution.py:127
  52.4 1.0 %copy-done.3 = bf16[384,512]{1,0:T(8,128)(2,1)S(1)} copy-done((bf16[384,512]{1,0:T(8,128)(2,1)S(1)}, bf16[384,512]{1,0:T(8,128)(2,1)}, u32[]{:S(2)}) %copy-start.3) | copy-done | bytes 393240
  53.4 3.0 %shard_map.40 = bf16[384,512]{1,0:T(8,128)(2,1)} custom-call(bf16[384,512]{1,0:T(8,128)(2,1)S(1)} %copy-done.3, bf16[384,512]{1,0:T(8,128)(2,1)S(1)} %collective-permute-done.17.recv_ref, s32[384,1]{1,0:T(8,128)S(1)} %copy.4.docs_q_ref, s32[1,768]{1,0:T(1,128)S(1)} %pad_add_fusion.docs_k_ref), custom_call_target="tpu_custom_call" | custom-call | flops 603979776 | bytes 1572864 | tf_op jit(solution)/shard_map/pallas_call | solution.py:338
  (36 shorter events, 4.0 us)
Async XLA Ops:
  0.0 1.0 %copy-start = (bf16[256,768]{1,0:T(8,128)(2,1)S(1)}, bf16[256,768]{1,0:T(8,128)(2,1)}, u32[]{:S(2)}) copy-start(bf16[256,768]{1,0:T(8,128)(2,1)} %param.4) | copy-start | bytes 1179652
  0.0 37.5 %copy-start.1 = (bf16[1,384,4096]{2,1,0:T(8,128)(2,1)S(1)}, bf16[1,384,4096]{2,1,0:T(8,128)(2,1)}, u32[]{:S(2)}) copy-start(bf16[1,384,4096]{2,1,0:T(8,128)(2,1)} %param.3) | copy-start | bytes 9437188
  0.0 34.7 %copy-start.4 = (s32[1,384]{1,0:T(1,128)S(1)}, s32[1,384]{1,0:T(1,128)}, u32[]{:S(2)}) copy-start(s32[1,384]{1,0:T(1,128)} %param.5) | copy-start | bytes 4612
  0.0 37.4 %collective-permute-start.1 = (bf16[384,4096]{1,0:T(8,128)(2,1)}, bf16[384,4096]{1,0:T(8,128)(2,1)}, u32[]{:S(2)}, u32[]{:S(2)}) collective-permute-start(bf16[384,4096]{1,0:T(8,128)(2,1)} %bitcast.5), channel_id=1, source_target_pairs={{0,1},{1,0},{2,3},{3,2},{4,5},{5,4},{6,7},{7,6},{8,9},{9,8},{10,11... | collective-permute-start | bytes 9437192 | tf_op jit(solution)/shard_map/ppermute | solution.py:127
  1.7 9.4 %collective-permute-start.2 = (bf16[256,384]{1,0:T(8,128)(2,1)}, bf16[256,384]{1,0:T(8,128)(2,1)}, u32[]{:S(2)}, u32[]{:S(2)}) collective-permute-start(bf16[256,384]{1,0:T(8,128)(2,1)} %pad_maximum_fusion.2.refs_2_), channel_id=1, source_target_pairs={{0,8},{1,9},{2,10},{3,11},{4,12},{5,13},{6,14},{7,15},{8,0},{9,1},... | collective-permute-start | bytes 589832 | tf_op jit(solution)/shard_map/ppermute | solution.py:123
  3.8 7.5 %collective-permute-start.11 = (bf16[256,384]{1,0:T(8,128)(2,1)}, bf16[256,384]{1,0:T(8,128)(2,1)}, u32[]{:S(2)}, u32[]{:S(2)}) collective-permute-start(bf16[256,384]{1,0:T(8,128)(2,1)} %pad_maximum_fusion.2.refs_2_), channel_id=1, source_target_pairs={{0,2},{1,5},{2,0},{3,7},{4,6},{5,1},{6,4},{7,3},{8,10},{9,13},{10,... | collective-permute-start | bytes 589832 | tf_op jit(solution)/shard_map/ppermute | solution.py:123
  5.1 7.1 %collective-permute-start.12 = (bf16[256,384]{1,0:T(8,128)(2,1)}, bf16[256,384]{1,0:T(8,128)(2,1)}, u32[]{:S(2)}, u32[]{:S(2)}) collective-permute-start(bf16[256,384]{1,0:T(8,128)(2,1)} %pad_maximum_fusion.2.refs_2_), channel_id=1, source_target_pairs={{0,4},{1,3},{2,6},{3,1},{4,0},{5,7},{6,2},{7,5},{8,12},{9,11},{10,... | collective-permute-start | bytes 589832 | tf_op jit(solution)/shard_map/ppermute | solution.py:123
  6.3 2.5 %collective-permute-start = (s32[1,384]{1,0:T(1,128)}, s32[1,384]{1,0:T(1,128)S(1)}, u32[]{:S(2)}, u32[]{:S(2)}) collective-permute-start(s32[1,384]{1,0:T(1,128)} %param.5), channel_id=1, source_target_pairs={{0,1},{1,0},{2,3},{3,2},{4,5},{5,4},{6,7},{7,6},{8,9},{9,8},{10,11... | collective-permute-start | bytes 4616 | tf_op jit(solution)/shard_map/ppermute | solution.py:127
  8.8 16.3 %collective-permute-start.6 = (bf16[256,384]{1,0:T(8,128)(2,1)}, bf16[256,384]{1,0:T(8,128)(2,1)S(1)}, u32[]{:S(2)}, u32[]{:S(2)}) collective-permute-start(bf16[256,384]{1,0:T(8,128)(2,1)} %pad_maximum_fusion.2.refs_2_), channel_id=1, source_target_pairs={{0,16},{1,17},{2,18},{3,19},{4,20},{5,21},{6,22},{7,23},{8,24},{9,... | collective-permute-start | bytes 589832 | tf_op jit(solution)/shard_map/ppermute | solution.py:123
  11.2 14.1 %collective-permute-start.14 = (bf16[256,384]{1,0:T(8,128)(2,1)}, bf16[256,384]{1,0:T(8,128)(2,1)S(1)}, u32[]{:S(2)}, u32[]{:S(2)}) collective-permute-start(bf16[256,384]{1,0:T(8,128)(2,1)} %collective-permute-done.2.refs_6_), channel_id=1, source_target_pairs={{0,2},{1,5},{2,0},{3,7},{4,6},{5,1},{6,4},{7,3},{8,10},{9,13},{10,... | collective-permute-start | bytes 589832 | tf_op jit(solution)/shard_map/ppermute | solution.py:123
  11.4 13.9 %collective-permute-start.15 = (bf16[256,384]{1,0:T(8,128)(2,1)}, bf16[256,384]{1,0:T(8,128)(2,1)S(1)}, u32[]{:S(2)}, u32[]{:S(2)}) collective-permute-start(bf16[256,384]{1,0:T(8,128)(2,1)} %collective-permute-done.2.refs_6_), channel_id=1, source_target_pairs={{0,4},{1,3},{2,6},{3,1},{4,0},{5,7},{6,2},{7,5},{8,12},{9,11},{10,... | collective-permute-start | bytes 589832 | tf_op jit(solution)/shard_map/ppermute | solution.py:123
  12.1 16.0 %collective-permute-start.3 = (bf16[256,384]{1,0:T(8,128)(2,1)}, bf16[256,384]{1,0:T(8,128)(2,1)S(1)}, u32[]{:S(2)}, u32[]{:S(2)}) collective-permute-start(bf16[256,384]{1,0:T(8,128)(2,1)} %pad_maximum_fusion.2.refs_2_), channel_id=1, source_target_pairs={{0,24},{1,25},{2,26},{3,27},{4,28},{5,29},{6,30},{7,31},{8,16},{9,... | collective-permute-start | bytes 589832 | tf_op jit(solution)/shard_map/ppermute | solution.py:123
  25.1 5.4 %collective-permute-start.13 = (bf16[256,384]{1,0:T(8,128)(2,1)}, bf16[256,384]{1,0:T(8,128)(2,1)S(1)}, u32[]{:S(2)}, u32[]{:S(2)}) collective-permute-start(bf16[256,384]{1,0:T(8,128)(2,1)} %collective-permute-done.11.refs_3_), channel_id=1, source_target_pairs={{0,4},{1,3},{2,6},{3,1},{4,0},{5,7},{6,2},{7,5},{8,12},{9,11},{10,... | collective-permute-start | bytes 589832 | tf_op jit(solution)/shard_map/ppermute | solution.py:123
  25.2 5.8 %collective-permute-start.7 = (bf16[256,384]{1,0:T(8,128)(2,1)S(1)}, bf16[256,384]{1,0:T(8,128)(2,1)S(1)}, u32[]{:S(2)}, u32[]{:S(2)}) collective-permute-start(bf16[256,384]{1,0:T(8,128)(2,1)S(1)} %collective-permute-done.6.refs_2_), channel_id=1, source_target_pairs={{0,2},{1,5},{2,0},{3,7},{4,6},{5,1},{6,4},{7,3},{8,10},{9,13},{10,... | collective-permute-start | bytes 589832 | tf_op jit(solution)/shard_map/ppermute | solution.py:123
  25.3 9.4 %collective-permute-start.16 = (bf16[256,384]{1,0:T(8,128)(2,1)S(1)}, bf16[256,384]{1,0:T(8,128)(2,1)S(1)}, u32[]{:S(2)}, u32[]{:S(2)}) collective-permute-start(bf16[256,384]{1,0:T(8,128)(2,1)S(1)} %collective-permute-done.14.refs_7_), channel_id=1, source_target_pairs={{0,4},{1,3},{2,6},{3,1},{4,0},{5,7},{6,2},{7,5},{8,12},{9,11},{10,... | collective-permute-start | bytes 589832 | tf_op jit(solution)/shard_map/ppermute | solution.py:123
  28.1 7.2 %collective-permute-start.4 = (bf16[256,384]{1,0:T(8,128)(2,1)S(1)}, bf16[256,384]{1,0:T(8,128)(2,1)S(1)}, u32[]{:S(2)}, u32[]{:S(2)}) collective-permute-start(bf16[256,384]{1,0:T(8,128)(2,1)S(1)} %collective-permute-done.3.refs_6_), channel_id=1, source_target_pairs={{0,2},{1,5},{2,0},{3,7},{4,6},{5,1},{6,4},{7,3},{8,10},{9,13},{10,... | collective-permute-start | bytes 589832 | tf_op jit(solution)/shard_map/ppermute | solution.py:123
  30.5 11.8 %collective-permute-start.8 = (bf16[256,384]{1,0:T(8,128)(2,1)S(1)}, bf16[256,384]{1,0:T(8,128)(2,1)S(1)}, u32[]{:S(2)}, u32[]{:S(2)}) collective-permute-start(bf16[256,384]{1,0:T(8,128)(2,1)S(1)} %collective-permute-done.6.refs_2_), channel_id=1, source_target_pairs={{0,4},{1,3},{2,6},{3,1},{4,0},{5,7},{6,2},{7,5},{8,12},{9,11},{10,... | collective-permute-start | bytes 589832 | tf_op jit(solution)/shard_map/ppermute | solution.py:123
  31.1 11.3 %collective-permute-start.10 = (bf16[256,384]{1,0:T(8,128)(2,1)S(1)}, bf16[256,384]{1,0:T(8,128)(2,1)S(1)}, u32[]{:S(2)}, u32[]{:S(2)}) collective-permute-start(bf16[256,384]{1,0:T(8,128)(2,1)S(1)} %collective-permute-done.3.refs_6_), channel_id=1, source_target_pairs={{0,4},{1,3},{2,6},{3,1},{4,0},{5,7},{6,2},{7,5},{8,12},{9,11},{10,... | collective-permute-start | bytes 589832 | tf_op jit(solution)/shard_map/ppermute | solution.py:123
  34.7 8.1 %collective-permute-start.9 = (bf16[256,384]{1,0:T(8,128)(2,1)S(1)}, bf16[256,384]{1,0:T(8,128)(2,1)S(1)}, u32[]{:S(2)}, u32[]{:S(2)}) collective-permute-start(bf16[256,384]{1,0:T(8,128)(2,1)S(1)} %collective-permute-done.7.refs_3_), channel_id=1, source_target_pairs={{0,4},{1,3},{2,6},{3,1},{4,0},{5,7},{6,2},{7,5},{8,12},{9,11},{10,... | collective-permute-start | bytes 589832 | tf_op jit(solution)/shard_map/ppermute | solution.py:123
  35.3 10.7 %collective-permute-start.5 = (bf16[256,384]{1,0:T(8,128)(2,1)S(1)}, bf16[256,384]{1,0:T(8,128)(2,1)S(1)}, u32[]{:S(2)}, u32[]{:S(2)}) collective-permute-start(bf16[256,384]{1,0:T(8,128)(2,1)S(1)} %collective-permute-done.4.refs_7_), channel_id=1, source_target_pairs={{0,4},{1,3},{2,6},{3,1},{4,0},{5,7},{6,2},{7,5},{8,12},{9,11},{10,... | collective-permute-start | bytes 589832 | tf_op jit(solution)/shard_map/ppermute | solution.py:123
  48.2 0.7 %copy-start.2 = (bf16[384,512]{1,0:T(8,128)(2,1)}, bf16[384,512]{1,0:T(8,128)(2,1)S(1)}, u32[]{:S(2)}) copy-start(bf16[384,512]{1,0:T(8,128)(2,1)S(1)} %get-tuple-element.17.keep_ref) | copy-start | bytes 1179652
  48.9 3.4 %collective-permute-start.17 = (bf16[384,512]{1,0:T(8,128)(2,1)}, bf16[384,512]{1,0:T(8,128)(2,1)S(1)}, u32[]{:S(2)}, u32[]{:S(2)}) collective-permute-start(bf16[384,512]{1,0:T(8,128)(2,1)} %get-tuple-element.18), channel_id=1, source_target_pairs={{0,1},{1,0},{2,3},{3,2},{4,5},{5,4},{6,7},{7,6},{8,9},{9,8},{10,11... | collective-permute-start | bytes 1179656 | tf_op jit(solution)/shard_map/ppermute | solution.py:127
  52.4 1.0 %copy-start.3 = (bf16[384,512]{1,0:T(8,128)(2,1)S(1)}, bf16[384,512]{1,0:T(8,128)(2,1)}, u32[]{:S(2)}) copy-start(bf16[384,512]{1,0:T(8,128)(2,1)} %copy-done.2) | copy-start | bytes 1179652

commit v2 on v1

--- a/solution.py
+++ b/solution.py
@@ -14,7 +14,9 @@
 
 THETA = 1000000.0
 
-VMEM_LIMIT = 40 * 1024 * 1024
+TILE = 16
+
+VMEM_LIMIT = 16 * 1024 * 1024
 
 
 def shifted(value, axis, steps):
@@ -131,26 +133,17 @@
     return lax.optimization_barrier((value,) + others)[0]
 
 
-def add_blocks(total, parts, masks, mine_ref, other_ref, held, sems):
+def add_blocks(total, parts, masks, mine_ref, other_ref):
     rows = parts[0].shape[0]
     chip = lax.axis_index("fsdp")
     core = lax.axis_index("ctx")
-    copies = []
-    for place, (first_mask, second_mask) in enumerate(masks):
+    sums = [None, None] if total is None else [total[0], total[1]]
+    for part, (first_mask, second_mask) in zip(parts, masks):
         source = jnp.where(core == 0, chip ^ first_mask, chip ^ second_mask)
         columns = pl.ds(pl.multiple_of(source * rows, rows), rows)
+        weights = part[...]
         for side, ref in enumerate((mine_ref, other_ref)):
-            copy = pltpu.make_async_copy(
-                ref.at[:, columns], held.at[side, place], sems.at[side, place]
-            )
-            copy.start()
-            copies.append(copy)
-    sums = [None, None] if total is None else [total[0], total[1]]
-    for place, part in enumerate(parts):
-        weights = part[...]
-        for side in range(2):
-            copies[place * 2 + side].wait()
-            term = jnp.dot(held[side, place], weights, preferred_element_type=jnp.float32)
+            term = jnp.dot(ref[:, columns], weights, preferred_element_type=jnp.float32)
             sums[side] = term if sums[side] is None else sums[side] + term
     return sums
 
@@ -163,8 +156,8 @@
     total = None
     if begun:
         total, rest = rest[0], rest[1:]
-    out_ref, held, sems = rest
-    sums = add_blocks(total, parts, masks, mine_ref, other_ref, held, sems)
+    (out_ref,) = rest
+    sums = add_blocks(total, parts, masks, mine_ref, other_ref)
     out_ref[0] = sums[0]
     out_ref[1] = sums[1]
 
@@ -173,8 +166,8 @@
     count = len(masks)
     mine_ref, other_ref = refs[:2]
     parts = refs[2 : 2 + count]
-    total, cos_ref, sin_ref, keep_ref, send_ref, held, sems = refs[2 + count :]
-    sums = add_blocks(total, parts, masks, mine_ref, other_ref, held, sems)
+    total, cos_ref, sin_ref, docs_ref, keep_ref, send_ref = refs[2 + count :]
+    sums = add_blocks(total, parts, masks, mine_ref, other_ref)
     turned = lax.axis_index("ctx") == 0
 
     def turn(block, cosine, sine):
@@ -194,21 +187,27 @@
             ),
         ]
         ends.append(blocks)
+    rows = docs_ref.shape[1]
     for ref, here, there in ((keep_ref, ends[0], ends[1]), (send_ref, ends[1], ends[0])):
-        ref[:, :HD] = here[0]
-        ref[:, HD : 2 * HD] = here[1]
-        ref[:, 2 * HD : 3 * HD] = here[2]
-        ref[:, 3 * HD :] = there[2]
-
-
-def attention_kernel(keep_ref, recv_ref, docs_q_ref, docs_k_ref, out_ref):
+        ref[:rows, :HD] = here[0]
+        ref[:rows, HD : 2 * HD] = here[1]
+        ref[:rows, 2 * HD : 3 * HD] = here[2]
+        ref[:rows, 3 * HD :] = there[2]
+        ref[rows:, :] = jnp.zeros((TILE, 4 * HD), ref.dtype)
+        ref[rows:, :rows] = jnp.broadcast_to(docs_ref[...], (TILE, rows)).astype(ref.dtype)
+
+
+def attention_kernel(keep_ref, recv_ref, docs_ref, out_ref):
     core = lax.axis_index("ctx")
-    rows = keep_ref.shape[0]
+    rows = docs_ref.shape[0]
     tile = 128
-    kept = jnp.concatenate([keep_ref[:, 3 * HD :], keep_ref[:, 2 * HD : 3 * HD]], axis=0)
-    received = jnp.concatenate([recv_ref[:, 3 * HD :], recv_ref[:, 2 * HD : 3 * HD]], axis=0)
+    kept = jnp.concatenate([keep_ref[:rows, 3 * HD :], keep_ref[:rows, 2 * HD : 3 * HD]], axis=0)
+    received = jnp.concatenate([recv_ref[:rows, 3 * HD :], recv_ref[:rows, 2 * HD : 3 * HD]], axis=0)
     keys = jnp.where(core == 0, kept, received)
     values = jnp.where(core == 0, received, kept)
+    docs = jnp.concatenate(
+        [recv_ref[rows : rows + 1, :rows], keep_ref[rows : rows + 1, :rows]], axis=1
+    ).astype(jnp.float32)
     factor = math.log2(math.e) / math.sqrt(HD)
     kept_first = pl.multiple_of(core * 2 * HD, 2 * HD)
     recv_first = pl.multiple_of((1 - core) * 2 * HD, 2 * HD)
@@ -231,7 +230,7 @@
         row = lax.broadcasted_iota(jnp.int32, (tile, width), 0) + (rows + step * tile)
         first = jnp.where(core == 0, rows, 0)
         visible = (
-            (column <= row) & (column >= first) & (docs_q_ref[here, :] == docs_k_ref[:, :width])
+            (column <= row) & (column >= first) & (docs_ref[here, :] == docs[:, :width])
         )
         scores = jnp.where(visible[None], scores.reshape(HEADS, tile, width), -jnp.inf)
         top = jnp.max(scores, axis=-1, keepdims=True)
@@ -251,7 +250,24 @@
 
 
 VMEM = pl.BlockSpec(memory_space=pltpu.VMEM)
-ANY = pl.BlockSpec(memory_space=pl.ANY)
+
+
+def stage_kernel(source_ref, out_ref, sem):
+    copy = pltpu.make_async_copy(source_ref, out_ref, sem)
+    copy.start()
+    copy.wait()
+
+
+def stage(value):
+    return pl.pallas_call(
+        stage_kernel,
+        out_shape=jax.ShapeDtypeStruct(value.shape, value.dtype),
+        in_specs=[pl.BlockSpec(memory_space=pl.ANY)],
+        out_specs=VMEM,
+        scratch_shapes=[pltpu.SemaphoreType.DMA],
+        compiler_params=pltpu.CompilerParams(vmem_limit_bytes=VMEM_LIMIT),
+        cost_estimate=pl.CostEstimate(flops=0, bytes_accessed=2 * value.size * 2, transcendentals=0),
+    )(value)
 
 
 def partial(mine, other, parts, masks, total=None, tables=None):
@@ -259,10 +275,6 @@
     tokens = mine.shape[0]
     count = len(parts)
     begun = total is not None
-    scratch = [
-        pltpu.VMEM((2, count, tokens, rows), mine.dtype),
-        pltpu.SemaphoreType.DMA((2, count)),
-    ]
     cost = pl.CostEstimate(
         flops=4 * tokens * rows * width * count,
         bytes_accessed=count * rows * (width + 2 * tokens) * 2 + 16 * tokens * width,
@@ -273,19 +285,17 @@
         return pl.pallas_call(
             functools.partial(partial_kernel, masks, begun),
             out_shape=jax.ShapeDtypeStruct((2, tokens, width), jnp.float32),
-            in_specs=[ANY, ANY] + [VMEM] * (count + begun),
+            in_specs=[VMEM] * (2 + count + begun),
             out_specs=VMEM,
-            scratch_shapes=scratch,
             compiler_params=params,
             cost_estimate=cost,
         )(mine, other, *parts, *([total] if begun else []))
-    out = jax.ShapeDtypeStruct((tokens, 4 * HD), jnp.bfloat16)
+    out = jax.ShapeDtypeStruct((tokens + TILE, 4 * HD), jnp.bfloat16)
     return pl.pallas_call(
         functools.partial(final_kernel, masks),
         out_shape=(out, out),
-        in_specs=[ANY, ANY] + [VMEM] * (count + 3),
+        in_specs=[VMEM] * (count + 6),
         out_specs=(VMEM, VMEM),
-        scratch_shapes=scratch,
         compiler_params=params,
         cost_estimate=cost,
     )(mine, other, *parts, total, *tables)
@@ -303,21 +313,6 @@
         axis=1,
     )
 
-    near = flip(own, 4, 4)
-    slots = [(own, 0), (near, 4), (flip(own, 8, 8), 8), (flip(after(own, near), 12, 12), 12)]
-    parts, masks = [], []
-    for block, base in slots:
-        one = flip(block, 1, 2)
-        two = flip(block, 2, 1)
-        both = flip(one, 2, 1)
-        parts += [block, one, two, both]
-        masks += [(base, base), (base ^ 1, base ^ 2), (base ^ 2, base ^ 1), (base ^ 3, base ^ 3)]
-
-    other = swap(mine)
-    docs_other = swap(doc_ids)
-    docs_q = doc_ids.reshape(tokens, 1)
-    docs_k = jnp.concatenate([docs_other, doc_ids], axis=1)
-
     frequency = jnp.exp(
         jnp.arange(HD // 2, dtype=jnp.float32) * (-2.0 * math.log(THETA) / HD)
     )
@@ -327,18 +322,39 @@
     cosine, sine = jnp.cos(angles), jnp.sin(angles)
     cosines = jnp.concatenate([cosine, cosine], axis=-1)
     sines = jnp.concatenate([-sine, sine], axis=-1)
-
-    mine_in, cosines, sines, docs_q, docs_k = lax.optimization_barrier(
-        (mine, cosines, sines, docs_q, docs_k)
-    )
-    total = partial(mine_in, other, parts[:8], masks[:8])
-    total = partial(mine_in, other, parts[8:15], masks[8:15], total)
-    keep, send = partial(mine_in, other, parts[15:], masks[15:], total, (cosines, sines))
+    docs = doc_ids.reshape(tokens, 1).astype(jnp.float32)
+
+    z1 = flip(own, 4, 4)
+    z2 = flip(own, 8, 8)
+    a0 = flip(own, 1, 2)
+    b0 = flip(own, 2, 1)
+    z3 = flip(z2, 4, 4)
+
+    other = stage(swap(mine))
+    z1, cosines, sines, docs, other = lax.optimization_barrier(
+        (z1, cosines, sines, docs, other)
+    )
+    a1, b1, c0 = flip(z1, 1, 2), flip(z1, 2, 1), flip(a0, 2, 1)
+    a2, b2, c1 = flip(z2, 1, 2), flip(z2, 2, 1), flip(a1, 2, 1)
+    a3, b3, c2 = flip(z3, 1, 2), flip(z3, 2, 1), flip(a2, 2, 1)
+    total = partial(
+        mine,
+        other,
+        [own, a0, b0, c0, z1, a1, b1, z2],
+        [(0, 0), (1, 2), (2, 1), (3, 3), (4, 4), (5, 6), (6, 5), (8, 8)],
+    )
+    a3, total = lax.optimization_barrier((a3, total))
+    c3 = flip(a3, 2, 1)
+    total = partial(
+        mine, other, [c1, a2, b2, z3], [(7, 7), (9, 10), (10, 9), (12, 12)], total
+    )
+    total = partial(mine, other, [c2, a3, b3], [(11, 11), (13, 14), (14, 13)], total)
+    keep, send = partial(mine, other, [c3], [(15, 15)], total, (cosines, sines, doc_ids))
     recv = swap(send)
     context = pl.pallas_call(
         attention_kernel,
         out_shape=jax.ShapeDtypeStruct((tokens, HEADS * HD), jnp.bfloat16),
-        in_specs=[VMEM] * 4,
+        in_specs=[VMEM] * 3,
         out_specs=VMEM,
         compiler_params=pltpu.CompilerParams(vmem_limit_bytes=VMEM_LIMIT),
         cost_estimate=pl.CostEstimate(
@@ -346,7 +362,7 @@
             bytes_accessed=tokens * HD * 32,
             transcendentals=2 * HEADS * tokens * tokens,
         ),
-    )(keep, recv, docs_q, docs_k)
+    )(keep, recv, docs)
     return context[None]
 
 

time: 56.9 us -> 46.8 us (0.82)
  Pallas kernels: 13.2 us -> 8.61 us
  waiting for transfers between devices: 16.9 us -> 14 us
  local copies, waits for them, and re-layouts: 2.78 us -> 1.1 us
  starting transfers between devices: 20.7 us -> 19.2 us
  other arithmetic: 2.57 us -> 3.26 us
    pallas_call x2 -> x3, Pallas kernels: 8.11 us -> 4.85 us  [partial(): pl.pallas_call(functools.partial(partial_kernel, masks, begun), out_shape...]
    ppermute x3 -> x2, starting transfers between devices: 3.47 us -> 0.59 us  [swap(): return lax.ppermute(value, 'ctx', [(0, 1), (1, 0)])]
    ppermute x15, waiting for transfers between devices: 14.5 us -> 12.7 us  [flip(): return lax.ppermute(value, ('fsdp', 'ctx'), pairs)]
    unnamed x10 -> x6, local copies, waits for them, and re-layouts: 2.63 us -> 0.95 us
    pallas_call x1, Pallas kernels: 2.13 us -> 0.54 us  [partial(): pl.pallas_call(functools.partial(final_kernel, masks), out_shape=(out, ou...]
    ppermute x15, starting transfers between devices: 17.3 us -> 18.6 us  [flip(): return lax.ppermute(value, ('fsdp', 'ctx'), pairs)]
    ppermute x3 -> x2, waiting for transfers between devices: 2.36 us -> 1.23 us  [swap(): return lax.ppermute(value, 'ctx', [(0, 1), (1, 0)])]
    convert_element_type x0 -> x1, other arithmetic: none -> 0.69 us  [paired_body(): docs = doc_ids.reshape(tokens, 1).astype(jnp.float32)]
  transfers between devices with their start and end apart: 18 -> 17, of which waited for: 9 -> 6; matrix products, arithmetic and copies ran while one was open for 5% -> 7% of each run, Pallas kernels for 14% -> 11%
where the time goes in v2:
time: 46.8 us; the launch traced here: 46.3 us
  starting transfers between devices  19.2 us (41%)
  waiting for transfers between devices  14 us (30%)
  Pallas kernels  8.61 us (18%)
  other arithmetic  3.26 us (7%)
  local copies, waits for them, and re-layouts  1.1 us (2%)
    ppermute x15, starting transfers between devices, flip(): return lax.ppermute(value, ('fsdp', 'ctx'), pairs)  18.6 us
    ppermute x15, waiting for transfers between devices, flip(): return lax.ppermute(value, ('fsdp', 'ctx'), pairs)  12.7 us
    pallas_call x3, Pallas kernels, partial(): pl.pallas_call(functools.partial(partial_kernel, masks, begun), out_shape...  4.85 us
    pallas_call x1, Pallas kernels, paired_body(): pl.pallas_call(attention_kernel, out_shape=jax.ShapeDtypeStruct((tokens,...  3 us
    neg x1, other arithmetic, paired_body(): sines = jnp.concatenate([-sine, sine], axis=-1)  1.45 us
    ppermute x2, waiting for transfers between devices, swap(): return lax.ppermute(value, 'ctx', [(0, 1), (1, 0)])  1.23 us
    unnamed x6, local copies, waits for them, and re-layouts  0.95 us
  transfers between devices with their start and end apart: 17, of which 6 were waited for; matrix products, arithmetic and copies ran while one was open for 7% of the time, Pallas kernels for 11%

profile of v2, /device:TPU:1, one launch (start us, length us, event | category | flops | bytes accessed | tf_op | source)
XLA Modules:
  0.0 46.3 jit_solution(18445748722101615668)
XLA Ops:
  0.1 0.9 %copy-done = bf16[256,768]{1,0:T(8,128)(2,1)S(1)} copy-done((bf16[256,768]{1,0:T(8,128)(2,1)S(1)}, bf16[256,768]{1,0:T(8,128)(2,1)}, u32[]{:S(2)}) %copy-start) | copy-done | bytes 393240
  1.0 0.7 %pad_maximum_fusion.2.refs_2_ = bf16[256,384]{1,0:T(8,128)(2,1)} fusion(bf16[256,128]{1,0:T(8,128)(2,1)S(1)} %constant_dynamic-slice_fusion, bf16[256,256]{1,0:T(8,128)(2,1)S(1)} %constant_dynamic-slice_fusion.1), kind=kLoop, calls=%fused_computation.4 | loop fusion | flops 393216 | bytes 393216 | tf_op jit(solution)/shard_map/concatenate | solution.py:308
  1.7 2.1 %collective-permute-start = (bf16[256,384]{1,0:T(8,128)(2,1)}, bf16[256,384]{1,0:T(8,128)(2,1)}, u32[]{:S(2)}, u32[]{:S(2)}) collective-permute-start(bf16[256,384]{1,0:T(8,128)(2,1)} %pad_maximum_fusion.2.refs_2_), channel_id=1, source_target_pairs={{0,8},{1,9},{2,10},{3,11},{4,12},{5,13},{6,14},{7,15},{8,0},{9,1},... | collective-permute-start | bytes 589832 | tf_op jit(solution)/shard_map/ppermute | solution.py:125
  3.8 2.3 %collective-permute-start.2 = (bf16[256,384]{1,0:T(8,128)(2,1)}, bf16[256,384]{1,0:T(8,128)(2,1)}, u32[]{:S(2)}, u32[]{:S(2)}) collective-permute-start(bf16[256,384]{1,0:T(8,128)(2,1)} %pad_maximum_fusion.2.refs_2_), channel_id=1, source_target_pairs={{0,16},{1,17},{2,18},{3,19},{4,20},{5,21},{6,22},{7,23},{8,24},{9,... | collective-permute-start | bytes 589832 | tf_op jit(solution)/shard_map/ppermute | solution.py:125
  6.2 1.2 %collective-permute-start.5 = (bf16[256,384]{1,0:T(8,128)(2,1)}, bf16[256,384]{1,0:T(8,128)(2,1)}, u32[]{:S(2)}, u32[]{:S(2)}) collective-permute-start(bf16[256,384]{1,0:T(8,128)(2,1)} %pad_maximum_fusion.2.refs_2_), channel_id=1, source_target_pairs={{0,2},{1,5},{2,0},{3,7},{4,6},{5,1},{6,4},{7,3},{8,10},{9,13},{10,... | collective-permute-start | bytes 589832 | tf_op jit(solution)/shard_map/ppermute | solution.py:125
  7.4 1.2 %collective-permute-start.6 = (bf16[256,384]{1,0:T(8,128)(2,1)}, bf16[256,384]{1,0:T(8,128)(2,1)}, u32[]{:S(2)}, u32[]{:S(2)}) collective-permute-start(bf16[256,384]{1,0:T(8,128)(2,1)} %pad_maximum_fusion.2.refs_2_), channel_id=1, source_target_pairs={{0,4},{1,3},{2,6},{3,1},{4,0},{5,7},{6,2},{7,5},{8,12},{9,11},{10,... | collective-permute-start | bytes 589832 | tf_op jit(solution)/shard_map/ppermute | solution.py:125
  8.8 1.5 %fusion = (f32[2,384,64]{2,1,0:T(8,128)S(1)}, f32[2,384,64]{2,1,0:T(8,128)S(1)}, f32[2,384,64]{2,1,0:T(8,128)S(1)}) fusion(f32[64]{0:T(128)S(1)} %multiply_exponential_fusion, f32[2,384]{1,0:T(2,128)S(1)} %add_convert_fusion), kind=kLoop, calls=%fused_computation.5 | loop fusion | flops 98304 | bytes 593152 | tf_op jit(solution)/shard_map/neg | solution.py:324
  10.2 0.7 %convert_bitcast_fusion = f32[384,1]{0,1:T(1,128)S(1)} fusion(s32[1,384]{1,0:T(1,128)} %refs_6_.1), kind=kLoop, calls=%fused_computation.7 | loop fusion | flops 384 | bytes 3072 | tf_op jit(solution)/shard_map/convert_element_type | solution.py:325
  10.9 1.1 %collective-permute-done.2.refs_9_ = bf16[256,384]{1,0:T(8,128)(2,1)} collective-permute-done((bf16[256,384]{1,0:T(8,128)(2,1)}, bf16[256,384]{1,0:T(8,128)(2,1)}, u32[]{:S(2)}, u32[]{:S(2)}) %collective-permute-start.2) | collective-permute-done | bytes 196640 | tf_op jit(solution)/shard_map/ppermute | solution.py:125
  12.0 3.2 %collective-permute-start.3 = (bf16[256,384]{1,0:T(8,128)(2,1)}, bf16[256,384]{1,0:T(8,128)(2,1)S(1)}, u32[]{:S(2)}, u32[]{:S(2)}) collective-permute-start(bf16[256,384]{1,0:T(8,128)(2,1)} %collective-permute-done.2.refs_9_), channel_id=1, source_target_pairs={{0,8},{1,9},{2,10},{3,11},{4,12},{5,13},{6,14},{7,15},{8,0},{9,1},... | collective-permute-start | bytes 589832 | tf_op jit(solution)/shard_map/ppermute | solution.py:125
  15.5 1.3 %collective-permute-start.11 = (bf16[256,384]{1,0:T(8,128)(2,1)}, bf16[256,384]{1,0:T(8,128)(2,1)S(1)}, u32[]{:S(2)}, u32[]{:S(2)}) collective-permute-start(bf16[256,384]{1,0:T(8,128)(2,1)} %collective-permute-done.2.refs_9_), channel_id=1, source_target_pairs={{0,2},{1,5},{2,0},{3,7},{4,6},{5,1},{6,4},{7,3},{8,10},{9,13},{10,... | collective-permute-start | bytes 589832 | tf_op jit(solution)/shard_map/ppermute | solution.py:125
  16.8 1.2 %collective-permute-start.7 = (bf16[256,384]{1,0:T(8,128)(2,1)}, bf16[256,384]{1,0:T(8,128)(2,1)S(1)}, u32[]{:S(2)}, u32[]{:S(2)}) collective-permute-start(bf16[256,384]{1,0:T(8,128)(2,1)} %collective-permute-done.5.refs_3_), channel_id=1, source_target_pairs={{0,4},{1,3},{2,6},{3,1},{4,0},{5,7},{6,2},{7,5},{8,12},{9,11},{10,... | collective-permute-start | bytes 589832 | tf_op jit(solution)/shard_map/ppermute | solution.py:125
  18.8 1.2 %collective-permute-start.4 = (bf16[256,384]{1,0:T(8,128)(2,1)S(1)}, bf16[256,384]{1,0:T(8,128)(2,1)S(1)}, u32[]{:S(2)}, u32[]{:S(2)}) collective-permute-start(bf16[256,384]{1,0:T(8,128)(2,1)S(1)} %collective-permute-done.3.refs_5_), channel_id=1, source_target_pairs={{0,2},{1,5},{2,0},{3,7},{4,6},{5,1},{6,4},{7,3},{8,10},{9,13},{10,... | collective-permute-start | bytes 589832 | tf_op jit(solution)/shard_map/ppermute | solution.py:125
  20.1 2.8 %collective-permute-done.7.refs_5_ = bf16[256,384]{1,0:T(8,128)(2,1)S(1)} collective-permute-done((bf16[256,384]{1,0:T(8,128)(2,1)}, bf16[256,384]{1,0:T(8,128)(2,1)S(1)}, u32[]{:S(2)}, u32[]{:S(2)}) %collective-permute-start.7) | collective-permute-done | bytes 196640 | tf_op jit(solution)/shard_map/ppermute | solution.py:125
  22.8 1.2 %collective-permute-start.15 = (bf16[256,384]{1,0:T(8,128)(2,1)}, bf16[256,384]{1,0:T(8,128)(2,1)S(1)}, u32[]{:S(2)}, u32[]{:S(2)}) collective-permute-start(bf16[256,384]{1,0:T(8,128)(2,1)} %collective-permute-done.2.refs_9_), channel_id=1, source_target_pairs={{0,4},{1,3},{2,6},{3,1},{4,0},{5,7},{6,2},{7,5},{8,12},{9,11},{10,... | collective-permute-start | bytes 589832 | tf_op jit(solution)/shard_map/ppermute | solution.py:125
  24.3 1.2 %collective-permute-start.12 = (bf16[256,384]{1,0:T(8,128)(2,1)S(1)}, bf16[256,384]{1,0:T(8,128)(2,1)S(1)}, u32[]{:S(2)}, u32[]{:S(2)}) collective-permute-start(bf16[256,384]{1,0:T(8,128)(2,1)S(1)} %collective-permute-done.11.refs_3_), channel_id=1, source_target_pairs={{0,4},{1,3},{2,6},{3,1},{4,0},{5,7},{6,2},{7,5},{8,12},{9,11},{10,... | collective-permute-start | bytes 589832 | tf_op jit(solution)/shard_map/ppermute | solution.py:125
  25.5 1.5 %collective-permute-done.9.refs_8_ = bf16[256,384]{1,0:T(8,128)(2,1)S(1)} collective-permute-done((bf16[256,384]{1,0:T(8,128)(2,1)}, bf16[256,384]{1,0:T(8,128)(2,1)S(1)}, u32[]{:S(2)}, u32[]{:S(2)}) %collective-permute-start.9) | collective-permute-done | bytes 196640 | tf_op jit(solution)/shard_map/ppermute | solution.py:125
  27.0 1.2 %collective-permute-start.14 = (bf16[256,384]{1,0:T(8,128)(2,1)S(1)}, bf16[256,384]{1,0:T(8,128)(2,1)S(1)}, u32[]{:S(2)}, u32[]{:S(2)}) collective-permute-start(bf16[256,384]{1,0:T(8,128)(2,1)S(1)} %collective-permute-done.8.refs_7_), channel_id=1, source_target_pairs={{0,4},{1,3},{2,6},{3,1},{4,0},{5,7},{6,2},{7,5},{8,12},{9,11},{10,... | collective-permute-start | bytes 589832 | tf_op jit(solution)/shard_map/ppermute | solution.py:125
  28.3 3.1 %shard_map.38.refs_6_ = f32[2,384,384]{2,1,0:T(8,128)S(1)} custom-call(bf16[384,4096]{1,0:T(8,128)(2,1)S(1)} %bitcast.7, bf16[384,4096]{1,0:T(8,128)(2,1)S(1)} %shard_map.37.refs_1_, bf16[256,384]{1,0:T(8,128)(2,1)} %pad_maximum_fusion.2.refs_2_, bf16[256,384]{1,0:T(8,128)(2,1)} %collective-permute-done.5.refs_3_, ...), custom_call_target="tpu_custom_call" | custom-call | flops 1207959552 | bytes 7077888 | tf_op jit(solution)/shard_map/pallas_call | solution.py:285
  31.7 7.0 %collective-permute-done.14.refs_2_ = bf16[256,384]{1,0:T(8,128)(2,1)S(1)} collective-permute-done((bf16[256,384]{1,0:T(8,128)(2,1)S(1)}, bf16[256,384]{1,0:T(8,128)(2,1)S(1)}, u32[]{:S(2)}, u32[]{:S(2)}) %collective-permute-start.14) | collective-permute-done | bytes 196640 | tf_op jit(solution)/shard_map/ppermute | solution.py:125
  38.7 1.0 %shard_map.39.refs_5_ = f32[2,384,384]{2,1,0:T(8,128)S(1)} custom-call(bf16[384,4096]{1,0:T(8,128)(2,1)S(1)} %bitcast.8, bf16[384,4096]{1,0:T(8,128)(2,1)S(1)} %shard_map.37.refs_1_, bf16[256,384]{1,0:T(8,128)(2,1)S(1)} %collective-permute-done.14.refs_2_, bf16[256,384]{1,0:T(8,128)(2,1)S(1)} %collective-permute-done.11.refs_3_, ...), custom_call_target="tpu_custom_call" | custom-call | flops 603979776 | bytes 4718592 | tf_op jit(solution)/shard_map/pallas_call | solution.py:285
  39.7 0.8 %shard_map.40.refs_3_ = f32[2,384,384]{2,1,0:T(8,128)S(1)} custom-call(bf16[384,4096]{1,0:T(8,128)(2,1)S(1)} %bitcast.9, bf16[384,4096]{1,0:T(8,128)(2,1)S(1)} %shard_map.37.refs_1_, bf16[256,384]{1,0:T(8,128)(2,1)S(1)} %collective-permute-done.12.refs_2_, bf16[256,384]{1,0:T(8,128)(2,1)S(1)} %collective-permute-done.4.refs_3_, ...), custom_call_target="tpu_custom_call" | custom-call | flops 452984832 | bytes 4128768 | tf_op jit(solution)/shard_map/pallas_call | solution.py:285
  42.0 1.2 %collective-permute-done.16.recv_ref = bf16[400,512]{1,0:T(8,128)(2,1)S(1)} collective-permute-done((bf16[400,512]{1,0:T(8,128)(2,1)S(1)}, bf16[400,512]{1,0:T(8,128)(2,1)S(1)}, u32[]{:S(2)}, u32[]{:S(2)}) %collective-permute-start.16) | collective-permute-done | bytes 409632 | tf_op jit(solution)/shard_map/ppermute | solution.py:129
  43.3 3.0 %shard_map.42 = bf16[384,512]{1,0:T(8,128)(2,1)} custom-call(bf16[400,512]{1,0:T(8,128)(2,1)S(1)} %get-tuple-element.20.keep_ref, bf16[400,512]{1,0:T(8,128)(2,1)S(1)} %collective-permute-done.16.recv_ref, f32[384,1]{1,0:T(8,128)S(1)} %copy.4.docs_ref), custom_call_target="tpu_custom_call" | custom-call | flops 603979776 | bytes 1572864 | tf_op jit(solution)/shard_map/pallas_call | solution.py:354
  (32 shorter events, 3.4 us)
Async XLA Ops:
  0.0 1.0 %copy-start = (bf16[256,768]{1,0:T(8,128)(2,1)S(1)}, bf16[256,768]{1,0:T(8,128)(2,1)}, u32[]{:S(2)}) copy-start(bf16[256,768]{1,0:T(8,128)(2,1)} %param.4) | copy-start | bytes 1179652
  0.0 16.8 %collective-permute-start.1 = (bf16[384,4096]{1,0:T(8,128)(2,1)}, bf16[384,4096]{1,0:T(8,128)(2,1)S(1)}, u32[]{:S(2)}, u32[]{:S(2)}) collective-permute-start(bf16[384,4096]{1,0:T(8,128)(2,1)} %bitcast.6), channel_id=1, source_target_pairs={{0,1},{1,0},{2,3},{3,2},{4,5},{5,4},{6,7},{7,6},{8,9},{9,8},{10,11... | collective-permute-start | bytes 9437192 | tf_op jit(solution)/shard_map/ppermute | solution.py:129
  1.7 16.5 %collective-permute-start = (bf16[256,384]{1,0:T(8,128)(2,1)}, bf16[256,384]{1,0:T(8,128)(2,1)}, u32[]{:S(2)}, u32[]{:S(2)}) collective-permute-start(bf16[256,384]{1,0:T(8,128)(2,1)} %pad_maximum_fusion.2.refs_2_), channel_id=1, source_target_pairs={{0,8},{1,9},{2,10},{3,11},{4,12},{5,13},{6,14},{7,15},{8,0},{9,1},... | collective-permute-start | bytes 589832 | tf_op jit(solution)/shard_map/ppermute | solution.py:125
  3.8 8.1 %collective-permute-start.2 = (bf16[256,384]{1,0:T(8,128)(2,1)}, bf16[256,384]{1,0:T(8,128)(2,1)}, u32[]{:S(2)}, u32[]{:S(2)}) collective-permute-start(bf16[256,384]{1,0:T(8,128)(2,1)} %pad_maximum_fusion.2.refs_2_), channel_id=1, source_target_pairs={{0,16},{1,17},{2,18},{3,19},{4,20},{5,21},{6,22},{7,23},{8,24},{9,... | collective-permute-start | bytes 589832 | tf_op jit(solution)/shard_map/ppermute | solution.py:125
  6.2 9.3 %collective-permute-start.5 = (bf16[256,384]{1,0:T(8,128)(2,1)}, bf16[256,384]{1,0:T(8,128)(2,1)}, u32[]{:S(2)}, u32[]{:S(2)}) collective-permute-start(bf16[256,384]{1,0:T(8,128)(2,1)} %pad_maximum_fusion.2.refs_2_), channel_id=1, source_target_pairs={{0,2},{1,5},{2,0},{3,7},{4,6},{5,1},{6,4},{7,3},{8,10},{9,13},{10,... | collective-permute-start | bytes 589832 | tf_op jit(solution)/shard_map/ppermute | solution.py:125
  7.4 11.2 %collective-permute-start.6 = (bf16[256,384]{1,0:T(8,128)(2,1)}, bf16[256,384]{1,0:T(8,128)(2,1)}, u32[]{:S(2)}, u32[]{:S(2)}) collective-permute-start(bf16[256,384]{1,0:T(8,128)(2,1)} %pad_maximum_fusion.2.refs_2_), channel_id=1, source_target_pairs={{0,4},{1,3},{2,6},{3,1},{4,0},{5,7},{6,2},{7,5},{8,12},{9,11},{10,... | collective-permute-start | bytes 589832 | tf_op jit(solution)/shard_map/ppermute | solution.py:125
  12.0 6.8 %collective-permute-start.3 = (bf16[256,384]{1,0:T(8,128)(2,1)}, bf16[256,384]{1,0:T(8,128)(2,1)S(1)}, u32[]{:S(2)}, u32[]{:S(2)}) collective-permute-start(bf16[256,384]{1,0:T(8,128)(2,1)} %collective-permute-done.2.refs_9_), channel_id=1, source_target_pairs={{0,8},{1,9},{2,10},{3,11},{4,12},{5,13},{6,14},{7,15},{8,0},{9,1},... | collective-permute-start | bytes 589832 | tf_op jit(solution)/shard_map/ppermute | solution.py:125
  15.5 12.8 %copy-start.1 = (bf16[1,384,4096]{2,1,0:T(8,128)(2,1)S(1)}, bf16[1,384,4096]{2,1,0:T(8,128)(2,1)}, u32[]{:S(2)}) copy-start(bf16[1,384,4096]{2,1,0:T(8,128)(2,1)} %param.3) | copy-start | bytes 9437188
  15.5 8.5 %collective-permute-start.11 = (bf16[256,384]{1,0:T(8,128)(2,1)}, bf16[256,384]{1,0:T(8,128)(2,1)S(1)}, u32[]{:S(2)}, u32[]{:S(2)}) collective-permute-start(bf16[256,384]{1,0:T(8,128)(2,1)} %collective-permute-done.2.refs_9_), channel_id=1, source_target_pairs={{0,2},{1,5},{2,0},{3,7},{4,6},{5,1},{6,4},{7,3},{8,10},{9,13},{10,... | collective-permute-start | bytes 589832 | tf_op jit(solution)/shard_map/ppermute | solution.py:125
  16.8 6.0 %collective-permute-start.7 = (bf16[256,384]{1,0:T(8,128)(2,1)}, bf16[256,384]{1,0:T(8,128)(2,1)S(1)}, u32[]{:S(2)}, u32[]{:S(2)}) collective-permute-start(bf16[256,384]{1,0:T(8,128)(2,1)} %collective-permute-done.5.refs_3_), channel_id=1, source_target_pairs={{0,4},{1,3},{2,6},{3,1},{4,0},{5,7},{6,2},{7,5},{8,12},{9,11},{10,... | collective-permute-start | bytes 589832 | tf_op jit(solution)/shard_map/ppermute | solution.py:125
  18.3 6.1 %collective-permute-start.8 = (bf16[256,384]{1,0:T(8,128)(2,1)}, bf16[256,384]{1,0:T(8,128)(2,1)S(1)}, u32[]{:S(2)}, u32[]{:S(2)}) collective-permute-start(bf16[256,384]{1,0:T(8,128)(2,1)} %collective-permute-done.refs_6_), channel_id=1, source_target_pairs={{0,2},{1,5},{2,0},{3,7},{4,6},{5,1},{6,4},{7,3},{8,10},{9,13},{10,... | collective-permute-start | bytes 589832 | tf_op jit(solution)/shard_map/ppermute | solution.py:125
  18.6 8.5 %collective-permute-start.9 = (bf16[256,384]{1,0:T(8,128)(2,1)}, bf16[256,384]{1,0:T(8,128)(2,1)S(1)}, u32[]{:S(2)}, u32[]{:S(2)}) collective-permute-start(bf16[256,384]{1,0:T(8,128)(2,1)} %collective-permute-done.refs_6_), channel_id=1, source_target_pairs={{0,4},{1,3},{2,6},{3,1},{4,0},{5,7},{6,2},{7,5},{8,12},{9,11},{10,... | collective-permute-start | bytes 589832 | tf_op jit(solution)/shard_map/ppermute | solution.py:125
  18.8 12.5 %collective-permute-start.4 = (bf16[256,384]{1,0:T(8,128)(2,1)S(1)}, bf16[256,384]{1,0:T(8,128)(2,1)S(1)}, u32[]{:S(2)}, u32[]{:S(2)}) collective-permute-start(bf16[256,384]{1,0:T(8,128)(2,1)S(1)} %collective-permute-done.3.refs_5_), channel_id=1, source_target_pairs={{0,2},{1,5},{2,0},{3,7},{4,6},{5,1},{6,4},{7,3},{8,10},{9,13},{10,... | collective-permute-start | bytes 589832 | tf_op jit(solution)/shard_map/ppermute | solution.py:125
  22.8 8.9 %collective-permute-start.15 = (bf16[256,384]{1,0:T(8,128)(2,1)}, bf16[256,384]{1,0:T(8,128)(2,1)S(1)}, u32[]{:S(2)}, u32[]{:S(2)}) collective-permute-start(bf16[256,384]{1,0:T(8,128)(2,1)} %collective-permute-done.2.refs_9_), channel_id=1, source_target_pairs={{0,4},{1,3},{2,6},{3,1},{4,0},{5,7},{6,2},{7,5},{8,12},{9,11},{10,... | collective-permute-start | bytes 589832 | tf_op jit(solution)/shard_map/ppermute | solution.py:125
  24.0 15.7 %collective-permute-start.13 = (bf16[256,384]{1,0:T(8,128)(2,1)S(1)}, bf16[256,384]{1,0:T(8,128)(2,1)S(1)}, u32[]{:S(2)}, u32[]{:S(2)}) collective-permute-start(bf16[256,384]{1,0:T(8,128)(2,1)S(1)} %collective-permute-done.3.refs_5_), channel_id=1, source_target_pairs={{0,4},{1,3},{2,6},{3,1},{4,0},{5,7},{6,2},{7,5},{8,12},{9,11},{10,... | collective-permute-start | bytes 589832 | tf_op jit(solution)/shard_map/ppermute | solution.py:125
  24.3 15.4 %collective-permute-start.12 = (bf16[256,384]{1,0:T(8,128)(2,1)S(1)}, bf16[256,384]{1,0:T(8,128)(2,1)S(1)}, u32[]{:S(2)}, u32[]{:S(2)}) collective-permute-start(bf16[256,384]{1,0:T(8,128)(2,1)S(1)} %collective-permute-done.11.refs_3_), channel_id=1, source_target_pairs={{0,4},{1,3},{2,6},{3,1},{4,0},{5,7},{6,2},{7,5},{8,12},{9,11},{10,... | collective-permute-start | bytes 589832 | tf_op jit(solution)/shard_map/ppermute | solution.py:125
  27.0 11.6 %collective-permute-start.14 = (bf16[256,384]{1,0:T(8,128)(2,1)S(1)}, bf16[256,384]{1,0:T(8,128)(2,1)S(1)}, u32[]{:S(2)}, u32[]{:S(2)}) collective-permute-start(bf16[256,384]{1,0:T(8,128)(2,1)S(1)} %collective-permute-done.8.refs_7_), channel_id=1, source_target_pairs={{0,4},{1,3},{2,6},{3,1},{4,0},{5,7},{6,2},{7,5},{8,12},{9,11},{10,... | collective-permute-start | bytes 589832 | tf_op jit(solution)/shard_map/ppermute | solution.py:125
  31.3 9.4 %collective-permute-start.10 = (bf16[256,384]{1,0:T(8,128)(2,1)S(1)}, bf16[256,384]{1,0:T(8,128)(2,1)S(1)}, u32[]{:S(2)}, u32[]{:S(2)}) collective-permute-start(bf16[256,384]{1,0:T(8,128)(2,1)S(1)} %collective-permute-done.4.refs_3_), channel_id=1, source_target_pairs={{0,4},{1,3},{2,6},{3,1},{4,0},{5,7},{6,2},{7,5},{8,12},{9,11},{10,... | collective-permute-start | bytes 589832 | tf_op jit(solution)/shard_map/ppermute | solution.py:125
  39.7 1.1 %copy-start.2 = (s32[1,384]{1,0:T(1,128)S(1)}, s32[1,384]{1,0:T(1,128)}, u32[]{:S(2)}) copy-start(s32[1,384]{1,0:T(1,128)} %refs_6_.1) | copy-start | bytes 4612
  41.3 1.9 %collective-permute-start.16 = (bf16[400,512]{1,0:T(8,128)(2,1)S(1)}, bf16[400,512]{1,0:T(8,128)(2,1)S(1)}, u32[]{:S(2)}, u32[]{:S(2)}) collective-permute-start(bf16[400,512]{1,0:T(8,128)(2,1)S(1)} %get-tuple-element.21), channel_id=1, source_target_pairs={{0,1},{1,0},{2,3},{3,2},{4,5},{5,4},{6,7},{7,6},{8,9},{9,8},{10,11... | collective-permute-start | bytes 1228808 | tf_op jit(solution)/shard_map/ppermute | solution.py:129

commit v3 on v2

--- a/solution.py
+++ b/solution.py
@@ -14,7 +14,7 @@
 
 THETA = 1000000.0
 
-TILE = 16
+STEP = 128
 
 VMEM_LIMIT = 16 * 1024 * 1024
 
@@ -166,9 +166,9 @@
     count = len(masks)
     mine_ref, other_ref = refs[:2]
     parts = refs[2 : 2 + count]
-    total, cos_ref, sin_ref, docs_ref, keep_ref, send_ref = refs[2 + count :]
+    total, cos_ref, sin_ref, keep_ref, send_ref = refs[2 + count :]
     sums = add_blocks(total, parts, masks, mine_ref, other_ref)
-    turned = lax.axis_index("ctx") == 0
+    turned = lax.axis_index("ctx") == 1
 
     def turn(block, cosine, sine):
         swapped = jnp.concatenate([block[:, HD // 2 :], block[:, : HD // 2]], axis=1)
@@ -187,87 +187,179 @@
             ),
         ]
         ends.append(blocks)
-    rows = docs_ref.shape[1]
     for ref, here, there in ((keep_ref, ends[0], ends[1]), (send_ref, ends[1], ends[0])):
-        ref[:rows, :HD] = here[0]
-        ref[:rows, HD : 2 * HD] = here[1]
-        ref[:rows, 2 * HD : 3 * HD] = here[2]
-        ref[:rows, 3 * HD :] = there[2]
-        ref[rows:, :] = jnp.zeros((TILE, 4 * HD), ref.dtype)
-        ref[rows:, :rows] = jnp.broadcast_to(docs_ref[...], (TILE, rows)).astype(ref.dtype)
-
-
-def attention_kernel(keep_ref, recv_ref, docs_ref, out_ref):
+        ref[:, :HD] = here[0]
+        ref[:, HD : 2 * HD] = here[1]
+        ref[:, 2 * HD : 3 * HD] = here[2]
+        ref[:, 3 * HD :] = there[2]
+
+
+def weigh(queries, keys, visible):
+    step, width = visible.shape
+    heads = queries.shape[0] // step
+    scores = lax.dot_general(
+        queries, keys, (((1,), (0,)), ((), ())), preferred_element_type=jnp.float32
+    )
+    scores = jnp.where(visible[None], scores.reshape(heads, step, width), -jnp.inf)
+    top = jnp.max(scores, axis=-1, keepdims=True)
+    weights = jnp.exp2((scores - top) * (math.log2(math.e) / math.sqrt(HD)))
+    return weights.astype(jnp.bfloat16).reshape(heads * step, width)
+
+
+def visible_keys(column_ref, row_ref, place, first, last):
+    same = column_ref[place, :] == row_ref[:, first:last]
+    own = lax.broadcasted_iota(jnp.int32, (STEP, STEP), 1)
+    query = lax.broadcasted_iota(jnp.int32, (STEP, STEP), 0)
+    width = last - first
+    if width == STEP:
+        return same & (own <= query)
+    return jnp.concatenate([same[:, : width - STEP], same[:, width - STEP :] & (own <= query)], axis=1)
+
+
+def head_columns(ref, place):
+    return jnp.concatenate([ref[place, :HD], ref[place, HD : 2 * HD]], axis=0)
+
+
+def both_ends(ref):
+    return jnp.concatenate([ref[:, 3 * HD :], ref[:, 2 * HD : 3 * HD]], axis=0)
+
+
+def with_ones(values):
+    return jnp.concatenate([values, jnp.ones_like(values)], axis=1)
+
+
+def early_kernel(keep_ref, column_ref, row_ref, probs_ref, keys_ref):
+    rows = keep_ref.shape[0]
+
+    @pl.when(lax.axis_index("ctx") == 1)
+    def _():
+        keys = both_ends(keep_ref).T
+        keys_ref[...] = keys
+        for step in range(rows // STEP):
+            place = slice(step * STEP, (step + 1) * STEP)
+            width = rows + (step + 1) * STEP
+            probs_ref[step, :, :width] = weigh(
+                head_columns(keep_ref, place),
+                keys[:, :width],
+                visible_keys(column_ref, row_ref, place, 0, width),
+            )
+
+
+def attention_kernel(
+    keep_ref, recv_ref, probs_ref, keys_ref, column_ref, row_ref, out_ref, held, sems
+):
     core = lax.axis_index("ctx")
-    rows = docs_ref.shape[0]
-    tile = 128
-    kept = jnp.concatenate([keep_ref[:rows, 3 * HD :], keep_ref[:rows, 2 * HD : 3 * HD]], axis=0)
-    received = jnp.concatenate([recv_ref[:rows, 3 * HD :], recv_ref[:rows, 2 * HD : 3 * HD]], axis=0)
-    keys = jnp.where(core == 0, kept, received)
-    values = jnp.where(core == 0, received, kept)
-    docs = jnp.concatenate(
-        [recv_ref[rows : rows + 1, :rows], keep_ref[rows : rows + 1, :rows]], axis=1
-    ).astype(jnp.float32)
-    factor = math.log2(math.e) / math.sqrt(HD)
-    kept_first = pl.multiple_of(core * 2 * HD, 2 * HD)
-    recv_first = pl.multiple_of((1 - core) * 2 * HD, 2 * HD)
-    for step in range(rows // tile):
-        here = slice(step * tile, (step + 1) * tile)
-        width = rows + (step + 1) * tile
-        queries = jnp.concatenate(
-            [
-                keep_ref[here, :HD],
-                keep_ref[here, HD : 2 * HD],
-                recv_ref[here, :HD],
-                recv_ref[here, HD : 2 * HD],
-            ],
-            axis=0,
-        )
-        scores = lax.dot_general(
-            queries, keys[:width], (((1,), (1,)), ((), ())), preferred_element_type=jnp.float32
-        )
-        column = lax.broadcasted_iota(jnp.int32, (tile, width), 1)
-        row = lax.broadcasted_iota(jnp.int32, (tile, width), 0) + (rows + step * tile)
-        first = jnp.where(core == 0, rows, 0)
-        visible = (
-            (column <= row) & (column >= first) & (docs_ref[here, :] == docs[:, :width])
-        )
-        scores = jnp.where(visible[None], scores.reshape(HEADS, tile, width), -jnp.inf)
-        top = jnp.max(scores, axis=-1, keepdims=True)
-        weights = jnp.exp2((scores - top) * factor)
-        totals = jnp.sum(weights, axis=-1, keepdims=True)
-        context = jnp.dot(
-            weights.astype(jnp.bfloat16).reshape(HEADS * tile, width),
-            values[:width],
-            preferred_element_type=jnp.float32,
-        ).reshape(HEADS, tile, HD)
-        context = (context / totals).astype(jnp.bfloat16)
-        for head in range(HEADS // 2):
-            out_ref[here, pl.ds(pl.multiple_of(kept_first + head * HD, HD), HD)] = context[head]
-            out_ref[here, pl.ds(pl.multiple_of(recv_first + head * HD, HD), HD)] = context[
-                head + HEADS // 2
+    rows = keep_ref.shape[0]
+
+    def write(step, context, order):
+        place = slice(step * STEP, (step + 1) * STEP)
+        for head, column in enumerate(order):
+            held[place, column * HD : (column + 1) * HD] = context[
+                head * STEP : (head + 1) * STEP
             ]
+        pltpu.make_async_copy(held.at[place], out_ref.at[place], sems.at[step]).start()
+
+    @pl.when(core == 0)
+    def _():
+        keys, values = recv_ref[:, 2 * HD : 3 * HD].T, with_ones(keep_ref[:, 2 * HD : 3 * HD])
+        for step in range(rows // STEP):
+            place = slice(step * STEP, (step + 1) * STEP)
+            width = (step + 1) * STEP
+            probs = weigh(
+                jnp.concatenate(
+                    [head_columns(keep_ref, place), head_columns(recv_ref, place)], axis=0
+                ),
+                keys[:, :width],
+                visible_keys(column_ref, row_ref, place, rows, rows + width),
+            )
+            context = jnp.dot(probs, values[:width], preferred_element_type=jnp.float32)
+            write(step, (context[:, :HD] / context[:, HD:]).astype(jnp.bfloat16), (0, 1, 2, 3))
+
+    @pl.when(core == 1)
+    def _():
+        keys, values = keys_ref[...], with_ones(both_ends(recv_ref))
+        for step in range(rows // STEP):
+            place = slice(step * STEP, (step + 1) * STEP)
+            width = rows + (step + 1) * STEP
+            probs = weigh(
+                head_columns(recv_ref, place),
+                keys[:, :width],
+                visible_keys(column_ref, row_ref, place, 0, width),
+            )
+            probs = jnp.concatenate([probs, probs_ref[step, :, :width]], axis=0)
+            context = jnp.dot(probs, values[:width], preferred_element_type=jnp.float32)
+            write(step, (context[:, :HD] / context[:, HD:]).astype(jnp.bfloat16), (0, 1, 2, 3))
+
+    for step in range(rows // STEP):
+        place = slice(step * STEP, (step + 1) * STEP)
+        pltpu.make_async_copy(held.at[place], out_ref.at[place], sems.at[step]).wait()
 
 
 VMEM = pl.BlockSpec(memory_space=pltpu.VMEM)
-
-
-def stage_kernel(source_ref, out_ref, sem):
+ANY = pl.BlockSpec(memory_space=pl.ANY)
+
+
+def stage_kernel(source_ref, docs_ref, docs_other_ref, out_ref, column_ref, row_ref, sem):
     copy = pltpu.make_async_copy(source_ref, out_ref, sem)
     copy.start()
+    rows = docs_ref.shape[1]
+    docs = docs_ref[...].astype(jnp.float32)
+    row_ref[:, :rows] = docs_other_ref[...].astype(jnp.float32)
+    row_ref[:, rows:] = docs
+    for first in range(0, rows, STEP):
+        place = slice(first, first + STEP)
+        column_ref[place, :] = jnp.broadcast_to(docs[:, place], (STEP, STEP)).T[:, :1]
     copy.wait()
 
 
-def stage(value):
+def stage(value, docs, docs_other):
+    tokens = value.shape[0]
     return pl.pallas_call(
         stage_kernel,
-        out_shape=jax.ShapeDtypeStruct(value.shape, value.dtype),
-        in_specs=[pl.BlockSpec(memory_space=pl.ANY)],
-        out_specs=VMEM,
+        out_shape=(
+            jax.ShapeDtypeStruct(value.shape, value.dtype),
+            jax.ShapeDtypeStruct((tokens, 1), jnp.float32),
+            jax.ShapeDtypeStruct((1, 2 * tokens), jnp.float32),
+        ),
+        in_specs=[ANY, VMEM, VMEM],
+        out_specs=(VMEM, VMEM, VMEM),
         scratch_shapes=[pltpu.SemaphoreType.DMA],
         compiler_params=pltpu.CompilerParams(vmem_limit_bytes=VMEM_LIMIT),
-        cost_estimate=pl.CostEstimate(flops=0, bytes_accessed=2 * value.size * 2, transcendentals=0),
-    )(value)
+        cost_estimate=pl.CostEstimate(
+            flops=0, bytes_accessed=4 * value.size, transcendentals=0
+        ),
+    )(value, docs, docs_other)
+
+
+def own_kernel(weight_ref, out_ref, sems):
+    core = lax.axis_index("ctx")
+    copies = [
+        pltpu.make_async_copy(
+            weight_ref.at[:, pl.ds(pl.multiple_of(core * 2 * HD, 2 * HD), 2 * HD)],
+            out_ref.at[:, pl.ds(0, 2 * HD)],
+            sems.at[0],
+        ),
+        pltpu.make_async_copy(
+            weight_ref.at[:, pl.ds(pl.multiple_of((HEADS + 1 - core) * HD, HD), HD)],
+            out_ref.at[:, pl.ds(2 * HD, HD)],
+            sems.at[1],
+        ),
+    ]
+    for copy in copies:
+        copy.start()
+    for copy in copies:
+        copy.wait()
+
+
+def own_columns(weight):
+    return pl.pallas_call(
+        own_kernel,
+        out_shape=jax.ShapeDtypeStruct((weight.shape[0], 3 * HD), weight.dtype),
+        in_specs=[ANY],
+        out_specs=VMEM,
+        scratch_shapes=[pltpu.SemaphoreType.DMA((2,))],
+        compiler_params=pltpu.CompilerParams(vmem_limit_bytes=VMEM_LIMIT),
+    )(weight)
 
 
 def partial(mine, other, parts, masks, total=None, tables=None):
@@ -290,11 +382,11 @@
             compiler_params=params,
             cost_estimate=cost,
         )(mine, other, *parts, *([total] if begun else []))
-    out = jax.ShapeDtypeStruct((tokens + TILE, 4 * HD), jnp.bfloat16)
+    out = jax.ShapeDtypeStruct((tokens, 4 * HD), jnp.bfloat16)
     return pl.pallas_call(
         functools.partial(final_kernel, masks),
         out_shape=(out, out),
-        in_specs=[VMEM] * (count + 6),
+        in_specs=[VMEM] * (count + 5),
         out_specs=(VMEM, VMEM),
         compiler_params=params,
         cost_estimate=cost,
@@ -305,13 +397,7 @@
     mine = hidden_states[0]
     tokens = mine.shape[0]
     core = lax.axis_index("ctx")
-    own = jnp.concatenate(
-        [
-            lax.dynamic_slice_in_dim(qkv_weight, core * 2 * HD, 2 * HD, 1),
-            lax.dynamic_slice_in_dim(qkv_weight, (HEADS + core) * HD, HD, 1),
-        ],
-        axis=1,
-    )
+    own = own_columns(qkv_weight)
 
     frequency = jnp.exp(
         jnp.arange(HD // 2, dtype=jnp.float32) * (-2.0 * math.log(THETA) / HD)
@@ -322,47 +408,68 @@
     cosine, sine = jnp.cos(angles), jnp.sin(angles)
     cosines = jnp.concatenate([cosine, cosine], axis=-1)
     sines = jnp.concatenate([-sine, sine], axis=-1)
-    docs = doc_ids.reshape(tokens, 1).astype(jnp.float32)
-
+    other, column, row = stage(swap(mine), doc_ids, swap(doc_ids))
     z1 = flip(own, 4, 4)
     z2 = flip(own, 8, 8)
     a0 = flip(own, 1, 2)
     b0 = flip(own, 2, 1)
     z3 = flip(z2, 4, 4)
-
-    other = stage(swap(mine))
-    z1, cosines, sines, docs, other = lax.optimization_barrier(
-        (z1, cosines, sines, docs, other)
-    )
-    a1, b1, c0 = flip(z1, 1, 2), flip(z1, 2, 1), flip(a0, 2, 1)
-    a2, b2, c1 = flip(z2, 1, 2), flip(z2, 2, 1), flip(a1, 2, 1)
-    a3, b3, c2 = flip(z3, 1, 2), flip(z3, 2, 1), flip(a2, 2, 1)
-    total = partial(
-        mine,
-        other,
-        [own, a0, b0, c0, z1, a1, b1, z2],
-        [(0, 0), (1, 2), (2, 1), (3, 3), (4, 4), (5, 6), (6, 5), (8, 8)],
-    )
-    a3, total = lax.optimization_barrier((a3, total))
-    c3 = flip(a3, 2, 1)
-    total = partial(
-        mine, other, [c1, a2, b2, z3], [(7, 7), (9, 10), (10, 9), (12, 12)], total
-    )
-    total = partial(mine, other, [c2, a3, b3], [(11, 11), (13, 14), (14, 13)], total)
-    keep, send = partial(mine, other, [c3], [(15, 15)], total, (cosines, sines, doc_ids))
+    c0 = flip(a0, 2, 1)
+    a1 = flip(after(z1, b0), 1, 2)
+    K1 = partial(mine, other, [own, z1, z2, a0, b0, z3, c0, a1], [(0, 0), (4, 4), (8, 8), (1, 2), (2, 1), (12, 12), (3, 3), (5, 6)])
+    b1 = flip(z1, 2, 1)
+    c1 = flip(c0, 4, 4)
+    c3 = flip(c0, 12, 12)
+    (z2_a2, cosines, sines,) = lax.optimization_barrier(
+        (z2, cosines, sines)
+    )
+    a2 = flip(z2_a2, 1, 2)
+    K2 = partial(mine, other, [b1, c1, c3, a2], [(6, 5), (7, 7), (15, 15), (9, 10)], K1)
+    b2 = flip(z2, 2, 1)
+    c2 = flip(a2, 2, 1)
+    (z3_a3, K1,) = lax.optimization_barrier(
+        (z3, K1)
+    )
+    a3 = flip(z3_a3, 1, 2)
+    K3 = partial(mine, other, [b2, c2, a3], [(10, 9), (11, 11), (13, 14)], K2)
+    b3 = flip(z3, 2, 1)
+    keep, send = partial(
+        mine, other, [b3], [(14, 13)], K3, (cosines, sines)
+    )
     recv = swap(send)
+    steps = tokens // STEP
+    params = pltpu.CompilerParams(vmem_limit_bytes=VMEM_LIMIT)
+    probs, keys = pl.pallas_call(
+        early_kernel,
+        out_shape=(
+            jax.ShapeDtypeStruct((steps, 2 * STEP, 2 * tokens), jnp.bfloat16),
+            jax.ShapeDtypeStruct((HD, 2 * tokens), jnp.bfloat16),
+        ),
+        in_specs=[VMEM] * 3,
+        out_specs=(VMEM, VMEM),
+        compiler_params=params,
+        cost_estimate=pl.CostEstimate(
+            flops=4 * tokens * tokens * HD,
+            bytes_accessed=4 * tokens * tokens,
+            transcendentals=2 * tokens * tokens,
+        ),
+    )(keep, column, row)
     context = pl.pallas_call(
         attention_kernel,
         out_shape=jax.ShapeDtypeStruct((tokens, HEADS * HD), jnp.bfloat16),
-        in_specs=[VMEM] * 3,
-        out_specs=VMEM,
-        compiler_params=pltpu.CompilerParams(vmem_limit_bytes=VMEM_LIMIT),
+        in_specs=[VMEM] * 6,
+        out_specs=ANY,
+        scratch_shapes=[
+            pltpu.VMEM((tokens, HEADS * HD), jnp.bfloat16),
+            pltpu.SemaphoreType.DMA((steps,)),
+        ],
+        compiler_params=params,
         cost_estimate=pl.CostEstimate(
             flops=8 * HEADS * tokens * tokens * HD,
             bytes_accessed=tokens * HD * 32,
             transcendentals=2 * HEADS * tokens * tokens,
         ),
-    )(keep, recv, docs)
+    )(keep, recv, probs, keys, column, row)
     return context[None]
 
 

time: 46.8 us -> 42.9 us (0.917)
  waiting for transfers between devices: 14 us -> 6 us
  starting transfers between devices: 19.2 us -> 25.2 us
  other arithmetic: 3.26 us -> 1.88 us
    ppermute x15, waiting for transfers between devices: 12.7 us -> 5.35 us  [flip(): return lax.ppermute(value, ('fsdp', 'ctx'), pairs)]
    ppermute x2 -> x3, starting transfers between devices: 0.59 us -> 4.31 us  [swap(): return lax.ppermute(value, 'ctx', [(0, 1), (1, 0)])]
    ppermute x15, starting transfers between devices: 18.6 us -> 20.9 us  [flip(): return lax.ppermute(value, ('fsdp', 'ctx'), pairs)]
    pallas_call x1 -> x3, Pallas kernels: 0.22 us -> 1.1 us  [the longest x1 0.7 us: paired_body(): pl.pallas_call(early_kernel, out_shape=(jax.ShapeDtypeStruct((steps, 2 *...]
    pallas_call x1, Pallas kernels: 3 us -> 2.14 us  [paired_body(): pl.pallas_call(attention_kernel, out_shape=jax.ShapeDtypeStruct((tokens,...]
    concatenate x1 -> x0, other arithmetic: 0.7 us -> none  [paired_body(): jnp.concatenate([lax.dynamic_slice_in_dim(qkv_weight, core * 2 * HD, 2 *...]
    convert_element_type x1 -> x0, other arithmetic: 0.69 us -> none  [paired_body(): docs = doc_ids.reshape(tokens, 1).astype(jnp.float32)]
    ppermute x2 -> x3, waiting for transfers between devices: 1.23 us -> 0.65 us  [swap(): return lax.ppermute(value, 'ctx', [(0, 1), (1, 0)])]
  transfers between devices with their start and end apart: 17 -> 18, of which waited for: 6 -> 6; matrix products, arithmetic and copies ran while one was open for 7% -> 4% of each run, Pallas kernels for 11% -> 14%
where the time goes in v3:
time: 42.9 us; the launch traced here: 42.7 us
  starting transfers between devices  25.2 us (59%)
  Pallas kernels  8.46 us (20%)
  waiting for transfers between devices  6 us (14%)
  other arithmetic  1.88 us (4%)
  local copies, waits for them, and re-layouts  1 us (2%)
    ppermute x15, starting transfers between devices, flip(): return lax.ppermute(value, ('fsdp', 'ctx'), pairs)  20.9 us
    ppermute x15, waiting for transfers between devices, flip(): return lax.ppermute(value, ('fsdp', 'ctx'), pairs)  5.35 us
    pallas_call x3, Pallas kernels, partial(): pl.pallas_call(functools.partial(partial_kernel, masks, begun), out_shape...  4.67 us
    ppermute x3, starting transfers between devices, swap(): return lax.ppermute(value, 'ctx', [(0, 1), (1, 0)])  4.31 us
    pallas_call x1, Pallas kernels, paired_body(): pl.pallas_call(attention_kernel, out_shape=jax.ShapeDtypeStruct((tokens,...  2.14 us
    neg x1, other arithmetic, paired_body(): sines = jnp.concatenate([-sine, sine], axis=-1)  1.45 us
    unnamed x6, local copies, waits for them, and re-layouts  1 us
  transfers between devices with their start and end apart: 18, of which 6 were waited for; matrix products, arithmetic and copies ran while one was open for 4% of the time, Pallas kernels for 14%

profile of v3, /device:TPU:1, one launch (start us, length us, event | category | flops | bytes accessed | tf_op | source)
XLA Modules:
  0.0 42.7 jit_solution(321719602075066070)
XLA Ops:
  0.1 1.0 %copy-done.1 = bf16[256,768]{1,0:T(8,128)(2,1)S(1)} copy-done((bf16[256,768]{1,0:T(8,128)(2,1)S(1)}, bf16[256,768]{1,0:T(8,128)(2,1)}, u32[]{:S(2)}) %copy-start.1) | copy-done | bytes 393240
  1.1 2.8 %collective-permute-start.8 = (bf16[256,384]{1,0:T(8,128)(2,1)S(1)}, bf16[256,384]{1,0:T(8,128)(2,1)}, u32[]{:S(2)}, u32[]{:S(2)}) collective-permute-start(bf16[256,384]{1,0:T(8,128)(2,1)S(1)} %shard_map.38.refs_2_), channel_id=1, source_target_pairs={{0,8},{1,9},{2,10},{3,11},{4,12},{5,13},{6,14},{7,15},{8,0},{9,1},... | collective-permute-start | bytes 589832 | tf_op jit(solution)/shard_map/ppermute | solution.py:125
  3.9 1.2 %collective-permute-start.10 = (bf16[256,384]{1,0:T(8,128)(2,1)S(1)}, bf16[256,384]{1,0:T(8,128)(2,1)}, u32[]{:S(2)}, u32[]{:S(2)}) collective-permute-start(bf16[256,384]{1,0:T(8,128)(2,1)S(1)} %shard_map.38.refs_2_), channel_id=1, source_target_pairs={{0,4},{1,3},{2,6},{3,1},{4,0},{5,7},{6,2},{7,5},{8,12},{9,11},{10,... | collective-permute-start | bytes 589832 | tf_op jit(solution)/shard_map/ppermute | solution.py:125
  5.1 2.3 %collective-permute-start.2 = (bf16[256,384]{1,0:T(8,128)(2,1)S(1)}, bf16[256,384]{1,0:T(8,128)(2,1)S(1)}, u32[]{:S(2)}, u32[]{:S(2)}) collective-permute-start(bf16[256,384]{1,0:T(8,128)(2,1)S(1)} %shard_map.38.refs_2_), channel_id=1, source_target_pairs={{0,16},{1,17},{2,18},{3,19},{4,20},{5,21},{6,22},{7,23},{8,24},{9,... | collective-permute-start | bytes 589832 | tf_op jit(solution)/shard_map/ppermute | solution.py:125
  7.4 1.2 %collective-permute-start.9 = (bf16[256,384]{1,0:T(8,128)(2,1)S(1)}, bf16[256,384]{1,0:T(8,128)(2,1)}, u32[]{:S(2)}, u32[]{:S(2)}) collective-permute-start(bf16[256,384]{1,0:T(8,128)(2,1)S(1)} %shard_map.38.refs_2_), channel_id=1, source_target_pairs={{0,2},{1,5},{2,0},{3,7},{4,6},{5,1},{6,4},{7,3},{8,10},{9,13},{10,... | collective-permute-start | bytes 589832 | tf_op jit(solution)/shard_map/ppermute | solution.py:125
  8.8 1.5 %fusion = (f32[2,384,64]{2,1,0:T(8,128)S(1)}, f32[2,384,64]{2,1,0:T(8,128)S(1)}, f32[2,384,64]{2,1,0:T(8,128)S(1)}) fusion(f32[64]{0:T(128)S(1)} %multiply_exponential_fusion, f32[2,384]{1,0:T(2,128)S(1)} %add_convert_fusion), kind=kLoop, calls=%fused_computation.4 | loop fusion | flops 98304 | bytes 593152 | tf_op jit(solution)/shard_map/neg | solution.py:410
  10.3 1.8 %collective-permute-done.8.refs_3_ = bf16[256,384]{1,0:T(8,128)(2,1)} collective-permute-done((bf16[256,384]{1,0:T(8,128)(2,1)S(1)}, bf16[256,384]{1,0:T(8,128)(2,1)}, u32[]{:S(2)}, u32[]{:S(2)}) %collective-permute-start.8) | collective-permute-done | bytes 196640 | tf_op jit(solution)/shard_map/ppermute | solution.py:125
  12.1 0.7 %collective-permute-start.1 = (s32[1,384]{1,0:T(1,128)S(1)}, s32[1,384]{1,0:T(1,128)S(1)}, u32[]{:S(2)}, u32[]{:S(2)}) collective-permute-start(s32[1,384]{1,0:T(1,128)S(1)} %copy-done.2), channel_id=1, source_target_pairs={{0,1},{1,0},{2,3},{3,2},{4,5},{5,4},{6,7},{7,6},{8,9},{9,8},{10,11... | collective-permute-start | bytes 4616 | tf_op jit(solution)/shard_map/ppermute | solution.py:129
  12.8 2.3 %collective-permute-start.11 = (bf16[256,384]{1,0:T(8,128)(2,1)}, bf16[256,384]{1,0:T(8,128)(2,1)S(1)}, u32[]{:S(2)}, u32[]{:S(2)}) collective-permute-start(bf16[256,384]{1,0:T(8,128)(2,1)} %collective-permute-done.9.refs_5_), channel_id=1, source_target_pairs={{0,4},{1,3},{2,6},{3,1},{4,0},{5,7},{6,2},{7,5},{8,12},{9,11},{10,... | collective-permute-start | bytes 589832 | tf_op jit(solution)/shard_map/ppermute | solution.py:125
  15.4 1.3 %collective-permute-start.12 = (bf16[256,384]{1,0:T(8,128)(2,1)}, bf16[256,384]{1,0:T(8,128)(2,1)S(1)}, u32[]{:S(2)}, u32[]{:S(2)}) collective-permute-start(bf16[256,384]{1,0:T(8,128)(2,1)} %collective-permute-done.8.refs_3_), channel_id=1, source_target_pairs={{0,2},{1,5},{2,0},{3,7},{4,6},{5,1},{6,4},{7,3},{8,10},{9,13},{10,... | collective-permute-start | bytes 589832 | tf_op jit(solution)/shard_map/ppermute | solution.py:125
  16.7 1.8 %collective-permute-start.6 = (bf16[256,384]{1,0:T(8,128)(2,1)S(1)}, bf16[256,384]{1,0:T(8,128)(2,1)S(1)}, u32[]{:S(2)}, u32[]{:S(2)}) collective-permute-start(bf16[256,384]{1,0:T(8,128)(2,1)S(1)} %collective-permute-done.2.refs_4_), channel_id=1, source_target_pairs={{0,2},{1,5},{2,0},{3,7},{4,6},{5,1},{6,4},{7,3},{8,10},{9,13},{10,... | collective-permute-start | bytes 589832 | tf_op jit(solution)/shard_map/ppermute | solution.py:125
  18.7 1.5 %collective-permute-start.14 = (bf16[256,384]{1,0:T(8,128)(2,1)}, bf16[256,384]{1,0:T(8,128)(2,1)S(1)}, u32[]{:S(2)}, u32[]{:S(2)}) collective-permute-start(bf16[256,384]{1,0:T(8,128)(2,1)} %collective-permute-done.8.refs_3_), channel_id=1, source_target_pairs={{0,4},{1,3},{2,6},{3,1},{4,0},{5,7},{6,2},{7,5},{8,12},{9,11},{10,... | collective-permute-start | bytes 589832 | tf_op jit(solution)/shard_map/ppermute | solution.py:125
  20.5 1.2 %collective-permute-done.12.refs_9_ = bf16[256,384]{1,0:T(8,128)(2,1)S(1)} collective-permute-done((bf16[256,384]{1,0:T(8,128)(2,1)}, bf16[256,384]{1,0:T(8,128)(2,1)S(1)}, u32[]{:S(2)}, u32[]{:S(2)}) %collective-permute-start.12) | collective-permute-done | bytes 196640 | tf_op jit(solution)/shard_map/ppermute | solution.py:125
  22.3 2.3 %collective-permute-start.16 = (bf16[256,384]{1,0:T(8,128)(2,1)S(1)}, bf16[256,384]{1,0:T(8,128)(2,1)S(1)}, u32[]{:S(2)}, u32[]{:S(2)}) collective-permute-start(bf16[256,384]{1,0:T(8,128)(2,1)S(1)} %collective-permute-done.11.refs_8_), channel_id=1, source_target_pairs={{0,24},{1,25},{2,26},{3,27},{4,28},{5,29},{6,30},{7,31},{8,16},{9,... | collective-permute-start | bytes 589832 | tf_op jit(solution)/shard_map/ppermute | solution.py:125
  24.7 2.9 %shard_map.39.refs_6_ = f32[2,384,384]{2,1,0:T(8,128)S(1)} custom-call(bf16[384,4096]{1,0:T(8,128)(2,1)S(1)} %bitcast.5, bf16[384,4096]{1,0:T(8,128)(2,1)S(1)} %get-tuple-element.17.refs_1_, bf16[256,384]{1,0:T(8,128)(2,1)S(1)} %shard_map.38.refs_2_, bf16[256,384]{1,0:T(8,128)(2,1)} %collective-permute-done.8.refs_3_, ...), custom_call_target="tpu_custom_call" | custom-call | flops 1207959552 | bytes 7077888 | tf_op jit(solution)/shard_map/pallas_call | solution.py:377
  27.6 2.0 %collective-permute-start.13 = (bf16[256,384]{1,0:T(8,128)(2,1)S(1)}, bf16[256,384]{1,0:T(8,128)(2,1)S(1)}, u32[]{:S(2)}, u32[]{:S(2)}) collective-permute-start(bf16[256,384]{1,0:T(8,128)(2,1)S(1)} %collective-permute-done.3.refs_7_), channel_id=1, source_target_pairs={{0,2},{1,5},{2,0},{3,7},{4,6},{5,1},{6,4},{7,3},{8,10},{9,13},{10,... | collective-permute-start | bytes 589832 | tf_op jit(solution)/shard_map/ppermute | solution.py:125
  29.6 1.5 %collective-permute-start.4 = (bf16[256,384]{1,0:T(8,128)(2,1)S(1)}, bf16[256,384]{1,0:T(8,128)(2,1)S(1)}, u32[]{:S(2)}, u32[]{:S(2)}) collective-permute-start(bf16[256,384]{1,0:T(8,128)(2,1)S(1)} %collective-permute-done.3.refs_7_), channel_id=1, source_target_pairs={{0,4},{1,3},{2,6},{3,1},{4,0},{5,7},{6,2},{7,5},{8,12},{9,11},{10,... | collective-permute-start | bytes 589832 | tf_op jit(solution)/shard_map/ppermute | solution.py:125
  31.4 1.0 %shard_map.40.refs_5_ = f32[2,384,384]{2,1,0:T(8,128)S(1)} custom-call(bf16[384,4096]{1,0:T(8,128)(2,1)S(1)} %bitcast.6, bf16[384,4096]{1,0:T(8,128)(2,1)S(1)} %get-tuple-element.17.refs_1_, bf16[256,384]{1,0:T(8,128)(2,1)S(1)} %collective-permute-done.14.refs_2_, bf16[256,384]{1,0:T(8,128)(2,1)S(1)} %collective-permute-done.15.refs_3_, ...), custom_call_target="tpu_custom_call" | custom-call | flops 603979776 | bytes 4718592 | tf_op jit(solution)/shard_map/pallas_call | solution.py:377
  32.4 1.9 %collective-permute-done.13.refs_4_ = bf16[256,384]{1,0:T(8,128)(2,1)S(1)} collective-permute-done((bf16[256,384]{1,0:T(8,128)(2,1)S(1)}, bf16[256,384]{1,0:T(8,128)(2,1)S(1)}, u32[]{:S(2)}, u32[]{:S(2)}) %collective-permute-start.13) | collective-permute-done | bytes 196640 | tf_op jit(solution)/shard_map/ppermute | solution.py:125
  34.3 0.8 %shard_map.41.refs_3_ = f32[2,384,384]{2,1,0:T(8,128)S(1)} custom-call(bf16[384,4096]{1,0:T(8,128)(2,1)S(1)} %bitcast.7, bf16[384,4096]{1,0:T(8,128)(2,1)S(1)} %get-tuple-element.17.refs_1_, bf16[256,384]{1,0:T(8,128)(2,1)S(1)} %collective-permute-done.5.refs_2_, bf16[256,384]{1,0:T(8,128)(2,1)S(1)} %collective-permute-done.7.refs_3_, ...), custom_call_target="tpu_custom_call" | custom-call | flops 452984832 | bytes 4128768 | tf_op jit(solution)/shard_map/pallas_call | solution.py:377
  35.7 3.6 %collective-permute-start.17 = (bf16[384,512]{1,0:T(8,128)(2,1)S(1)}, bf16[384,512]{1,0:T(8,128)(2,1)S(1)}, u32[]{:S(2)}, u32[]{:S(2)}) collective-permute-start(bf16[384,512]{1,0:T(8,128)(2,1)S(1)} %get-tuple-element.24), channel_id=1, source_target_pairs={{0,1},{1,0},{2,3},{3,2},{4,5},{5,4},{6,7},{7,6},{8,9},{9,8},{10,11... | collective-permute-start | bytes 1179656 | tf_op jit(solution)/shard_map/ppermute | solution.py:129
  39.2 0.7 %shard_map.43 = (bf16[3,256,768]{2,1,0:T(8,128)(2,1)S(1)}, bf16[128,768]{1,0:T(8,128)(2,1)S(1)}) custom-call(bf16[384,512]{1,0:T(8,128)(2,1)S(1)} %get-tuple-element.23.keep_ref, f32[384,1]{1,0:T(8,128)S(1)} %get-tuple-element.25.column_ref, f32[1,768]{1,0:T(1,128)S(1)} %get-tuple-element.26.row_ref), custom_call_target="tpu_custom_call" | custom-call | flops 75497472 | bytes 589824 | tf_op jit(solution)/shard_map/pallas_call | solution.py:442
  39.9 0.6 %collective-permute-done.17.recv_ref = bf16[384,512]{1,0:T(8,128)(2,1)S(1)} collective-permute-done((bf16[384,512]{1,0:T(8,128)(2,1)S(1)}, bf16[384,512]{1,0:T(8,128)(2,1)S(1)}, u32[]{:S(2)}, u32[]{:S(2)}) %collective-permute-start.17) | collective-permute-done | bytes 393248 | tf_op jit(solution)/shard_map/ppermute | solution.py:129
  40.6 2.1 %shard_map.44 = bf16[384,512]{1,0:T(8,128)(2,1)} custom-call(bf16[384,512]{1,0:T(8,128)(2,1)S(1)} %get-tuple-element.23.keep_ref, bf16[384,512]{1,0:T(8,128)(2,1)S(1)} %collective-permute-done.17.recv_ref, bf16[3,256,768]{2,1,0:T(8,128)(2,1)S(1)} %get-tuple-element.27.probs_ref, bf16[128,768]{1,0:T(8,128)(2,1)S(1)} %get-tuple-element.28.keys_ref, ...), custom_call_target="tpu_custom_call" | custom-call | flops 603979776 | bytes 1572864 | tf_op jit(solution)/shard_map/pallas_call | solution.py:457
  (31 shorter events, 2.6 us)
Async XLA Ops:
  0.0 12.1 %copy-start.2 = (s32[1,384]{1,0:T(1,128)S(1)}, s32[1,384]{1,0:T(1,128)}, u32[]{:S(2)}) copy-start(s32[1,384]{1,0:T(1,128)} %docs_ref.1) | copy-start | bytes 4612
  0.0 20.1 %collective-permute-start = (bf16[384,4096]{1,0:T(8,128)(2,1)}, bf16[384,4096]{1,0:T(8,128)(2,1)S(1)}, u32[]{:S(2)}, u32[]{:S(2)}) collective-permute-start(bf16[384,4096]{1,0:T(8,128)(2,1)} %bitcast.4), channel_id=1, source_target_pairs={{0,1},{1,0},{2,3},{3,2},{4,5},{5,4},{6,7},{7,6},{8,9},{9,8},{10,11... | collective-permute-start | bytes 9437192 | tf_op jit(solution)/shard_map/ppermute | solution.py:129
  0.1 1.0 %copy-start.1 = (bf16[256,768]{1,0:T(8,128)(2,1)S(1)}, bf16[256,768]{1,0:T(8,128)(2,1)}, u32[]{:S(2)}) copy-start(bf16[256,768]{1,0:T(8,128)(2,1)} %weight_ref.1) | copy-start | bytes 1179652
  1.1 11.0 %collective-permute-start.8 = (bf16[256,384]{1,0:T(8,128)(2,1)S(1)}, bf16[256,384]{1,0:T(8,128)(2,1)}, u32[]{:S(2)}, u32[]{:S(2)}) collective-permute-start(bf16[256,384]{1,0:T(8,128)(2,1)S(1)} %shard_map.38.refs_2_), channel_id=1, source_target_pairs={{0,8},{1,9},{2,10},{3,11},{4,12},{5,13},{6,14},{7,15},{8,0},{9,1},... | collective-permute-start | bytes 589832 | tf_op jit(solution)/shard_map/ppermute | solution.py:125
  3.9 11.5 %collective-permute-start.10 = (bf16[256,384]{1,0:T(8,128)(2,1)S(1)}, bf16[256,384]{1,0:T(8,128)(2,1)}, u32[]{:S(2)}, u32[]{:S(2)}) collective-permute-start(bf16[256,384]{1,0:T(8,128)(2,1)S(1)} %shard_map.38.refs_2_), channel_id=1, source_target_pairs={{0,4},{1,3},{2,6},{3,1},{4,0},{5,7},{6,2},{7,5},{8,12},{9,11},{10,... | collective-permute-start | bytes 589832 | tf_op jit(solution)/shard_map/ppermute | solution.py:125
  5.1 11.6 %collective-permute-start.2 = (bf16[256,384]{1,0:T(8,128)(2,1)S(1)}, bf16[256,384]{1,0:T(8,128)(2,1)S(1)}, u32[]{:S(2)}, u32[]{:S(2)}) collective-permute-start(bf16[256,384]{1,0:T(8,128)(2,1)S(1)} %shard_map.38.refs_2_), channel_id=1, source_target_pairs={{0,16},{1,17},{2,18},{3,19},{4,20},{5,21},{6,22},{7,23},{8,24},{9,... | collective-permute-start | bytes 589832 | tf_op jit(solution)/shard_map/ppermute | solution.py:125
  7.4 5.3 %collective-permute-start.9 = (bf16[256,384]{1,0:T(8,128)(2,1)S(1)}, bf16[256,384]{1,0:T(8,128)(2,1)}, u32[]{:S(2)}, u32[]{:S(2)}) collective-permute-start(bf16[256,384]{1,0:T(8,128)(2,1)S(1)} %shard_map.38.refs_2_), channel_id=1, source_target_pairs={{0,2},{1,5},{2,0},{3,7},{4,6},{5,1},{6,4},{7,3},{8,10},{9,13},{10,... | collective-permute-start | bytes 589832 | tf_op jit(solution)/shard_map/ppermute | solution.py:125
  12.1 4.6 %collective-permute-start.1 = (s32[1,384]{1,0:T(1,128)S(1)}, s32[1,384]{1,0:T(1,128)S(1)}, u32[]{:S(2)}, u32[]{:S(2)}) collective-permute-start(s32[1,384]{1,0:T(1,128)S(1)} %copy-done.2), channel_id=1, source_target_pairs={{0,1},{1,0},{2,3},{3,2},{4,5},{5,4},{6,7},{7,6},{8,9},{9,8},{10,11... | collective-permute-start | bytes 4616 | tf_op jit(solution)/shard_map/ppermute | solution.py:129
  12.8 5.9 %collective-permute-start.11 = (bf16[256,384]{1,0:T(8,128)(2,1)}, bf16[256,384]{1,0:T(8,128)(2,1)S(1)}, u32[]{:S(2)}, u32[]{:S(2)}) collective-permute-start(bf16[256,384]{1,0:T(8,128)(2,1)} %collective-permute-done.9.refs_5_), channel_id=1, source_target_pairs={{0,4},{1,3},{2,6},{3,1},{4,0},{5,7},{6,2},{7,5},{8,12},{9,11},{10,... | collective-permute-start | bytes 589832 | tf_op jit(solution)/shard_map/ppermute | solution.py:125
  15.4 6.3 %collective-permute-start.12 = (bf16[256,384]{1,0:T(8,128)(2,1)}, bf16[256,384]{1,0:T(8,128)(2,1)S(1)}, u32[]{:S(2)}, u32[]{:S(2)}) collective-permute-start(bf16[256,384]{1,0:T(8,128)(2,1)} %collective-permute-done.8.refs_3_), channel_id=1, source_target_pairs={{0,2},{1,5},{2,0},{3,7},{4,6},{5,1},{6,4},{7,3},{8,10},{9,13},{10,... | collective-permute-start | bytes 589832 | tf_op jit(solution)/shard_map/ppermute | solution.py:125
  16.7 8.0 %copy-start = (bf16[1,384,4096]{2,1,0:T(8,128)(2,1)S(1)}, bf16[1,384,4096]{2,1,0:T(8,128)(2,1)}, u32[]{:S(2)}) copy-start(bf16[1,384,4096]{2,1,0:T(8,128)(2,1)} %param.3) | copy-start | bytes 9437188
  16.7 5.6 %collective-permute-start.3 = (bf16[256,384]{1,0:T(8,128)(2,1)S(1)}, bf16[256,384]{1,0:T(8,128)(2,1)S(1)}, u32[]{:S(2)}, u32[]{:S(2)}) collective-permute-start(bf16[256,384]{1,0:T(8,128)(2,1)S(1)} %collective-permute-done.2.refs_4_), channel_id=1, source_target_pairs={{0,8},{1,9},{2,10},{3,11},{4,12},{5,13},{6,14},{7,15},{8,0},{9,1},... | collective-permute-start | bytes 589832 | tf_op jit(solution)/shard_map/ppermute | solution.py:125
  16.7 7.9 %collective-permute-start.6 = (bf16[256,384]{1,0:T(8,128)(2,1)S(1)}, bf16[256,384]{1,0:T(8,128)(2,1)S(1)}, u32[]{:S(2)}, u32[]{:S(2)}) collective-permute-start(bf16[256,384]{1,0:T(8,128)(2,1)S(1)} %collective-permute-done.2.refs_4_), channel_id=1, source_target_pairs={{0,2},{1,5},{2,0},{3,7},{4,6},{5,1},{6,4},{7,3},{8,10},{9,13},{10,... | collective-permute-start | bytes 589832 | tf_op jit(solution)/shard_map/ppermute | solution.py:125
  18.7 8.9 %collective-permute-start.14 = (bf16[256,384]{1,0:T(8,128)(2,1)}, bf16[256,384]{1,0:T(8,128)(2,1)S(1)}, u32[]{:S(2)}, u32[]{:S(2)}) collective-permute-start(bf16[256,384]{1,0:T(8,128)(2,1)} %collective-permute-done.8.refs_3_), channel_id=1, source_target_pairs={{0,4},{1,3},{2,6},{3,1},{4,0},{5,7},{6,2},{7,5},{8,12},{9,11},{10,... | collective-permute-start | bytes 589832 | tf_op jit(solution)/shard_map/ppermute | solution.py:125
  20.1 9.5 %collective-permute-start.15 = (bf16[256,384]{1,0:T(8,128)(2,1)S(1)}, bf16[256,384]{1,0:T(8,128)(2,1)S(1)}, u32[]{:S(2)}, u32[]{:S(2)}) collective-permute-start(bf16[256,384]{1,0:T(8,128)(2,1)S(1)} %collective-permute-done.11.refs_8_), channel_id=1, source_target_pairs={{0,8},{1,9},{2,10},{3,11},{4,12},{5,13},{6,14},{7,15},{8,0},{9,1},... | collective-permute-start | bytes 589832 | tf_op jit(solution)/shard_map/ppermute | solution.py:125
  21.7 10.7 %collective-permute-start.5 = (bf16[256,384]{1,0:T(8,128)(2,1)S(1)}, bf16[256,384]{1,0:T(8,128)(2,1)S(1)}, u32[]{:S(2)}, u32[]{:S(2)}) collective-permute-start(bf16[256,384]{1,0:T(8,128)(2,1)S(1)} %collective-permute-done.2.refs_4_), channel_id=1, source_target_pairs={{0,4},{1,3},{2,6},{3,1},{4,0},{5,7},{6,2},{7,5},{8,12},{9,11},{10,... | collective-permute-start | bytes 589832 | tf_op jit(solution)/shard_map/ppermute | solution.py:125
  22.3 9.1 %collective-permute-start.16 = (bf16[256,384]{1,0:T(8,128)(2,1)S(1)}, bf16[256,384]{1,0:T(8,128)(2,1)S(1)}, u32[]{:S(2)}, u32[]{:S(2)}) collective-permute-start(bf16[256,384]{1,0:T(8,128)(2,1)S(1)} %collective-permute-done.11.refs_8_), channel_id=1, source_target_pairs={{0,24},{1,25},{2,26},{3,27},{4,28},{5,29},{6,30},{7,31},{8,16},{9,... | collective-permute-start | bytes 589832 | tf_op jit(solution)/shard_map/ppermute | solution.py:125
  24.6 7.8 %collective-permute-start.7 = (bf16[256,384]{1,0:T(8,128)(2,1)S(1)}, bf16[256,384]{1,0:T(8,128)(2,1)S(1)}, u32[]{:S(2)}, u32[]{:S(2)}) collective-permute-start(bf16[256,384]{1,0:T(8,128)(2,1)S(1)} %collective-permute-done.6.refs_5_), channel_id=1, source_target_pairs={{0,4},{1,3},{2,6},{3,1},{4,0},{5,7},{6,2},{7,5},{8,12},{9,11},{10,... | collective-permute-start | bytes 589832 | tf_op jit(solution)/shard_map/ppermute | solution.py:125
  27.6 6.7 %collective-permute-start.13 = (bf16[256,384]{1,0:T(8,128)(2,1)S(1)}, bf16[256,384]{1,0:T(8,128)(2,1)S(1)}, u32[]{:S(2)}, u32[]{:S(2)}) collective-permute-start(bf16[256,384]{1,0:T(8,128)(2,1)S(1)} %collective-permute-done.3.refs_7_), channel_id=1, source_target_pairs={{0,2},{1,5},{2,0},{3,7},{4,6},{5,1},{6,4},{7,3},{8,10},{9,13},{10,... | collective-permute-start | bytes 589832 | tf_op jit(solution)/shard_map/ppermute | solution.py:125
  29.6 5.4 %collective-permute-start.4 = (bf16[256,384]{1,0:T(8,128)(2,1)S(1)}, bf16[256,384]{1,0:T(8,128)(2,1)S(1)}, u32[]{:S(2)}, u32[]{:S(2)}) collective-permute-start(bf16[256,384]{1,0:T(8,128)(2,1)S(1)} %collective-permute-done.3.refs_7_), channel_id=1, source_target_pairs={{0,4},{1,3},{2,6},{3,1},{4,0},{5,7},{6,2},{7,5},{8,12},{9,11},{10,... | collective-permute-start | bytes 589832 | tf_op jit(solution)/shard_map/ppermute | solution.py:125
  35.7 4.9 %collective-permute-start.17 = (bf16[384,512]{1,0:T(8,128)(2,1)S(1)}, bf16[384,512]{1,0:T(8,128)(2,1)S(1)}, u32[]{:S(2)}, u32[]{:S(2)}) collective-permute-start(bf16[384,512]{1,0:T(8,128)(2,1)S(1)} %get-tuple-element.24), channel_id=1, source_target_pairs={{0,1},{1,0},{2,3},{3,2},{4,5},{5,4},{6,7},{7,6},{8,9},{9,8},{10,11... | collective-permute-start | bytes 1179656 | tf_op jit(solution)/shard_map/ppermute | solution.py:129

commit v4 on v3

--- a/solution.py
+++ b/solution.py
@@ -15,6 +15,8 @@
 THETA = 1000000.0
 
 STEP = 128
+
+OWN_PARTS = 4
 
 VMEM_LIMIT = 16 * 1024 * 1024
 
@@ -133,22 +135,34 @@
     return lax.optimization_barrier((value,) + others)[0]
 
 
-def add_blocks(total, parts, masks, mine_ref, other_ref):
-    rows = parts[0].shape[0]
+def add_blocks(total, parts, masks, late, mine_ref, other_ref, held, sems):
+    rows = mine_ref.shape[1] // lax.axis_size("fsdp")
     chip = lax.axis_index("fsdp")
     core = lax.axis_index("ctx")
+    copies = [
+        pltpu.make_async_copy(part, held.at[place], sems.at[place])
+        for place, part in enumerate(parts[late:])
+    ]
+    for copy in copies:
+        copy.start()
     sums = [None, None] if total is None else [total[0], total[1]]
-    for part, (first_mask, second_mask) in zip(parts, masks):
-        source = jnp.where(core == 0, chip ^ first_mask, chip ^ second_mask)
-        columns = pl.ds(pl.multiple_of(source * rows, rows), rows)
-        weights = part[...]
-        for side, ref in enumerate((mine_ref, other_ref)):
-            term = jnp.dot(ref[:, columns], weights, preferred_element_type=jnp.float32)
-            sums[side] = term if sums[side] is None else sums[side] + term
+    for place, (part, blocks) in enumerate(zip(parts, masks)):
+        if place >= late:
+            copies[place - late].wait()
+        for number, (first_mask, second_mask) in enumerate(blocks):
+            source = jnp.where(core == 0, chip ^ first_mask, chip ^ second_mask)
+            columns = pl.ds(pl.multiple_of(source * rows, rows), rows)
+            if place < late:
+                weights = part[number * rows : (number + 1) * rows]
+            else:
+                weights = held[place - late]
+            for side, ref in enumerate((mine_ref, other_ref)):
+                term = jnp.dot(ref[:, columns], weights, preferred_element_type=jnp.float32)
+                sums[side] = term if sums[side] is None else sums[side] + term
     return sums
 
 
-def partial_kernel(masks, begun, *refs):
+def partial_kernel(masks, late, begun, *refs):
     count = len(masks)
     mine_ref, other_ref = refs[:2]
     parts = refs[2 : 2 + count]
@@ -156,18 +170,18 @@
     total = None
     if begun:
         total, rest = rest[0], rest[1:]
-    (out_ref,) = rest
-    sums = add_blocks(total, parts, masks, mine_ref, other_ref)
+    out_ref, held, sems = rest
+    sums = add_blocks(total, parts, masks, late, mine_ref, other_ref, held, sems)
     out_ref[0] = sums[0]
     out_ref[1] = sums[1]
 
 
-def final_kernel(masks, *refs):
+def final_kernel(masks, late, *refs):
     count = len(masks)
     mine_ref, other_ref = refs[:2]
     parts = refs[2 : 2 + count]
-    total, cos_ref, sin_ref, keep_ref, send_ref = refs[2 + count :]
-    sums = add_blocks(total, parts, masks, mine_ref, other_ref)
+    total, cos_ref, sin_ref, keep_ref, send_ref, held, sems = refs[2 + count :]
+    sums = add_blocks(total, parts, masks, late, mine_ref, other_ref, held, sems)
     turned = lax.axis_index("ctx") == 1
 
     def turn(block, cosine, sine):
@@ -331,20 +345,24 @@
     )(value, docs, docs_other)
 
 
-def own_kernel(weight_ref, out_ref, sems):
+def own_kernel(weight_ref, out_ref, sem):
     core = lax.axis_index("ctx")
-    copies = [
-        pltpu.make_async_copy(
-            weight_ref.at[:, pl.ds(pl.multiple_of(core * 2 * HD, 2 * HD), 2 * HD)],
-            out_ref.at[:, pl.ds(0, 2 * HD)],
-            sems.at[0],
-        ),
-        pltpu.make_async_copy(
-            weight_ref.at[:, pl.ds(pl.multiple_of((HEADS + 1 - core) * HD, HD), HD)],
-            out_ref.at[:, pl.ds(2 * HD, HD)],
-            sems.at[1],
-        ),
-    ]
+    rows = weight_ref.shape[0]
+    part = rows // OWN_PARTS
+    copies = []
+    for first in range(0, rows, part):
+        place = pl.ds(first, part)
+        for column, source, width in (
+            (0, pl.multiple_of(core * 2 * HD, 2 * HD), 2 * HD),
+            (2 * HD, pl.multiple_of((HEADS + 1 - core) * HD, HD), HD),
+        ):
+            copies.append(
+                pltpu.make_async_copy(
+                    weight_ref.at[place, pl.ds(source, width)],
+                    out_ref.at[place, pl.ds(column, width)],
+                    sem.at[len(copies)],
+                )
+            )
     for copy in copies:
         copy.start()
     for copy in copies:
@@ -355,39 +373,48 @@
     return pl.pallas_call(
         own_kernel,
         out_shape=jax.ShapeDtypeStruct((weight.shape[0], 3 * HD), weight.dtype),
-        in_specs=[ANY],
+        in_specs=[pl.BlockSpec(memory_space=pltpu.HBM)],
         out_specs=VMEM,
-        scratch_shapes=[pltpu.SemaphoreType.DMA((2,))],
+        scratch_shapes=[pltpu.SemaphoreType.DMA((2 * OWN_PARTS,))],
         compiler_params=pltpu.CompilerParams(vmem_limit_bytes=VMEM_LIMIT),
-    )(weight)
-
-
-def partial(mine, other, parts, masks, total=None, tables=None):
-    rows, width = parts[0].shape
+    )(pltpu.with_memory_space_constraint(weight, pltpu.HBM))
+
+
+def partial(mine, other, parts, masks, total=None, tables=None, late=None):
+    width = parts[0].shape[1]
     tokens = mine.shape[0]
     count = len(parts)
+    rows = sum(part.shape[0] for part in parts)
+    late = count if late is None else late
     begun = total is not None
     cost = pl.CostEstimate(
-        flops=4 * tokens * rows * width * count,
-        bytes_accessed=count * rows * (width + 2 * tokens) * 2 + 16 * tokens * width,
+        flops=4 * tokens * rows * width,
+        bytes_accessed=rows * (width + 2 * tokens) * 2 + 16 * tokens * width,
         transcendentals=0,
     )
+    part_specs = [VMEM] * late + [ANY] * (count - late)
+    scratch = [
+        pltpu.VMEM((max(1, count - late),) + parts[-1].shape, mine.dtype),
+        pltpu.SemaphoreType.DMA((max(1, count - late),)),
+    ]
     params = pltpu.CompilerParams(vmem_limit_bytes=VMEM_LIMIT)
     if tables is None:
         return pl.pallas_call(
-            functools.partial(partial_kernel, masks, begun),
+            functools.partial(partial_kernel, masks, late, begun),
             out_shape=jax.ShapeDtypeStruct((2, tokens, width), jnp.float32),
-            in_specs=[VMEM] * (2 + count + begun),
+            in_specs=[VMEM] * 2 + part_specs + [VMEM] * begun,
             out_specs=VMEM,
+            scratch_shapes=scratch,
             compiler_params=params,
             cost_estimate=cost,
         )(mine, other, *parts, *([total] if begun else []))
     out = jax.ShapeDtypeStruct((tokens, 4 * HD), jnp.bfloat16)
     return pl.pallas_call(
-        functools.partial(final_kernel, masks),
+        functools.partial(final_kernel, masks, late),
         out_shape=(out, out),
-        in_specs=[VMEM] * (count + 5),
+        in_specs=[VMEM] * 2 + part_specs + [VMEM] * 3,
         out_specs=(VMEM, VMEM),
+        scratch_shapes=scratch,
         compiler_params=params,
         cost_estimate=cost,
     )(mine, other, *parts, total, *tables)
@@ -410,31 +437,30 @@
     sines = jnp.concatenate([-sine, sine], axis=-1)
     other, column, row = stage(swap(mine), doc_ids, swap(doc_ids))
     z1 = flip(own, 4, 4)
+    a0 = flip(own, 1, 2)
     z2 = flip(own, 8, 8)
-    a0 = flip(own, 1, 2)
-    b0 = flip(own, 2, 1)
-    z3 = flip(z2, 4, 4)
-    c0 = flip(a0, 2, 1)
-    a1 = flip(after(z1, b0), 1, 2)
-    K1 = partial(mine, other, [own, z1, z2, a0, b0, z3, c0, a1], [(0, 0), (4, 4), (8, 8), (1, 2), (2, 1), (12, 12), (3, 3), (5, 6)])
-    b1 = flip(z1, 2, 1)
-    c1 = flip(c0, 4, 4)
-    c3 = flip(c0, 12, 12)
+    a1 = flip(z1, 1, 2)
     (z2_a2, cosines, sines,) = lax.optimization_barrier(
         (z2, cosines, sines)
     )
     a2 = flip(z2_a2, 1, 2)
-    K2 = partial(mine, other, [b1, c1, c3, a2], [(6, 5), (7, 7), (15, 15), (9, 10)], K1)
+    own_a0 = jnp.concatenate([own, a0])
+    B0 = flip(own_a0, 2, 1)
+    K1 = partial(mine, other, [own, z2, a1, a2, B0, z1, a0], [[(0, 0)], [(8, 8)], [(5, 6)], [(9, 10)], [(2, 1), (3, 3)], [(4, 4)], [(1, 2)]], late=5)
+    z3 = flip(z2, 4, 4)
+    C1 = flip(B0, 4, 4)
     b2 = flip(z2, 2, 1)
+    K2 = partial(mine, other, [z3, C1, b2], [[(12, 12)], [(6, 5), (7, 7)], [(10, 9)]], K1)
+    a3 = flip(z3, 1, 2)
     c2 = flip(a2, 2, 1)
-    (z3_a3, K1,) = lax.optimization_barrier(
+    (z3_b3, K1,) = lax.optimization_barrier(
         (z3, K1)
     )
-    a3 = flip(z3_a3, 1, 2)
-    K3 = partial(mine, other, [b2, c2, a3], [(10, 9), (11, 11), (13, 14)], K2)
-    b3 = flip(z3, 2, 1)
+    b3 = flip(z3_b3, 2, 1)
+    K3 = partial(mine, other, [a3, c2, b3], [[(13, 14)], [(11, 11)], [(14, 13)]], K2)
+    c3 = flip(a3, 2, 1)
     keep, send = partial(
-        mine, other, [b3], [(14, 13)], K3, (cosines, sines)
+        mine, other, [c3], [[(15, 15)]], K3, (cosines, sines)
     )
     recv = swap(send)
     steps = tokens // STEP

time: 42.9 us -> 41.6 us (0.970)
  starting transfers between devices: 25.2 us -> 16.9 us
  waiting for transfers between devices: 6 us -> 12.9 us
  Pallas kernels: 8.46 us -> 9.53 us
  local copies, waits for them, and re-layouts: 1 us -> 0.01 us
    ppermute x15 -> x13, waiting for transfers between devices: 5.35 us -> 12.3 us  [flip(): return lax.ppermute(value, ('fsdp', 'ctx'), pairs)]
    ppermute x15 -> x13, starting transfers between devices: 20.9 us -> 14.1 us  [flip(): return lax.ppermute(value, ('fsdp', 'ctx'), pairs)]
    ppermute x3, starting transfers between devices: 4.31 us -> 2.78 us  [swap(): return lax.ppermute(value, 'ctx', [(0, 1), (1, 0)])]
    unnamed x6 -> x4, local copies, waits for them, and re-layouts: 1 us -> 0.01 us
    pallas_call x1, Pallas kernels: 0.04 us -> 0.93 us  [own_columns(): pl.pallas_call(own_kernel, out_shape=jax.ShapeDtypeStruct((weight.shape[0...]
  transfers between devices with their start and end apart: 18 -> 16, of which waited for: 6 -> 10; matrix products, arithmetic and copies ran while one was open for 4% -> 5% of each run, Pallas kernels for 14% -> 17%
where the time goes in v4:
time: 41.6 us; the launch traced here: 41.4 us
  starting transfers between devices  16.9 us (41%)
  waiting for transfers between devices  12.9 us (31%)
  Pallas kernels  9.53 us (23%)
  other arithmetic  1.91 us (5%)
    ppermute x13, starting transfers between devices, flip(): return lax.ppermute(value, ('fsdp', 'ctx'), pairs)  14.1 us
    ppermute x13, waiting for transfers between devices, flip(): return lax.ppermute(value, ('fsdp', 'ctx'), pairs)  12.3 us
    pallas_call x3, Pallas kernels, partial(): pl.pallas_call(functools.partial(partial_kernel, masks, late, begun), out...  4.86 us
    ppermute x3, starting transfers between devices, swap(): return lax.ppermute(value, 'ctx', [(0, 1), (1, 0)])  2.78 us
    pallas_call x1, Pallas kernels, paired_body(): pl.pallas_call(attention_kernel, out_shape=jax.ShapeDtypeStruct((tokens,...  2.14 us
    neg x1, other arithmetic, paired_body(): sines = jnp.concatenate([-sine, sine], axis=-1)  1.44 us
    pallas_call x1, Pallas kernels, own_columns(): pl.pallas_call(own_kernel, out_shape=jax.ShapeDtypeStruct((weight.shape[0...  0.93 us
  transfers between devices with their start and end apart: 16, of which 10 were waited for; matrix products, arithmetic and copies ran while one was open for 5% of the time, Pallas kernels for 17%

profile of v4, /device:TPU:1, one launch (start us, length us, event | category | flops | bytes accessed | tf_op | source)
XLA Modules:
  0.0 41.4 jit_solution(13429736674679493664)
XLA Ops:
  0.1 0.9 %shard_map.38.refs_2_ = bf16[256,384]{1,0:T(8,128)(2,1)S(1)} custom-call(bf16[256,768]{1,0:T(8,128)(2,1)} %weight_ref.1), custom_call_target="tpu_custom_call" | custom-call | tf_op jit(solution)/shard_map/pallas_call | solution.py:373
  1.0 3.8 %collective-permute-start.2 = (bf16[256,384]{1,0:T(8,128)(2,1)S(1)}, bf16[256,384]{1,0:T(8,128)(2,1)}, u32[]{:S(2)}, u32[]{:S(2)}) collective-permute-start(bf16[256,384]{1,0:T(8,128)(2,1)S(1)} %shard_map.38.refs_2_), channel_id=1, source_target_pairs={{0,16},{1,17},{2,18},{3,19},{4,20},{5,21},{6,22},{7,23},{8,24},{9,... | collective-permute-start | bytes 589832 | tf_op jit(solution)/shard_map/ppermute | solution.py:127
  4.8 1.3 %collective-permute-start.8 = (bf16[256,384]{1,0:T(8,128)(2,1)S(1)}, bf16[256,384]{1,0:T(8,128)(2,1)}, u32[]{:S(2)}, u32[]{:S(2)}) collective-permute-start(bf16[256,384]{1,0:T(8,128)(2,1)S(1)} %shard_map.38.refs_2_), channel_id=1, source_target_pairs={{0,8},{1,9},{2,10},{3,11},{4,12},{5,13},{6,14},{7,15},{8,0},{9,1},... | collective-permute-start | bytes 589832 | tf_op jit(solution)/shard_map/ppermute | solution.py:127
  6.1 1.2 %collective-permute-start.10 = (bf16[256,384]{1,0:T(8,128)(2,1)S(1)}, bf16[256,384]{1,0:T(8,128)(2,1)S(1)}, u32[]{:S(2)}, u32[]{:S(2)}) collective-permute-start(bf16[256,384]{1,0:T(8,128)(2,1)S(1)} %shard_map.38.refs_2_), channel_id=1, source_target_pairs={{0,2},{1,5},{2,0},{3,7},{4,6},{5,1},{6,4},{7,3},{8,10},{9,13},{10,... | collective-permute-start | bytes 589832 | tf_op jit(solution)/shard_map/ppermute | solution.py:127
  7.4 0.8 %collective-permute-start.1 = (s32[1,384]{1,0:T(1,128)}, s32[1,384]{1,0:T(1,128)S(1)}, u32[]{:S(2)}, u32[]{:S(2)}) collective-permute-start(s32[1,384]{1,0:T(1,128)} %docs_ref.1), channel_id=1, source_target_pairs={{0,1},{1,0},{2,3},{3,2},{4,5},{5,4},{6,7},{7,6},{8,9},{9,8},{10,11... | collective-permute-start | bytes 4616 | tf_op jit(solution)/shard_map/ppermute | solution.py:131
  8.3 2.7 %collective-permute-done.10.refs_8_ = bf16[256,384]{1,0:T(8,128)(2,1)S(1)} collective-permute-done((bf16[256,384]{1,0:T(8,128)(2,1)S(1)}, bf16[256,384]{1,0:T(8,128)(2,1)S(1)}, u32[]{:S(2)}, u32[]{:S(2)}) %collective-permute-start.10) | collective-permute-done | bytes 196640 | tf_op jit(solution)/shard_map/ppermute | solution.py:127
  11.1 1.3 %collective-permute-start.11 = (bf16[512,384]{1,0:T(8,128)(2,1)S(1)}, bf16[512,384]{1,0:T(8,128)(2,1)S(1)}, u32[]{:S(2)}, u32[]{:S(2)}) collective-permute-start(bf16[512,384]{1,0:T(8,128)(2,1)S(1)} %pad_maximum_fusion.2), channel_id=1, source_target_pairs={{0,4},{1,3},{2,6},{3,1},{4,0},{5,7},{6,2},{7,5},{8,12},{9,11},{10,... | collective-permute-start | bytes 1179656 | tf_op jit(solution)/shard_map/ppermute | solution.py:127
  12.4 1.4 %fusion = (f32[2,384,64]{2,1,0:T(8,128)S(1)}, f32[2,384,64]{2,1,0:T(8,128)S(1)}, f32[2,384,64]{2,1,0:T(8,128)S(1)}) fusion(f32[64]{0:T(128)S(1)} %multiply_exponential_fusion, f32[2,384]{1,0:T(2,128)S(1)} %add_convert_fusion), kind=kLoop, calls=%fused_computation.5 | loop fusion | flops 98304 | bytes 593152 | tf_op jit(solution)/shard_map/neg | solution.py:437
  15.2 1.3 %collective-permute-start.6 = (bf16[256,384]{1,0:T(8,128)(2,1)}, bf16[256,384]{1,0:T(8,128)(2,1)S(1)}, u32[]{:S(2)}, u32[]{:S(2)}) collective-permute-start(bf16[256,384]{1,0:T(8,128)(2,1)} %collective-permute-done.2.refs_3_), channel_id=1, source_target_pairs={{0,2},{1,5},{2,0},{3,7},{4,6},{5,1},{6,4},{7,3},{8,10},{9,13},{10,... | collective-permute-start | bytes 589832 | tf_op jit(solution)/shard_map/ppermute | solution.py:127
  16.7 1.3 %collective-permute-done.11.refs_6_ = bf16[512,384]{1,0:T(8,128)(2,1)S(1)} collective-permute-done((bf16[512,384]{1,0:T(8,128)(2,1)S(1)}, bf16[512,384]{1,0:T(8,128)(2,1)S(1)}, u32[]{:S(2)}, u32[]{:S(2)}) %collective-permute-start.11) | collective-permute-done | bytes 393248 | tf_op jit(solution)/shard_map/ppermute | solution.py:127
  18.2 1.8 %collective-permute-done.3.refs_2_ = bf16[256,384]{1,0:T(8,128)(2,1)S(1)} collective-permute-done((bf16[256,384]{1,0:T(8,128)(2,1)}, bf16[256,384]{1,0:T(8,128)(2,1)S(1)}, u32[]{:S(2)}, u32[]{:S(2)}) %collective-permute-start.3) | collective-permute-done | bytes 196640 | tf_op jit(solution)/shard_map/ppermute | solution.py:127
  20.0 1.3 %collective-permute-start.4 = (bf16[256,384]{1,0:T(8,128)(2,1)S(1)}, bf16[256,384]{1,0:T(8,128)(2,1)S(1)}, u32[]{:S(2)}, u32[]{:S(2)}) collective-permute-start(bf16[256,384]{1,0:T(8,128)(2,1)S(1)} %collective-permute-done.3.refs_2_), channel_id=1, source_target_pairs={{0,2},{1,5},{2,0},{3,7},{4,6},{5,1},{6,4},{7,3},{8,10},{9,13},{10,... | collective-permute-start | bytes 589832 | tf_op jit(solution)/shard_map/ppermute | solution.py:127
  21.9 1.2 %collective-permute-start.14 = (bf16[256,384]{1,0:T(8,128)(2,1)}, bf16[256,384]{1,0:T(8,128)(2,1)S(1)}, u32[]{:S(2)}, u32[]{:S(2)}) collective-permute-start(bf16[256,384]{1,0:T(8,128)(2,1)} %collective-permute-done.2.refs_3_), channel_id=1, source_target_pairs={{0,4},{1,3},{2,6},{3,1},{4,0},{5,7},{6,2},{7,5},{8,12},{9,11},{10,... | collective-permute-start | bytes 589832 | tf_op jit(solution)/shard_map/ppermute | solution.py:127
  23.9 3.1 %shard_map.39.refs_5_ = f32[2,384,384]{2,1,0:T(8,128)S(1)} custom-call(bf16[384,4096]{1,0:T(8,128)(2,1)S(1)} %bitcast.5, bf16[384,4096]{1,0:T(8,128)(2,1)S(1)} %get-tuple-element.16.refs_1_, bf16[256,384]{1,0:T(8,128)(2,1)S(1)} %shard_map.38.refs_2_, bf16[256,384]{1,0:T(8,128)(2,1)} %collective-permute-done.2.refs_3_, ...), custom_call_target="tpu_custom_call" | custom-call | flops 1207959552 | bytes 7077888 | tf_op jit(solution)/shard_map/pallas_call | solution.py:402
  27.0 1.3 %collective-permute-start.12 = (bf16[256,384]{1,0:T(8,128)(2,1)S(1)}, bf16[256,384]{1,0:T(8,128)(2,1)S(1)}, u32[]{:S(2)}, u32[]{:S(2)}) collective-permute-start(bf16[256,384]{1,0:T(8,128)(2,1)S(1)} %collective-permute-done.3.refs_2_), channel_id=1, source_target_pairs={{0,4},{1,3},{2,6},{3,1},{4,0},{5,7},{6,2},{7,5},{8,12},{9,11},{10,... | collective-permute-start | bytes 589832 | tf_op jit(solution)/shard_map/ppermute | solution.py:127
  28.5 1.0 %shard_map.40.refs_5_ = f32[2,384,384]{2,1,0:T(8,128)S(1)} custom-call(bf16[384,4096]{1,0:T(8,128)(2,1)S(1)} %bitcast.6, bf16[384,4096]{1,0:T(8,128)(2,1)S(1)} %get-tuple-element.16.refs_1_, bf16[256,384]{1,0:T(8,128)(2,1)S(1)} %collective-permute-done.3.refs_2_, bf16[512,384]{1,0:T(8,128)(2,1)S(1)} %collective-permute-done.13.refs_3_, ...), custom_call_target="tpu_custom_call" | custom-call | flops 603979776 | bytes 4718592 | tf_op jit(solution)/shard_map/pallas_call | solution.py:402
  29.5 1.6 %collective-permute-done.7.refs_3_ = bf16[256,384]{1,0:T(8,128)(2,1)S(1)} collective-permute-done((bf16[256,384]{1,0:T(8,128)(2,1)S(1)}, bf16[256,384]{1,0:T(8,128)(2,1)S(1)}, u32[]{:S(2)}, u32[]{:S(2)}) %collective-permute-start.7) | collective-permute-done | bytes 196640 | tf_op jit(solution)/shard_map/ppermute | solution.py:127
  31.2 2.1 %collective-permute-done.12.refs_4_ = bf16[256,384]{1,0:T(8,128)(2,1)S(1)} collective-permute-done((bf16[256,384]{1,0:T(8,128)(2,1)S(1)}, bf16[256,384]{1,0:T(8,128)(2,1)S(1)}, u32[]{:S(2)}, u32[]{:S(2)}) %collective-permute-start.12) | collective-permute-done | bytes 196640 | tf_op jit(solution)/shard_map/ppermute | solution.py:127
  33.3 0.8 %shard_map.41.refs_3_ = f32[2,384,384]{2,1,0:T(8,128)S(1)} custom-call(bf16[384,4096]{1,0:T(8,128)(2,1)S(1)} %bitcast.7, bf16[384,4096]{1,0:T(8,128)(2,1)S(1)} %get-tuple-element.16.refs_1_, bf16[256,384]{1,0:T(8,128)(2,1)S(1)} %collective-permute-done.4.refs_2_, bf16[256,384]{1,0:T(8,128)(2,1)S(1)} %collective-permute-done.7.refs_3_, ...), custom_call_target="tpu_custom_call" | custom-call | flops 452984832 | bytes 4128768 | tf_op jit(solution)/shard_map/pallas_call | solution.py:402
  34.1 1.3 %collective-permute-done.5.refs_2_ = bf16[256,384]{1,0:T(8,128)(2,1)S(1)} collective-permute-done((bf16[256,384]{1,0:T(8,128)(2,1)S(1)}, bf16[256,384]{1,0:T(8,128)(2,1)S(1)}, u32[]{:S(2)}, u32[]{:S(2)}) %collective-permute-start.5) | collective-permute-done | bytes 196640 | tf_op jit(solution)/shard_map/ppermute | solution.py:127
  36.0 1.9 %collective-permute-start.15 = (bf16[384,512]{1,0:T(8,128)(2,1)S(1)}, bf16[384,512]{1,0:T(8,128)(2,1)S(1)}, u32[]{:S(2)}, u32[]{:S(2)}) collective-permute-start(bf16[384,512]{1,0:T(8,128)(2,1)S(1)} %get-tuple-element.22), channel_id=1, source_target_pairs={{0,1},{1,0},{2,3},{3,2},{4,5},{5,4},{6,7},{7,6},{8,9},{9,8},{10,11... | collective-permute-start | bytes 1179656 | tf_op jit(solution)/shard_map/ppermute | solution.py:131
  37.9 0.7 %shard_map.43 = (bf16[3,256,768]{2,1,0:T(8,128)(2,1)S(1)}, bf16[128,768]{1,0:T(8,128)(2,1)S(1)}) custom-call(bf16[384,512]{1,0:T(8,128)(2,1)S(1)} %get-tuple-element.21.keep_ref, f32[384,1]{1,0:T(8,128)S(1)} %get-tuple-element.23.column_ref, f32[1,768]{1,0:T(1,128)S(1)} %get-tuple-element.24.row_ref), custom_call_target="tpu_custom_call" | custom-call | flops 75497472 | bytes 589824 | tf_op jit(solution)/shard_map/pallas_call | solution.py:468
  38.6 0.7 %collective-permute-done.15.recv_ref = bf16[384,512]{1,0:T(8,128)(2,1)S(1)} collective-permute-done((bf16[384,512]{1,0:T(8,128)(2,1)S(1)}, bf16[384,512]{1,0:T(8,128)(2,1)S(1)}, u32[]{:S(2)}, u32[]{:S(2)}) %collective-permute-start.15) | collective-permute-done | bytes 393248 | tf_op jit(solution)/shard_map/ppermute | solution.py:131
  39.2 2.1 %shard_map.44 = bf16[384,512]{1,0:T(8,128)(2,1)} custom-call(bf16[384,512]{1,0:T(8,128)(2,1)S(1)} %get-tuple-element.21.keep_ref, bf16[384,512]{1,0:T(8,128)(2,1)S(1)} %collective-permute-done.15.recv_ref, bf16[3,256,768]{2,1,0:T(8,128)(2,1)S(1)} %get-tuple-element.25.probs_ref, bf16[128,768]{1,0:T(8,128)(2,1)S(1)} %get-tuple-element.26.keys_ref, ...), custom_call_target="tpu_custom_call" | custom-call | flops 603979776 | bytes 1572864 | tf_op jit(solution)/shard_map/pallas_call | solution.py:483
  (26 shorter events, 4.2 us)
Async XLA Ops:
  0.0 23.2 %collective-permute-start = (bf16[384,4096]{1,0:T(8,128)(2,1)}, bf16[384,4096]{1,0:T(8,128)(2,1)S(1)}, u32[]{:S(2)}, u32[]{:S(2)}) collective-permute-start(bf16[384,4096]{1,0:T(8,128)(2,1)} %bitcast.4), channel_id=1, source_target_pairs={{0,1},{1,0},{2,3},{3,2},{4,5},{5,4},{6,7},{7,6},{8,9},{9,8},{10,11... | collective-permute-start | bytes 9437192 | tf_op jit(solution)/shard_map/ppermute | solution.py:131
  1.0 13.5 %collective-permute-start.2 = (bf16[256,384]{1,0:T(8,128)(2,1)S(1)}, bf16[256,384]{1,0:T(8,128)(2,1)}, u32[]{:S(2)}, u32[]{:S(2)}) collective-permute-start(bf16[256,384]{1,0:T(8,128)(2,1)S(1)} %shard_map.38.refs_2_), channel_id=1, source_target_pairs={{0,16},{1,17},{2,18},{3,19},{4,20},{5,21},{6,22},{7,23},{8,24},{9,... | collective-permute-start | bytes 589832 | tf_op jit(solution)/shard_map/ppermute | solution.py:127
  4.8 11.7 %collective-permute-start.8 = (bf16[256,384]{1,0:T(8,128)(2,1)S(1)}, bf16[256,384]{1,0:T(8,128)(2,1)}, u32[]{:S(2)}, u32[]{:S(2)}) collective-permute-start(bf16[256,384]{1,0:T(8,128)(2,1)S(1)} %shard_map.38.refs_2_), channel_id=1, source_target_pairs={{0,8},{1,9},{2,10},{3,11},{4,12},{5,13},{6,14},{7,15},{8,0},{9,1},... | collective-permute-start | bytes 589832 | tf_op jit(solution)/shard_map/ppermute | solution.py:127
  6.1 4.9 %collective-permute-start.10 = (bf16[256,384]{1,0:T(8,128)(2,1)S(1)}, bf16[256,384]{1,0:T(8,128)(2,1)S(1)}, u32[]{:S(2)}, u32[]{:S(2)}) collective-permute-start(bf16[256,384]{1,0:T(8,128)(2,1)S(1)} %shard_map.38.refs_2_), channel_id=1, source_target_pairs={{0,2},{1,5},{2,0},{3,7},{4,6},{5,1},{6,4},{7,3},{8,10},{9,13},{10,... | collective-permute-start | bytes 589832 | tf_op jit(solution)/shard_map/ppermute | solution.py:127
  7.4 7.8 %collective-permute-start.1 = (s32[1,384]{1,0:T(1,128)}, s32[1,384]{1,0:T(1,128)S(1)}, u32[]{:S(2)}, u32[]{:S(2)}) collective-permute-start(s32[1,384]{1,0:T(1,128)} %docs_ref.1), channel_id=1, source_target_pairs={{0,1},{1,0},{2,3},{3,2},{4,5},{5,4},{6,7},{7,6},{8,9},{9,8},{10,11... | collective-permute-start | bytes 4616 | tf_op jit(solution)/shard_map/ppermute | solution.py:131
  11.1 7.0 %collective-permute-start.11 = (bf16[512,384]{1,0:T(8,128)(2,1)S(1)}, bf16[512,384]{1,0:T(8,128)(2,1)S(1)}, u32[]{:S(2)}, u32[]{:S(2)}) collective-permute-start(bf16[512,384]{1,0:T(8,128)(2,1)S(1)} %pad_maximum_fusion.2), channel_id=1, source_target_pairs={{0,4},{1,3},{2,6},{3,1},{4,0},{5,7},{6,2},{7,5},{8,12},{9,11},{10,... | collective-permute-start | bytes 1179656 | tf_op jit(solution)/shard_map/ppermute | solution.py:127
  13.8 9.6 %copy-start.1 = (s32[1,384]{1,0:T(1,128)S(1)}, s32[1,384]{1,0:T(1,128)}, u32[]{:S(2)}) copy-start(s32[1,384]{1,0:T(1,128)} %docs_ref.1) | copy-start | bytes 4612
  14.5 5.5 %collective-permute-start.3 = (bf16[256,384]{1,0:T(8,128)(2,1)}, bf16[256,384]{1,0:T(8,128)(2,1)S(1)}, u32[]{:S(2)}, u32[]{:S(2)}) collective-permute-start(bf16[256,384]{1,0:T(8,128)(2,1)} %collective-permute-done.2.refs_3_), channel_id=1, source_target_pairs={{0,8},{1,9},{2,10},{3,11},{4,12},{5,13},{6,14},{7,15},{8,0},{9,1},... | collective-permute-start | bytes 589832 | tf_op jit(solution)/shard_map/ppermute | solution.py:127
  15.2 8.8 %copy-start = (bf16[1,384,4096]{2,1,0:T(8,128)(2,1)S(1)}, bf16[1,384,4096]{2,1,0:T(8,128)(2,1)}, u32[]{:S(2)}) copy-start(bf16[1,384,4096]{2,1,0:T(8,128)(2,1)} %param.3) | copy-start | bytes 9437188
  15.2 6.8 %collective-permute-start.6 = (bf16[256,384]{1,0:T(8,128)(2,1)}, bf16[256,384]{1,0:T(8,128)(2,1)S(1)}, u32[]{:S(2)}, u32[]{:S(2)}) collective-permute-start(bf16[256,384]{1,0:T(8,128)(2,1)} %collective-permute-done.2.refs_3_), channel_id=1, source_target_pairs={{0,2},{1,5},{2,0},{3,7},{4,6},{5,1},{6,4},{7,3},{8,10},{9,13},{10,... | collective-permute-start | bytes 589832 | tf_op jit(solution)/shard_map/ppermute | solution.py:127
  16.5 7.4 %collective-permute-start.9 = (bf16[256,384]{1,0:T(8,128)(2,1)}, bf16[256,384]{1,0:T(8,128)(2,1)S(1)}, u32[]{:S(2)}, u32[]{:S(2)}) collective-permute-start(bf16[256,384]{1,0:T(8,128)(2,1)} %collective-permute-done.8.refs_7_), channel_id=1, source_target_pairs={{0,2},{1,5},{2,0},{3,7},{4,6},{5,1},{6,4},{7,3},{8,10},{9,13},{10,... | collective-permute-start | bytes 589832 | tf_op jit(solution)/shard_map/ppermute | solution.py:127
  18.1 10.5 %collective-permute-start.13 = (bf16[512,384]{1,0:T(8,128)(2,1)S(1)}, bf16[512,384]{1,0:T(8,128)(2,1)S(1)}, u32[]{:S(2)}, u32[]{:S(2)}) collective-permute-start(bf16[512,384]{1,0:T(8,128)(2,1)S(1)} %collective-permute-done.11.refs_6_), channel_id=1, source_target_pairs={{0,8},{1,9},{2,10},{3,11},{4,12},{5,13},{6,14},{7,15},{8,0},{9,1},... | collective-permute-start | bytes 1179656 | tf_op jit(solution)/shard_map/ppermute | solution.py:127
  20.0 8.3 %collective-permute-start.4 = (bf16[256,384]{1,0:T(8,128)(2,1)S(1)}, bf16[256,384]{1,0:T(8,128)(2,1)S(1)}, u32[]{:S(2)}, u32[]{:S(2)}) collective-permute-start(bf16[256,384]{1,0:T(8,128)(2,1)S(1)} %collective-permute-done.3.refs_2_), channel_id=1, source_target_pairs={{0,2},{1,5},{2,0},{3,7},{4,6},{5,1},{6,4},{7,3},{8,10},{9,13},{10,... | collective-permute-start | bytes 589832 | tf_op jit(solution)/shard_map/ppermute | solution.py:127
  21.9 6.6 %collective-permute-start.14 = (bf16[256,384]{1,0:T(8,128)(2,1)}, bf16[256,384]{1,0:T(8,128)(2,1)S(1)}, u32[]{:S(2)}, u32[]{:S(2)}) collective-permute-start(bf16[256,384]{1,0:T(8,128)(2,1)} %collective-permute-done.2.refs_3_), channel_id=1, source_target_pairs={{0,4},{1,3},{2,6},{3,1},{4,0},{5,7},{6,2},{7,5},{8,12},{9,11},{10,... | collective-permute-start | bytes 589832 | tf_op jit(solution)/shard_map/ppermute | solution.py:127
  23.2 8.0 %collective-permute-start.7 = (bf16[256,384]{1,0:T(8,128)(2,1)S(1)}, bf16[256,384]{1,0:T(8,128)(2,1)S(1)}, u32[]{:S(2)}, u32[]{:S(2)}) collective-permute-start(bf16[256,384]{1,0:T(8,128)(2,1)S(1)} %collective-permute-done.6.refs_5_), channel_id=1, source_target_pairs={{0,4},{1,3},{2,6},{3,1},{4,0},{5,7},{6,2},{7,5},{8,12},{9,11},{10,... | collective-permute-start | bytes 589832 | tf_op jit(solution)/shard_map/ppermute | solution.py:127
  27.0 6.3 %collective-permute-start.12 = (bf16[256,384]{1,0:T(8,128)(2,1)S(1)}, bf16[256,384]{1,0:T(8,128)(2,1)S(1)}, u32[]{:S(2)}, u32[]{:S(2)}) collective-permute-start(bf16[256,384]{1,0:T(8,128)(2,1)S(1)} %collective-permute-done.3.refs_2_), channel_id=1, source_target_pairs={{0,4},{1,3},{2,6},{3,1},{4,0},{5,7},{6,2},{7,5},{8,12},{9,11},{10,... | collective-permute-start | bytes 589832 | tf_op jit(solution)/shard_map/ppermute | solution.py:127
  28.3 7.1 %collective-permute-start.5 = (bf16[256,384]{1,0:T(8,128)(2,1)S(1)}, bf16[256,384]{1,0:T(8,128)(2,1)S(1)}, u32[]{:S(2)}, u32[]{:S(2)}) collective-permute-start(bf16[256,384]{1,0:T(8,128)(2,1)S(1)} %collective-permute-done.4.refs_2_), channel_id=1, source_target_pairs={{0,4},{1,3},{2,6},{3,1},{4,0},{5,7},{6,2},{7,5},{8,12},{9,11},{10,... | collective-permute-start | bytes 589832 | tf_op jit(solution)/shard_map/ppermute | solution.py:127
  36.0 3.3 %collective-permute-start.15 = (bf16[384,512]{1,0:T(8,128)(2,1)S(1)}, bf16[384,512]{1,0:T(8,128)(2,1)S(1)}, u32[]{:S(2)}, u32[]{:S(2)}) collective-permute-start(bf16[384,512]{1,0:T(8,128)(2,1)S(1)} %get-tuple-element.22), channel_id=1, source_target_pairs={{0,1},{1,0},{2,3},{3,2},{4,5},{5,4},{6,7},{7,6},{8,9},{9,8},{10,11... | collective-permute-start | bytes 1179656 | tf_op jit(solution)/shard_map/ppermute | solution.py:131

commit v5 on v4

--- a/solution.py
+++ b/solution.py
@@ -437,27 +437,27 @@
     sines = jnp.concatenate([-sine, sine], axis=-1)
     other, column, row = stage(swap(mine), doc_ids, swap(doc_ids))
     z1 = flip(own, 4, 4)
-    a0 = flip(own, 1, 2)
     z2 = flip(own, 8, 8)
-    a1 = flip(z1, 1, 2)
     (z2_a2, cosines, sines,) = lax.optimization_barrier(
         (z2, cosines, sines)
     )
     a2 = flip(z2_a2, 1, 2)
+    z3 = flip(z2, 4, 4)
+    a1 = flip(z1, 1, 2)
+    a0 = flip(own, 1, 2)
+    K1 = partial(mine, other, [own, z2, a2, z3, a1, z1, a0], [[(0, 0)], [(8, 8)], [(9, 10)], [(12, 12)], [(5, 6)], [(4, 4)], [(1, 2)]], late=5)
     own_a0 = jnp.concatenate([own, a0])
     B0 = flip(own_a0, 2, 1)
-    K1 = partial(mine, other, [own, z2, a1, a2, B0, z1, a0], [[(0, 0)], [(8, 8)], [(5, 6)], [(9, 10)], [(2, 1), (3, 3)], [(4, 4)], [(1, 2)]], late=5)
-    z3 = flip(z2, 4, 4)
+    b2 = flip(z2, 2, 1)
+    a3 = flip(z3, 1, 2)
+    K2 = partial(mine, other, [B0, b2, a3], [[(2, 1), (3, 3)], [(10, 9)], [(13, 14)]], K1)
     C1 = flip(B0, 4, 4)
-    b2 = flip(z2, 2, 1)
-    K2 = partial(mine, other, [z3, C1, b2], [[(12, 12)], [(6, 5), (7, 7)], [(10, 9)]], K1)
-    a3 = flip(z3, 1, 2)
     c2 = flip(a2, 2, 1)
     (z3_b3, K1,) = lax.optimization_barrier(
         (z3, K1)
     )
     b3 = flip(z3_b3, 2, 1)
-    K3 = partial(mine, other, [a3, c2, b3], [[(13, 14)], [(11, 11)], [(14, 13)]], K2)
+    K3 = partial(mine, other, [C1, c2, b3], [[(6, 5), (7, 7)], [(11, 11)], [(14, 13)]], K2)
     c3 = flip(a3, 2, 1)
     keep, send = partial(
         mine, other, [c3], [[(15, 15)]], K3, (cosines, sines)

time: 41.6 us -> 41.4 us (level)
  no operation moved by 1% of the time
where the time goes in v5:
time: 41.4 us; the launch traced here: 41.2 us
  starting transfers between devices  16.7 us (40%)
  waiting for transfers between devices  12.9 us (31%)
  Pallas kernels  9.52 us (23%)
  other arithmetic  1.91 us (5%)
    ppermute x13, starting transfers between devices, flip(): return lax.ppermute(value, ('fsdp', 'ctx'), pairs)  14.1 us
    ppermute x13, waiting for transfers between devices, flip(): return lax.ppermute(value, ('fsdp', 'ctx'), pairs)  12.3 us
    pallas_call x3, Pallas kernels, partial(): pl.pallas_call(functools.partial(partial_kernel, masks, late, begun), out...  4.85 us
    ppermute x3, starting transfers between devices, swap(): return lax.ppermute(value, 'ctx', [(0, 1), (1, 0)])  2.58 us
    pallas_call x1, Pallas kernels, paired_body(): pl.pallas_call(attention_kernel, out_shape=jax.ShapeDtypeStruct((tokens,...  2.14 us
    neg x1, other arithmetic, paired_body(): sines = jnp.concatenate([-sine, sine], axis=-1)  1.44 us
    pallas_call x1, Pallas kernels, own_columns(): pl.pallas_call(own_kernel, out_shape=jax.ShapeDtypeStruct((weight.shape[0...  0.93 us
  transfers between devices with their start and end apart: 16, of which 10 were waited for; matrix products, arithmetic and copies ran while one was open for 5% of the time, Pallas kernels for 17%

profile of v5, /device:TPU:1, one launch (start us, length us, event | category | flops | bytes accessed | tf_op | source)
XLA Modules:
  0.0 41.2 jit_solution(9868509387905202115)
XLA Ops:
  0.1 0.9 %shard_map.38.refs_2_ = bf16[256,384]{1,0:T(8,128)(2,1)S(1)} custom-call(bf16[256,768]{1,0:T(8,128)(2,1)} %weight_ref.1), custom_call_target="tpu_custom_call" | custom-call | tf_op jit(solution)/shard_map/pallas_call | solution.py:373
  1.0 3.8 %collective-permute-start.2 = (bf16[256,384]{1,0:T(8,128)(2,1)S(1)}, bf16[256,384]{1,0:T(8,128)(2,1)}, u32[]{:S(2)}, u32[]{:S(2)}) collective-permute-start(bf16[256,384]{1,0:T(8,128)(2,1)S(1)} %shard_map.38.refs_2_), channel_id=1, source_target_pairs={{0,16},{1,17},{2,18},{3,19},{4,20},{5,21},{6,22},{7,23},{8,24},{9,... | collective-permute-start | bytes 589832 | tf_op jit(solution)/shard_map/ppermute | solution.py:127
  4.8 1.3 %collective-permute-start.11 = (bf16[256,384]{1,0:T(8,128)(2,1)S(1)}, bf16[256,384]{1,0:T(8,128)(2,1)}, u32[]{:S(2)}, u32[]{:S(2)}) collective-permute-start(bf16[256,384]{1,0:T(8,128)(2,1)S(1)} %shard_map.38.refs_2_), channel_id=1, source_target_pairs={{0,8},{1,9},{2,10},{3,11},{4,12},{5,13},{6,14},{7,15},{8,0},{9,1},... | collective-permute-start | bytes 589832 | tf_op jit(solution)/shard_map/ppermute | solution.py:127
  6.1 1.2 %collective-permute-start.6 = (bf16[256,384]{1,0:T(8,128)(2,1)S(1)}, bf16[256,384]{1,0:T(8,128)(2,1)S(1)}, u32[]{:S(2)}, u32[]{:S(2)}) collective-permute-start(bf16[256,384]{1,0:T(8,128)(2,1)S(1)} %shard_map.38.refs_2_), channel_id=1, source_target_pairs={{0,2},{1,5},{2,0},{3,7},{4,6},{5,1},{6,4},{7,3},{8,10},{9,13},{10,... | collective-permute-start | bytes 589832 | tf_op jit(solution)/shard_map/ppermute | solution.py:127
  7.4 0.8 %collective-permute-start.1 = (s32[1,384]{1,0:T(1,128)}, s32[1,384]{1,0:T(1,128)S(1)}, u32[]{:S(2)}, u32[]{:S(2)}) collective-permute-start(s32[1,384]{1,0:T(1,128)} %docs_ref.1), channel_id=1, source_target_pairs={{0,1},{1,0},{2,3},{3,2},{4,5},{5,4},{6,7},{7,6},{8,9},{9,8},{10,11... | collective-permute-start | bytes 4616 | tf_op jit(solution)/shard_map/ppermute | solution.py:131
  8.3 2.7 %collective-permute-done.6.refs_8_ = bf16[256,384]{1,0:T(8,128)(2,1)S(1)} collective-permute-done((bf16[256,384]{1,0:T(8,128)(2,1)S(1)}, bf16[256,384]{1,0:T(8,128)(2,1)S(1)}, u32[]{:S(2)}, u32[]{:S(2)}) %collective-permute-start.6) | collective-permute-done | bytes 196640 | tf_op jit(solution)/shard_map/ppermute | solution.py:127
  11.1 1.3 %collective-permute-start.7 = (bf16[512,384]{1,0:T(8,128)(2,1)S(1)}, bf16[512,384]{1,0:T(8,128)(2,1)S(1)}, u32[]{:S(2)}, u32[]{:S(2)}) collective-permute-start(bf16[512,384]{1,0:T(8,128)(2,1)S(1)} %pad_maximum_fusion), channel_id=1, source_target_pairs={{0,4},{1,3},{2,6},{3,1},{4,0},{5,7},{6,2},{7,5},{8,12},{9,11},{10,... | collective-permute-start | bytes 1179656 | tf_op jit(solution)/shard_map/ppermute | solution.py:127
  12.4 1.4 %fusion = (f32[2,384,64]{2,1,0:T(8,128)S(1)}, f32[2,384,64]{2,1,0:T(8,128)S(1)}, f32[2,384,64]{2,1,0:T(8,128)S(1)}) fusion(f32[64]{0:T(128)S(1)} %multiply_exponential_fusion, f32[2,384]{1,0:T(2,128)S(1)} %add_convert_fusion), kind=kLoop, calls=%fused_computation.5 | loop fusion | flops 98304 | bytes 593152 | tf_op jit(solution)/shard_map/neg | solution.py:437
  15.2 1.3 %collective-permute-start.9 = (bf16[256,384]{1,0:T(8,128)(2,1)}, bf16[256,384]{1,0:T(8,128)(2,1)S(1)}, u32[]{:S(2)}, u32[]{:S(2)}) collective-permute-start(bf16[256,384]{1,0:T(8,128)(2,1)} %collective-permute-done.2.refs_3_), channel_id=1, source_target_pairs={{0,2},{1,5},{2,0},{3,7},{4,6},{5,1},{6,4},{7,3},{8,10},{9,13},{10,... | collective-permute-start | bytes 589832 | tf_op jit(solution)/shard_map/ppermute | solution.py:127
  16.7 1.3 %collective-permute-done.7.refs_2_ = bf16[512,384]{1,0:T(8,128)(2,1)S(1)} collective-permute-done((bf16[512,384]{1,0:T(8,128)(2,1)S(1)}, bf16[512,384]{1,0:T(8,128)(2,1)S(1)}, u32[]{:S(2)}, u32[]{:S(2)}) %collective-permute-start.7) | collective-permute-done | bytes 393248 | tf_op jit(solution)/shard_map/ppermute | solution.py:127
  18.2 1.8 %collective-permute-done.3.refs_5_ = bf16[256,384]{1,0:T(8,128)(2,1)S(1)} collective-permute-done((bf16[256,384]{1,0:T(8,128)(2,1)}, bf16[256,384]{1,0:T(8,128)(2,1)S(1)}, u32[]{:S(2)}, u32[]{:S(2)}) %collective-permute-start.3) | collective-permute-done | bytes 196640 | tf_op jit(solution)/shard_map/ppermute | solution.py:127
  20.0 1.3 %collective-permute-start.4 = (bf16[256,384]{1,0:T(8,128)(2,1)S(1)}, bf16[256,384]{1,0:T(8,128)(2,1)S(1)}, u32[]{:S(2)}, u32[]{:S(2)}) collective-permute-start(bf16[256,384]{1,0:T(8,128)(2,1)S(1)} %collective-permute-done.3.refs_5_), channel_id=1, source_target_pairs={{0,2},{1,5},{2,0},{3,7},{4,6},{5,1},{6,4},{7,3},{8,10},{9,13},{10,... | collective-permute-start | bytes 589832 | tf_op jit(solution)/shard_map/ppermute | solution.py:127
  21.9 1.2 %collective-permute-start.14 = (bf16[256,384]{1,0:T(8,128)(2,1)}, bf16[256,384]{1,0:T(8,128)(2,1)S(1)}, u32[]{:S(2)}, u32[]{:S(2)}) collective-permute-start(bf16[256,384]{1,0:T(8,128)(2,1)} %collective-permute-done.2.refs_3_), channel_id=1, source_target_pairs={{0,4},{1,3},{2,6},{3,1},{4,0},{5,7},{6,2},{7,5},{8,12},{9,11},{10,... | collective-permute-start | bytes 589832 | tf_op jit(solution)/shard_map/ppermute | solution.py:127
  23.9 2.9 %shard_map.39.refs_5_ = f32[2,384,384]{2,1,0:T(8,128)S(1)} custom-call(bf16[384,4096]{1,0:T(8,128)(2,1)S(1)} %bitcast.5, bf16[384,4096]{1,0:T(8,128)(2,1)S(1)} %get-tuple-element.16.refs_1_, bf16[256,384]{1,0:T(8,128)(2,1)S(1)} %shard_map.38.refs_2_, bf16[256,384]{1,0:T(8,128)(2,1)} %collective-permute-done.2.refs_3_, ...), custom_call_target="tpu_custom_call" | custom-call | flops 1056964608 | bytes 6488064 | tf_op jit(solution)/shard_map/pallas_call | solution.py:402
  26.8 1.3 %collective-permute-start.13 = (bf16[256,384]{1,0:T(8,128)(2,1)S(1)}, bf16[256,384]{1,0:T(8,128)(2,1)S(1)}, u32[]{:S(2)}, u32[]{:S(2)}) collective-permute-start(bf16[256,384]{1,0:T(8,128)(2,1)S(1)} %collective-permute-done.3.refs_5_), channel_id=1, source_target_pairs={{0,4},{1,3},{2,6},{3,1},{4,0},{5,7},{6,2},{7,5},{8,12},{9,11},{10,... | collective-permute-start | bytes 589832 | tf_op jit(solution)/shard_map/ppermute | solution.py:127
  28.3 1.0 %shard_map.40.refs_5_ = f32[2,384,384]{2,1,0:T(8,128)S(1)} custom-call(bf16[384,4096]{1,0:T(8,128)(2,1)S(1)} %bitcast.6, bf16[384,4096]{1,0:T(8,128)(2,1)S(1)} %get-tuple-element.16.refs_1_, bf16[512,384]{1,0:T(8,128)(2,1)S(1)} %collective-permute-done.7.refs_2_, bf16[256,384]{1,0:T(8,128)(2,1)S(1)} %collective-permute-done.14.refs_3_, ...), custom_call_target="tpu_custom_call" | custom-call | flops 603979776 | bytes 4718592 | tf_op jit(solution)/shard_map/pallas_call | solution.py:402
  29.3 1.9 %collective-permute-done.10.refs_3_ = bf16[256,384]{1,0:T(8,128)(2,1)S(1)} collective-permute-done((bf16[256,384]{1,0:T(8,128)(2,1)S(1)}, bf16[256,384]{1,0:T(8,128)(2,1)S(1)}, u32[]{:S(2)}, u32[]{:S(2)}) %collective-permute-start.10) | collective-permute-done | bytes 196640 | tf_op jit(solution)/shard_map/ppermute | solution.py:127
  31.2 2.1 %collective-permute-done.13.refs_4_ = bf16[256,384]{1,0:T(8,128)(2,1)S(1)} collective-permute-done((bf16[256,384]{1,0:T(8,128)(2,1)S(1)}, bf16[256,384]{1,0:T(8,128)(2,1)S(1)}, u32[]{:S(2)}, u32[]{:S(2)}) %collective-permute-start.13) | collective-permute-done | bytes 196640 | tf_op jit(solution)/shard_map/ppermute | solution.py:127
  33.3 1.0 %shard_map.41.refs_3_ = f32[2,384,384]{2,1,0:T(8,128)S(1)} custom-call(bf16[384,4096]{1,0:T(8,128)(2,1)S(1)} %bitcast.7, bf16[384,4096]{1,0:T(8,128)(2,1)S(1)} %get-tuple-element.16.refs_1_, bf16[512,384]{1,0:T(8,128)(2,1)S(1)} %collective-permute-done.8.refs_2_, bf16[256,384]{1,0:T(8,128)(2,1)S(1)} %collective-permute-done.10.refs_3_, ...), custom_call_target="tpu_custom_call" | custom-call | flops 603979776 | bytes 4718592 | tf_op jit(solution)/shard_map/pallas_call | solution.py:402
  34.3 1.1 %collective-permute-done.5.refs_2_ = bf16[256,384]{1,0:T(8,128)(2,1)S(1)} collective-permute-done((bf16[256,384]{1,0:T(8,128)(2,1)S(1)}, bf16[256,384]{1,0:T(8,128)(2,1)S(1)}, u32[]{:S(2)}, u32[]{:S(2)}) %collective-permute-start.5) | collective-permute-done | bytes 196640 | tf_op jit(solution)/shard_map/ppermute | solution.py:127
  36.0 1.7 %collective-permute-start.15 = (bf16[384,512]{1,0:T(8,128)(2,1)S(1)}, bf16[384,512]{1,0:T(8,128)(2,1)S(1)}, u32[]{:S(2)}, u32[]{:S(2)}) collective-permute-start(bf16[384,512]{1,0:T(8,128)(2,1)S(1)} %get-tuple-element.22), channel_id=1, source_target_pairs={{0,1},{1,0},{2,3},{3,2},{4,5},{5,4},{6,7},{7,6},{8,9},{9,8},{10,11... | collective-permute-start | bytes 1179656 | tf_op jit(solution)/shard_map/ppermute | solution.py:131
  37.7 0.7 %shard_map.43 = (bf16[3,256,768]{2,1,0:T(8,128)(2,1)S(1)}, bf16[128,768]{1,0:T(8,128)(2,1)S(1)}) custom-call(bf16[384,512]{1,0:T(8,128)(2,1)S(1)} %get-tuple-element.21.keep_ref, f32[384,1]{1,0:T(8,128)S(1)} %get-tuple-element.23.column_ref, f32[1,768]{1,0:T(1,128)S(1)} %get-tuple-element.24.row_ref), custom_call_target="tpu_custom_call" | custom-call | flops 75497472 | bytes 589824 | tf_op jit(solution)/shard_map/pallas_call | solution.py:468
  38.4 0.7 %collective-permute-done.15.recv_ref = bf16[384,512]{1,0:T(8,128)(2,1)S(1)} collective-permute-done((bf16[384,512]{1,0:T(8,128)(2,1)S(1)}, bf16[384,512]{1,0:T(8,128)(2,1)S(1)}, u32[]{:S(2)}, u32[]{:S(2)}) %collective-permute-start.15) | collective-permute-done | bytes 393248 | tf_op jit(solution)/shard_map/ppermute | solution.py:131
  39.0 2.1 %shard_map.44 = bf16[384,512]{1,0:T(8,128)(2,1)} custom-call(bf16[384,512]{1,0:T(8,128)(2,1)S(1)} %get-tuple-element.21.keep_ref, bf16[384,512]{1,0:T(8,128)(2,1)S(1)} %collective-permute-done.15.recv_ref, bf16[3,256,768]{2,1,0:T(8,128)(2,1)S(1)} %get-tuple-element.25.probs_ref, bf16[128,768]{1,0:T(8,128)(2,1)S(1)} %get-tuple-element.26.keys_ref, ...), custom_call_target="tpu_custom_call" | custom-call | flops 603979776 | bytes 1572864 | tf_op jit(solution)/shard_map/pallas_call | solution.py:483
  (26 shorter events, 4.2 us)
Async XLA Ops:
  0.0 23.2 %collective-permute-start = (bf16[384,4096]{1,0:T(8,128)(2,1)}, bf16[384,4096]{1,0:T(8,128)(2,1)S(1)}, u32[]{:S(2)}, u32[]{:S(2)}) collective-permute-start(bf16[384,4096]{1,0:T(8,128)(2,1)} %bitcast.4), channel_id=1, source_target_pairs={{0,1},{1,0},{2,3},{3,2},{4,5},{5,4},{6,7},{7,6},{8,9},{9,8},{10,11... | collective-permute-start | bytes 9437192 | tf_op jit(solution)/shard_map/ppermute | solution.py:131
  1.0 13.5 %collective-permute-start.2 = (bf16[256,384]{1,0:T(8,128)(2,1)S(1)}, bf16[256,384]{1,0:T(8,128)(2,1)}, u32[]{:S(2)}, u32[]{:S(2)}) collective-permute-start(bf16[256,384]{1,0:T(8,128)(2,1)S(1)} %shard_map.38.refs_2_), channel_id=1, source_target_pairs={{0,16},{1,17},{2,18},{3,19},{4,20},{5,21},{6,22},{7,23},{8,24},{9,... | collective-permute-start | bytes 589832 | tf_op jit(solution)/shard_map/ppermute | solution.py:127
  4.8 11.7 %collective-permute-start.11 = (bf16[256,384]{1,0:T(8,128)(2,1)S(1)}, bf16[256,384]{1,0:T(8,128)(2,1)}, u32[]{:S(2)}, u32[]{:S(2)}) collective-permute-start(bf16[256,384]{1,0:T(8,128)(2,1)S(1)} %shard_map.38.refs_2_), channel_id=1, source_target_pairs={{0,8},{1,9},{2,10},{3,11},{4,12},{5,13},{6,14},{7,15},{8,0},{9,1},... | collective-permute-start | bytes 589832 | tf_op jit(solution)/shard_map/ppermute | solution.py:127
  6.1 4.9 %collective-permute-start.6 = (bf16[256,384]{1,0:T(8,128)(2,1)S(1)}, bf16[256,384]{1,0:T(8,128)(2,1)S(1)}, u32[]{:S(2)}, u32[]{:S(2)}) collective-permute-start(bf16[256,384]{1,0:T(8,128)(2,1)S(1)} %shard_map.38.refs_2_), channel_id=1, source_target_pairs={{0,2},{1,5},{2,0},{3,7},{4,6},{5,1},{6,4},{7,3},{8,10},{9,13},{10,... | collective-permute-start | bytes 589832 | tf_op jit(solution)/shard_map/ppermute | solution.py:127
  7.4 7.8 %collective-permute-start.1 = (s32[1,384]{1,0:T(1,128)}, s32[1,384]{1,0:T(1,128)S(1)}, u32[]{:S(2)}, u32[]{:S(2)}) collective-permute-start(s32[1,384]{1,0:T(1,128)} %docs_ref.1), channel_id=1, source_target_pairs={{0,1},{1,0},{2,3},{3,2},{4,5},{5,4},{6,7},{7,6},{8,9},{9,8},{10,11... | collective-permute-start | bytes 4616 | tf_op jit(solution)/shard_map/ppermute | solution.py:131
  11.1 7.0 %collective-permute-start.7 = (bf16[512,384]{1,0:T(8,128)(2,1)S(1)}, bf16[512,384]{1,0:T(8,128)(2,1)S(1)}, u32[]{:S(2)}, u32[]{:S(2)}) collective-permute-start(bf16[512,384]{1,0:T(8,128)(2,1)S(1)} %pad_maximum_fusion), channel_id=1, source_target_pairs={{0,4},{1,3},{2,6},{3,1},{4,0},{5,7},{6,2},{7,5},{8,12},{9,11},{10,... | collective-permute-start | bytes 1179656 | tf_op jit(solution)/shard_map/ppermute | solution.py:127
  13.8 9.6 %copy-start.1 = (s32[1,384]{1,0:T(1,128)S(1)}, s32[1,384]{1,0:T(1,128)}, u32[]{:S(2)}) copy-start(s32[1,384]{1,0:T(1,128)} %docs_ref.1) | copy-start | bytes 4612
  14.5 5.5 %collective-permute-start.3 = (bf16[256,384]{1,0:T(8,128)(2,1)}, bf16[256,384]{1,0:T(8,128)(2,1)S(1)}, u32[]{:S(2)}, u32[]{:S(2)}) collective-permute-start(bf16[256,384]{1,0:T(8,128)(2,1)} %collective-permute-done.2.refs_3_), channel_id=1, source_target_pairs={{0,8},{1,9},{2,10},{3,11},{4,12},{5,13},{6,14},{7,15},{8,0},{9,1},... | collective-permute-start | bytes 589832 | tf_op jit(solution)/shard_map/ppermute | solution.py:127
  15.2 8.8 %copy-start = (bf16[1,384,4096]{2,1,0:T(8,128)(2,1)S(1)}, bf16[1,384,4096]{2,1,0:T(8,128)(2,1)}, u32[]{:S(2)}) copy-start(bf16[1,384,4096]{2,1,0:T(8,128)(2,1)} %param.3) | copy-start | bytes 9437188
  15.2 6.8 %collective-permute-start.9 = (bf16[256,384]{1,0:T(8,128)(2,1)}, bf16[256,384]{1,0:T(8,128)(2,1)S(1)}, u32[]{:S(2)}, u32[]{:S(2)}) collective-permute-start(bf16[256,384]{1,0:T(8,128)(2,1)} %collective-permute-done.2.refs_3_), channel_id=1, source_target_pairs={{0,2},{1,5},{2,0},{3,7},{4,6},{5,1},{6,4},{7,3},{8,10},{9,13},{10,... | collective-permute-start | bytes 589832 | tf_op jit(solution)/shard_map/ppermute | solution.py:127
  16.5 7.4 %collective-permute-start.12 = (bf16[256,384]{1,0:T(8,128)(2,1)}, bf16[256,384]{1,0:T(8,128)(2,1)S(1)}, u32[]{:S(2)}, u32[]{:S(2)}) collective-permute-start(bf16[256,384]{1,0:T(8,128)(2,1)} %collective-permute-done.11.refs_7_), channel_id=1, source_target_pairs={{0,2},{1,5},{2,0},{3,7},{4,6},{5,1},{6,4},{7,3},{8,10},{9,13},{10,... | collective-permute-start | bytes 589832 | tf_op jit(solution)/shard_map/ppermute | solution.py:127
  18.1 13.1 %collective-permute-start.8 = (bf16[512,384]{1,0:T(8,128)(2,1)S(1)}, bf16[512,384]{1,0:T(8,128)(2,1)S(1)}, u32[]{:S(2)}, u32[]{:S(2)}) collective-permute-start(bf16[512,384]{1,0:T(8,128)(2,1)S(1)} %collective-permute-done.7.refs_2_), channel_id=1, source_target_pairs={{0,8},{1,9},{2,10},{3,11},{4,12},{5,13},{6,14},{7,15},{8,0},{9,1},... | collective-permute-start | bytes 1179656 | tf_op jit(solution)/shard_map/ppermute | solution.py:127
  20.0 8.1 %collective-permute-start.4 = (bf16[256,384]{1,0:T(8,128)(2,1)S(1)}, bf16[256,384]{1,0:T(8,128)(2,1)S(1)}, u32[]{:S(2)}, u32[]{:S(2)}) collective-permute-start(bf16[256,384]{1,0:T(8,128)(2,1)S(1)} %collective-permute-done.3.refs_5_), channel_id=1, source_target_pairs={{0,2},{1,5},{2,0},{3,7},{4,6},{5,1},{6,4},{7,3},{8,10},{9,13},{10,... | collective-permute-start | bytes 589832 | tf_op jit(solution)/shard_map/ppermute | solution.py:127
  21.9 6.4 %collective-permute-start.14 = (bf16[256,384]{1,0:T(8,128)(2,1)}, bf16[256,384]{1,0:T(8,128)(2,1)S(1)}, u32[]{:S(2)}, u32[]{:S(2)}) collective-permute-start(bf16[256,384]{1,0:T(8,128)(2,1)} %collective-permute-done.2.refs_3_), channel_id=1, source_target_pairs={{0,4},{1,3},{2,6},{3,1},{4,0},{5,7},{6,2},{7,5},{8,12},{9,11},{10,... | collective-permute-start | bytes 589832 | tf_op jit(solution)/shard_map/ppermute | solution.py:127
  23.2 8.0 %collective-permute-start.10 = (bf16[256,384]{1,0:T(8,128)(2,1)S(1)}, bf16[256,384]{1,0:T(8,128)(2,1)S(1)}, u32[]{:S(2)}, u32[]{:S(2)}) collective-permute-start(bf16[256,384]{1,0:T(8,128)(2,1)S(1)} %collective-permute-done.9.refs_4_), channel_id=1, source_target_pairs={{0,4},{1,3},{2,6},{3,1},{4,0},{5,7},{6,2},{7,5},{8,12},{9,11},{10,... | collective-permute-start | bytes 589832 | tf_op jit(solution)/shard_map/ppermute | solution.py:127
  26.8 6.5 %collective-permute-start.13 = (bf16[256,384]{1,0:T(8,128)(2,1)S(1)}, bf16[256,384]{1,0:T(8,128)(2,1)S(1)}, u32[]{:S(2)}, u32[]{:S(2)}) collective-permute-start(bf16[256,384]{1,0:T(8,128)(2,1)S(1)} %collective-permute-done.3.refs_5_), channel_id=1, source_target_pairs={{0,4},{1,3},{2,6},{3,1},{4,0},{5,7},{6,2},{7,5},{8,12},{9,11},{10,... | collective-permute-start | bytes 589832 | tf_op jit(solution)/shard_map/ppermute | solution.py:127
  28.1 7.3 %collective-permute-start.5 = (bf16[256,384]{1,0:T(8,128)(2,1)S(1)}, bf16[256,384]{1,0:T(8,128)(2,1)S(1)}, u32[]{:S(2)}, u32[]{:S(2)}) collective-permute-start(bf16[256,384]{1,0:T(8,128)(2,1)S(1)} %collective-permute-done.4.refs_4_), channel_id=1, source_target_pairs={{0,4},{1,3},{2,6},{3,1},{4,0},{5,7},{6,2},{7,5},{8,12},{9,11},{10,... | collective-permute-start | bytes 589832 | tf_op jit(solution)/shard_map/ppermute | solution.py:127
  36.0 3.1 %collective-permute-start.15 = (bf16[384,512]{1,0:T(8,128)(2,1)S(1)}, bf16[384,512]{1,0:T(8,128)(2,1)S(1)}, u32[]{:S(2)}, u32[]{:S(2)}) collective-permute-start(bf16[384,512]{1,0:T(8,128)(2,1)S(1)} %get-tuple-element.22), channel_id=1, source_target_pairs={{0,1},{1,0},{2,3},{3,2},{4,5},{5,4},{6,7},{7,6},{8,9},{9,8},{10,11... | collective-permute-start | bytes 1179656 | tf_op jit(solution)/shard_map/ppermute | solution.py:131

commit v6 on v5

--- a/solution.py
+++ b/solution.py
@@ -300,8 +300,13 @@
                 keys[:, :width],
                 visible_keys(column_ref, row_ref, place, 0, width),
             )
-            probs = jnp.concatenate([probs, probs_ref[step, :, :width]], axis=0)
-            context = jnp.dot(probs, values[:width], preferred_element_type=jnp.float32)
+            context = jnp.concatenate(
+                [
+                    jnp.dot(part, values[:width], preferred_element_type=jnp.float32)
+                    for part in (probs, probs_ref[step, :, :width])
+                ],
+                axis=0,
+            )
             write(step, (context[:, :HD] / context[:, HD:]).astype(jnp.bfloat16), (0, 1, 2, 3))
 
     for step in range(rows // STEP):
@@ -435,7 +440,7 @@
     cosine, sine = jnp.cos(angles), jnp.sin(angles)
     cosines = jnp.concatenate([cosine, cosine], axis=-1)
     sines = jnp.concatenate([-sine, sine], axis=-1)
-    other, column, row = stage(swap(mine), doc_ids, swap(doc_ids))
+    other, column, row = stage(swap(after(mine, own)), doc_ids, swap(after(doc_ids, own)))
     z1 = flip(own, 4, 4)
     z2 = flip(own, 8, 8)
     (z2_a2, cosines, sines,) = lax.optimization_barrier(
@@ -448,16 +453,16 @@
     K1 = partial(mine, other, [own, z2, a2, z3, a1, z1, a0], [[(0, 0)], [(8, 8)], [(9, 10)], [(12, 12)], [(5, 6)], [(4, 4)], [(1, 2)]], late=5)
     own_a0 = jnp.concatenate([own, a0])
     B0 = flip(own_a0, 2, 1)
+    C1 = flip(B0, 4, 4)
+    a3 = flip(z3, 1, 2)
+    K2 = partial(mine, other, [B0, C1, a3], [[(2, 1), (3, 3)], [(6, 5), (7, 7)], [(13, 14)]], K1)
     b2 = flip(z2, 2, 1)
-    a3 = flip(z3, 1, 2)
-    K2 = partial(mine, other, [B0, b2, a3], [[(2, 1), (3, 3)], [(10, 9)], [(13, 14)]], K1)
-    C1 = flip(B0, 4, 4)
     c2 = flip(a2, 2, 1)
     (z3_b3, K1,) = lax.optimization_barrier(
         (z3, K1)
     )
     b3 = flip(z3_b3, 2, 1)
-    K3 = partial(mine, other, [C1, c2, b3], [[(6, 5), (7, 7)], [(11, 11)], [(14, 13)]], K2)
+    K3 = partial(mine, other, [b2, c2, b3], [[(10, 9)], [(11, 11)], [(14, 13)]], K2)
     c3 = flip(a3, 2, 1)
     keep, send = partial(
         mine, other, [c3], [[(15, 15)]], K3, (cosines, sines)

time: 41.4 us -> 41.4 us (level)
  transfers between devices with their start and end apart: 16 -> 16, of which waited for: 10 -> 10; matrix products, arithmetic and copies ran while one was open for 5% -> 5% of each run, Pallas kernels for 17% -> 14%
where the time goes in v6:
time: 41.4 us; the launch traced here: 41.2 us
  starting transfers between devices  16.8 us (41%)
  waiting for transfers between devices  12.7 us (31%)
  Pallas kernels  9.64 us (23%)
  other arithmetic  1.91 us (5%)
    ppermute x13, starting transfers between devices, flip(): return lax.ppermute(value, ('fsdp', 'ctx'), pairs)  14.3 us
    ppermute x13, waiting for transfers between devices, flip(): return lax.ppermute(value, ('fsdp', 'ctx'), pairs)  12.1 us
    pallas_call x3, Pallas kernels, partial(): pl.pallas_call(functools.partial(partial_kernel, masks, late, begun), out...  4.85 us
    ppermute x3, starting transfers between devices, swap(): return lax.ppermute(value, 'ctx', [(0, 1), (1, 0)])  2.51 us
    pallas_call x1, Pallas kernels, paired_body(): pl.pallas_call(attention_kernel, out_shape=jax.ShapeDtypeStruct((tokens,...  2.26 us
    neg x1, other arithmetic, paired_body(): sines = jnp.concatenate([-sine, sine], axis=-1)  1.44 us
    pallas_call x1, Pallas kernels, own_columns(): pl.pallas_call(own_kernel, out_shape=jax.ShapeDtypeStruct((weight.shape[0...  0.93 us
  transfers between devices with their start and end apart: 16, of which 10 were waited for; matrix products, arithmetic and copies ran while one was open for 5% of the time, Pallas kernels for 14%

profile of v6, /device:TPU:1, one launch (start us, length us, event | category | flops | bytes accessed | tf_op | source)
XLA Modules:
  0.0 41.2 jit_solution(18218543930063467949)
XLA Ops:
  0.0 0.9 %shard_map.37.refs_2_ = bf16[256,384]{1,0:T(8,128)(2,1)S(1)} custom-call(bf16[256,768]{1,0:T(8,128)(2,1)} %weight_ref.1), custom_call_target="tpu_custom_call" | custom-call | tf_op jit(solution)/shard_map/pallas_call | solution.py:378
  1.1 3.8 %collective-permute-start.2 = (bf16[256,384]{1,0:T(8,128)(2,1)S(1)}, bf16[256,384]{1,0:T(8,128)(2,1)}, u32[]{:S(2)}, u32[]{:S(2)}) collective-permute-start(bf16[256,384]{1,0:T(8,128)(2,1)S(1)} %shard_map.37.refs_2_), channel_id=1, source_target_pairs={{0,16},{1,17},{2,18},{3,19},{4,20},{5,21},{6,22},{7,23},{8,24},{9,... | collective-permute-start | bytes 589832 | tf_op jit(solution)/shard_map/ppermute | solution.py:127
  4.8 1.3 %collective-permute-start.9 = (bf16[256,384]{1,0:T(8,128)(2,1)S(1)}, bf16[256,384]{1,0:T(8,128)(2,1)}, u32[]{:S(2)}, u32[]{:S(2)}) collective-permute-start(bf16[256,384]{1,0:T(8,128)(2,1)S(1)} %shard_map.37.refs_2_), channel_id=1, source_target_pairs={{0,8},{1,9},{2,10},{3,11},{4,12},{5,13},{6,14},{7,15},{8,0},{9,1},... | collective-permute-start | bytes 589832 | tf_op jit(solution)/shard_map/ppermute | solution.py:127
  6.1 1.2 %collective-permute-start.11 = (bf16[256,384]{1,0:T(8,128)(2,1)S(1)}, bf16[256,384]{1,0:T(8,128)(2,1)S(1)}, u32[]{:S(2)}, u32[]{:S(2)}) collective-permute-start(bf16[256,384]{1,0:T(8,128)(2,1)S(1)} %shard_map.37.refs_2_), channel_id=1, source_target_pairs={{0,2},{1,5},{2,0},{3,7},{4,6},{5,1},{6,4},{7,3},{8,10},{9,13},{10,... | collective-permute-start | bytes 589832 | tf_op jit(solution)/shard_map/ppermute | solution.py:127
  7.4 0.9 %collective-permute-start.1 = (s32[1,384]{1,0:T(1,128)}, s32[1,384]{1,0:T(1,128)S(1)}, u32[]{:S(2)}, u32[]{:S(2)}) collective-permute-start(s32[1,384]{1,0:T(1,128)} %docs_ref.1), channel_id=1, source_target_pairs={{0,1},{1,0},{2,3},{3,2},{4,5},{5,4},{6,7},{7,6},{8,9},{9,8},{10,11... | collective-permute-start | bytes 4616 | tf_op jit(solution)/shard_map/ppermute | solution.py:131
  8.4 2.6 %collective-permute-done.11.refs_8_ = bf16[256,384]{1,0:T(8,128)(2,1)S(1)} collective-permute-done((bf16[256,384]{1,0:T(8,128)(2,1)S(1)}, bf16[256,384]{1,0:T(8,128)(2,1)S(1)}, u32[]{:S(2)}, u32[]{:S(2)}) %collective-permute-start.11) | collective-permute-done | bytes 196640 | tf_op jit(solution)/shard_map/ppermute | solution.py:127
  11.1 1.3 %collective-permute-start.13 = (bf16[512,384]{1,0:T(8,128)(2,1)S(1)}, bf16[512,384]{1,0:T(8,128)(2,1)S(1)}, u32[]{:S(2)}, u32[]{:S(2)}) collective-permute-start(bf16[512,384]{1,0:T(8,128)(2,1)S(1)} %pad_maximum_fusion.2), channel_id=1, source_target_pairs={{0,4},{1,3},{2,6},{3,1},{4,0},{5,7},{6,2},{7,5},{8,12},{9,11},{10,... | collective-permute-start | bytes 1179656 | tf_op jit(solution)/shard_map/ppermute | solution.py:127
  12.4 1.4 %fusion = (f32[2,384,64]{2,1,0:T(8,128)S(1)}, f32[2,384,64]{2,1,0:T(8,128)S(1)}, f32[2,384,64]{2,1,0:T(8,128)S(1)}) fusion(f32[64]{0:T(128)S(1)} %multiply_exponential_fusion, f32[2,384]{1,0:T(2,128)S(1)} %add_convert_fusion), kind=kLoop, calls=%fused_computation.5 | loop fusion | flops 98304 | bytes 593152 | tf_op jit(solution)/shard_map/neg | solution.py:442
  15.2 1.3 %collective-permute-start.7 = (bf16[256,384]{1,0:T(8,128)(2,1)}, bf16[256,384]{1,0:T(8,128)(2,1)S(1)}, u32[]{:S(2)}, u32[]{:S(2)}) collective-permute-start(bf16[256,384]{1,0:T(8,128)(2,1)} %collective-permute-done.2.refs_3_), channel_id=1, source_target_pairs={{0,2},{1,5},{2,0},{3,7},{4,6},{5,1},{6,4},{7,3},{8,10},{9,13},{10,... | collective-permute-start | bytes 589832 | tf_op jit(solution)/shard_map/ppermute | solution.py:127
  16.7 1.3 %collective-permute-done.13.refs_2_ = bf16[512,384]{1,0:T(8,128)(2,1)S(1)} collective-permute-done((bf16[512,384]{1,0:T(8,128)(2,1)S(1)}, bf16[512,384]{1,0:T(8,128)(2,1)S(1)}, u32[]{:S(2)}, u32[]{:S(2)}) %collective-permute-start.13) | collective-permute-done | bytes 393248 | tf_op jit(solution)/shard_map/ppermute | solution.py:127
  18.2 1.5 %collective-permute-done.3.refs_5_ = bf16[256,384]{1,0:T(8,128)(2,1)S(1)} collective-permute-done((bf16[256,384]{1,0:T(8,128)(2,1)}, bf16[256,384]{1,0:T(8,128)(2,1)S(1)}, u32[]{:S(2)}, u32[]{:S(2)}) %collective-permute-start.3) | collective-permute-done | bytes 196640 | tf_op jit(solution)/shard_map/ppermute | solution.py:127
  19.8 1.4 %collective-permute-start.4 = (bf16[256,384]{1,0:T(8,128)(2,1)S(1)}, bf16[256,384]{1,0:T(8,128)(2,1)S(1)}, u32[]{:S(2)}, u32[]{:S(2)}) collective-permute-start(bf16[256,384]{1,0:T(8,128)(2,1)S(1)} %collective-permute-done.3.refs_5_), channel_id=1, source_target_pairs={{0,2},{1,5},{2,0},{3,7},{4,6},{5,1},{6,4},{7,3},{8,10},{9,13},{10,... | collective-permute-start | bytes 589832 | tf_op jit(solution)/shard_map/ppermute | solution.py:127
  21.2 0.8 %collective-permute-done.7.refs_4_ = bf16[256,384]{1,0:T(8,128)(2,1)S(1)} collective-permute-done((bf16[256,384]{1,0:T(8,128)(2,1)}, bf16[256,384]{1,0:T(8,128)(2,1)S(1)}, u32[]{:S(2)}, u32[]{:S(2)}) %collective-permute-start.7) | collective-permute-done | bytes 196640 | tf_op jit(solution)/shard_map/ppermute | solution.py:127
  22.0 1.2 %collective-permute-start.6 = (bf16[256,384]{1,0:T(8,128)(2,1)}, bf16[256,384]{1,0:T(8,128)(2,1)S(1)}, u32[]{:S(2)}, u32[]{:S(2)}) collective-permute-start(bf16[256,384]{1,0:T(8,128)(2,1)} %collective-permute-done.2.refs_3_), channel_id=1, source_target_pairs={{0,4},{1,3},{2,6},{3,1},{4,0},{5,7},{6,2},{7,5},{8,12},{9,11},{10,... | collective-permute-start | bytes 589832 | tf_op jit(solution)/shard_map/ppermute | solution.py:127
  24.0 2.9 %shard_map.39.refs_5_ = f32[2,384,384]{2,1,0:T(8,128)S(1)} custom-call(bf16[384,4096]{1,0:T(8,128)(2,1)S(1)} %bitcast.5, bf16[384,4096]{1,0:T(8,128)(2,1)S(1)} %get-tuple-element.20.refs_1_, bf16[256,384]{1,0:T(8,128)(2,1)S(1)} %shard_map.37.refs_2_, bf16[256,384]{1,0:T(8,128)(2,1)} %collective-permute-done.2.refs_3_, ...), custom_call_target="tpu_custom_call" | custom-call | flops 1056964608 | bytes 6488064 | tf_op jit(solution)/shard_map/pallas_call | solution.py:407
  26.9 1.3 %collective-permute-start.12 = (bf16[256,384]{1,0:T(8,128)(2,1)S(1)}, bf16[256,384]{1,0:T(8,128)(2,1)S(1)}, u32[]{:S(2)}, u32[]{:S(2)}) collective-permute-start(bf16[256,384]{1,0:T(8,128)(2,1)S(1)} %collective-permute-done.3.refs_5_), channel_id=1, source_target_pairs={{0,4},{1,3},{2,6},{3,1},{4,0},{5,7},{6,2},{7,5},{8,12},{9,11},{10,... | collective-permute-start | bytes 589832 | tf_op jit(solution)/shard_map/ppermute | solution.py:127
  28.4 1.2 %shard_map.40.refs_5_ = f32[2,384,384]{2,1,0:T(8,128)S(1)} custom-call(bf16[384,4096]{1,0:T(8,128)(2,1)S(1)} %bitcast.6, bf16[384,4096]{1,0:T(8,128)(2,1)S(1)} %get-tuple-element.20.refs_1_, bf16[512,384]{1,0:T(8,128)(2,1)S(1)} %collective-permute-done.13.refs_2_, bf16[512,384]{1,0:T(8,128)(2,1)S(1)} %collective-permute-done.14.refs_3_, ...), custom_call_target="tpu_custom_call" | custom-call | flops 754974720 | bytes 5308416 | tf_op jit(solution)/shard_map/pallas_call | solution.py:407
  29.6 1.6 %collective-permute-done.8.refs_3_ = bf16[256,384]{1,0:T(8,128)(2,1)S(1)} collective-permute-done((bf16[256,384]{1,0:T(8,128)(2,1)S(1)}, bf16[256,384]{1,0:T(8,128)(2,1)S(1)}, u32[]{:S(2)}, u32[]{:S(2)}) %collective-permute-start.8) | collective-permute-done | bytes 196640 | tf_op jit(solution)/shard_map/ppermute | solution.py:127
  31.3 2.1 %collective-permute-done.12.refs_4_ = bf16[256,384]{1,0:T(8,128)(2,1)S(1)} collective-permute-done((bf16[256,384]{1,0:T(8,128)(2,1)S(1)}, bf16[256,384]{1,0:T(8,128)(2,1)S(1)}, u32[]{:S(2)}, u32[]{:S(2)}) %collective-permute-start.12) | collective-permute-done | bytes 196640 | tf_op jit(solution)/shard_map/ppermute | solution.py:127
  33.4 0.8 %shard_map.41.refs_3_ = f32[2,384,384]{2,1,0:T(8,128)S(1)} custom-call(bf16[384,4096]{1,0:T(8,128)(2,1)S(1)} %bitcast.7, bf16[384,4096]{1,0:T(8,128)(2,1)S(1)} %get-tuple-element.20.refs_1_, bf16[256,384]{1,0:T(8,128)(2,1)S(1)} %collective-permute-done.6.refs_2_, bf16[256,384]{1,0:T(8,128)(2,1)S(1)} %collective-permute-done.8.refs_3_, ...), custom_call_target="tpu_custom_call" | custom-call | flops 452984832 | bytes 4128768 | tf_op jit(solution)/shard_map/pallas_call | solution.py:407
  34.2 1.3 %collective-permute-done.5.refs_2_ = bf16[256,384]{1,0:T(8,128)(2,1)S(1)} collective-permute-done((bf16[256,384]{1,0:T(8,128)(2,1)S(1)}, bf16[256,384]{1,0:T(8,128)(2,1)S(1)}, u32[]{:S(2)}, u32[]{:S(2)}) %collective-permute-start.5) | collective-permute-done | bytes 196640 | tf_op jit(solution)/shard_map/ppermute | solution.py:127
  36.0 1.5 %collective-permute-start.15 = (bf16[384,512]{1,0:T(8,128)(2,1)S(1)}, bf16[384,512]{1,0:T(8,128)(2,1)S(1)}, u32[]{:S(2)}, u32[]{:S(2)}) collective-permute-start(bf16[384,512]{1,0:T(8,128)(2,1)S(1)} %get-tuple-element.26), channel_id=1, source_target_pairs={{0,1},{1,0},{2,3},{3,2},{4,5},{5,4},{6,7},{7,6},{8,9},{9,8},{10,11... | collective-permute-start | bytes 1179656 | tf_op jit(solution)/shard_map/ppermute | solution.py:131
  37.5 0.7 %shard_map.43 = (bf16[3,256,768]{2,1,0:T(8,128)(2,1)S(1)}, bf16[128,768]{1,0:T(8,128)(2,1)S(1)}) custom-call(bf16[384,512]{1,0:T(8,128)(2,1)S(1)} %get-tuple-element.25.keep_ref, f32[384,1]{1,0:T(8,128)S(1)} %get-tuple-element.27.column_ref, f32[1,768]{1,0:T(1,128)S(1)} %get-tuple-element.28.row_ref), custom_call_target="tpu_custom_call" | custom-call | flops 75497472 | bytes 589824 | tf_op jit(solution)/shard_map/pallas_call | solution.py:473
  38.9 2.3 %shard_map.44 = bf16[384,512]{1,0:T(8,128)(2,1)} custom-call(bf16[384,512]{1,0:T(8,128)(2,1)S(1)} %get-tuple-element.25.keep_ref, bf16[384,512]{1,0:T(8,128)(2,1)S(1)} %collective-permute-done.15.recv_ref, bf16[3,256,768]{2,1,0:T(8,128)(2,1)S(1)} %get-tuple-element.29.probs_ref, bf16[128,768]{1,0:T(8,128)(2,1)S(1)} %get-tuple-element.30.keys_ref, ...), custom_call_target="tpu_custom_call" | custom-call | flops 603979776 | bytes 1572864 | tf_op jit(solution)/shard_map/pallas_call | solution.py:488
  (26 shorter events, 4.3 us)
Async XLA Ops:
  0.9 22.3 %collective-permute-start = (bf16[384,4096]{1,0:T(8,128)(2,1)}, bf16[384,4096]{1,0:T(8,128)(2,1)S(1)}, u32[]{:S(2)}, u32[]{:S(2)}) collective-permute-start(bf16[384,4096]{1,0:T(8,128)(2,1)} %bitcast.4), channel_id=1, source_target_pairs={{0,1},{1,0},{2,3},{3,2},{4,5},{5,4},{6,7},{7,6},{8,9},{9,8},{10,11... | collective-permute-start | bytes 9437192 | tf_op jit(solution)/shard_map/ppermute | solution.py:131
  1.1 13.3 %collective-permute-start.2 = (bf16[256,384]{1,0:T(8,128)(2,1)S(1)}, bf16[256,384]{1,0:T(8,128)(2,1)}, u32[]{:S(2)}, u32[]{:S(2)}) collective-permute-start(bf16[256,384]{1,0:T(8,128)(2,1)S(1)} %shard_map.37.refs_2_), channel_id=1, source_target_pairs={{0,16},{1,17},{2,18},{3,19},{4,20},{5,21},{6,22},{7,23},{8,24},{9,... | collective-permute-start | bytes 589832 | tf_op jit(solution)/shard_map/ppermute | solution.py:127
  4.8 11.7 %collective-permute-start.9 = (bf16[256,384]{1,0:T(8,128)(2,1)S(1)}, bf16[256,384]{1,0:T(8,128)(2,1)}, u32[]{:S(2)}, u32[]{:S(2)}) collective-permute-start(bf16[256,384]{1,0:T(8,128)(2,1)S(1)} %shard_map.37.refs_2_), channel_id=1, source_target_pairs={{0,8},{1,9},{2,10},{3,11},{4,12},{5,13},{6,14},{7,15},{8,0},{9,1},... | collective-permute-start | bytes 589832 | tf_op jit(solution)/shard_map/ppermute | solution.py:127
  6.1 4.9 %collective-permute-start.11 = (bf16[256,384]{1,0:T(8,128)(2,1)S(1)}, bf16[256,384]{1,0:T(8,128)(2,1)S(1)}, u32[]{:S(2)}, u32[]{:S(2)}) collective-permute-start(bf16[256,384]{1,0:T(8,128)(2,1)S(1)} %shard_map.37.refs_2_), channel_id=1, source_target_pairs={{0,2},{1,5},{2,0},{3,7},{4,6},{5,1},{6,4},{7,3},{8,10},{9,13},{10,... | collective-permute-start | bytes 589832 | tf_op jit(solution)/shard_map/ppermute | solution.py:127
  7.4 7.8 %collective-permute-start.1 = (s32[1,384]{1,0:T(1,128)}, s32[1,384]{1,0:T(1,128)S(1)}, u32[]{:S(2)}, u32[]{:S(2)}) collective-permute-start(s32[1,384]{1,0:T(1,128)} %docs_ref.1), channel_id=1, source_target_pairs={{0,1},{1,0},{2,3},{3,2},{4,5},{5,4},{6,7},{7,6},{8,9},{9,8},{10,11... | collective-permute-start | bytes 4616 | tf_op jit(solution)/shard_map/ppermute | solution.py:131
  11.1 7.0 %collective-permute-start.13 = (bf16[512,384]{1,0:T(8,128)(2,1)S(1)}, bf16[512,384]{1,0:T(8,128)(2,1)S(1)}, u32[]{:S(2)}, u32[]{:S(2)}) collective-permute-start(bf16[512,384]{1,0:T(8,128)(2,1)S(1)} %pad_maximum_fusion.2), channel_id=1, source_target_pairs={{0,4},{1,3},{2,6},{3,1},{4,0},{5,7},{6,2},{7,5},{8,12},{9,11},{10,... | collective-permute-start | bytes 1179656 | tf_op jit(solution)/shard_map/ppermute | solution.py:127
  13.8 9.7 %copy-start.1 = (s32[1,384]{1,0:T(1,128)S(1)}, s32[1,384]{1,0:T(1,128)}, u32[]{:S(2)}) copy-start(s32[1,384]{1,0:T(1,128)} %docs_ref.1) | copy-start | bytes 4612
  14.4 5.4 %collective-permute-start.3 = (bf16[256,384]{1,0:T(8,128)(2,1)}, bf16[256,384]{1,0:T(8,128)(2,1)S(1)}, u32[]{:S(2)}, u32[]{:S(2)}) collective-permute-start(bf16[256,384]{1,0:T(8,128)(2,1)} %collective-permute-done.2.refs_3_), channel_id=1, source_target_pairs={{0,8},{1,9},{2,10},{3,11},{4,12},{5,13},{6,14},{7,15},{8,0},{9,1},... | collective-permute-start | bytes 589832 | tf_op jit(solution)/shard_map/ppermute | solution.py:127
  15.2 8.8 %copy-start = (bf16[1,384,4096]{2,1,0:T(8,128)(2,1)S(1)}, bf16[1,384,4096]{2,1,0:T(8,128)(2,1)}, u32[]{:S(2)}) copy-start(bf16[1,384,4096]{2,1,0:T(8,128)(2,1)} %param.3) | copy-start | bytes 9437188
  15.2 6.8 %collective-permute-start.7 = (bf16[256,384]{1,0:T(8,128)(2,1)}, bf16[256,384]{1,0:T(8,128)(2,1)S(1)}, u32[]{:S(2)}, u32[]{:S(2)}) collective-permute-start(bf16[256,384]{1,0:T(8,128)(2,1)} %collective-permute-done.2.refs_3_), channel_id=1, source_target_pairs={{0,2},{1,5},{2,0},{3,7},{4,6},{5,1},{6,4},{7,3},{8,10},{9,13},{10,... | collective-permute-start | bytes 589832 | tf_op jit(solution)/shard_map/ppermute | solution.py:127
  16.5 7.5 %collective-permute-start.10 = (bf16[256,384]{1,0:T(8,128)(2,1)}, bf16[256,384]{1,0:T(8,128)(2,1)S(1)}, u32[]{:S(2)}, u32[]{:S(2)}) collective-permute-start(bf16[256,384]{1,0:T(8,128)(2,1)} %collective-permute-done.9.refs_7_), channel_id=1, source_target_pairs={{0,2},{1,5},{2,0},{3,7},{4,6},{5,1},{6,4},{7,3},{8,10},{9,13},{10,... | collective-permute-start | bytes 589832 | tf_op jit(solution)/shard_map/ppermute | solution.py:127
  18.1 10.3 %collective-permute-start.14 = (bf16[512,384]{1,0:T(8,128)(2,1)S(1)}, bf16[512,384]{1,0:T(8,128)(2,1)S(1)}, u32[]{:S(2)}, u32[]{:S(2)}) collective-permute-start(bf16[512,384]{1,0:T(8,128)(2,1)S(1)} %collective-permute-done.13.refs_2_), channel_id=1, source_target_pairs={{0,8},{1,9},{2,10},{3,11},{4,12},{5,13},{6,14},{7,15},{8,0},{9,1},... | collective-permute-start | bytes 1179656 | tf_op jit(solution)/shard_map/ppermute | solution.py:127
  19.8 8.4 %collective-permute-start.4 = (bf16[256,384]{1,0:T(8,128)(2,1)S(1)}, bf16[256,384]{1,0:T(8,128)(2,1)S(1)}, u32[]{:S(2)}, u32[]{:S(2)}) collective-permute-start(bf16[256,384]{1,0:T(8,128)(2,1)S(1)} %collective-permute-done.3.refs_5_), channel_id=1, source_target_pairs={{0,2},{1,5},{2,0},{3,7},{4,6},{5,1},{6,4},{7,3},{8,10},{9,13},{10,... | collective-permute-start | bytes 589832 | tf_op jit(solution)/shard_map/ppermute | solution.py:127
  22.0 7.6 %collective-permute-start.6 = (bf16[256,384]{1,0:T(8,128)(2,1)}, bf16[256,384]{1,0:T(8,128)(2,1)S(1)}, u32[]{:S(2)}, u32[]{:S(2)}) collective-permute-start(bf16[256,384]{1,0:T(8,128)(2,1)} %collective-permute-done.2.refs_3_), channel_id=1, source_target_pairs={{0,4},{1,3},{2,6},{3,1},{4,0},{5,7},{6,2},{7,5},{8,12},{9,11},{10,... | collective-permute-start | bytes 589832 | tf_op jit(solution)/shard_map/ppermute | solution.py:127
  23.2 8.0 %collective-permute-start.8 = (bf16[256,384]{1,0:T(8,128)(2,1)S(1)}, bf16[256,384]{1,0:T(8,128)(2,1)S(1)}, u32[]{:S(2)}, u32[]{:S(2)}) collective-permute-start(bf16[256,384]{1,0:T(8,128)(2,1)S(1)} %collective-permute-done.7.refs_4_), channel_id=1, source_target_pairs={{0,4},{1,3},{2,6},{3,1},{4,0},{5,7},{6,2},{7,5},{8,12},{9,11},{10,... | collective-permute-start | bytes 589832 | tf_op jit(solution)/shard_map/ppermute | solution.py:127
  26.9 6.5 %collective-permute-start.12 = (bf16[256,384]{1,0:T(8,128)(2,1)S(1)}, bf16[256,384]{1,0:T(8,128)(2,1)S(1)}, u32[]{:S(2)}, u32[]{:S(2)}) collective-permute-start(bf16[256,384]{1,0:T(8,128)(2,1)S(1)} %collective-permute-done.3.refs_5_), channel_id=1, source_target_pairs={{0,4},{1,3},{2,6},{3,1},{4,0},{5,7},{6,2},{7,5},{8,12},{9,11},{10,... | collective-permute-start | bytes 589832 | tf_op jit(solution)/shard_map/ppermute | solution.py:127
  28.1 7.3 %collective-permute-start.5 = (bf16[256,384]{1,0:T(8,128)(2,1)S(1)}, bf16[256,384]{1,0:T(8,128)(2,1)S(1)}, u32[]{:S(2)}, u32[]{:S(2)}) collective-permute-start(bf16[256,384]{1,0:T(8,128)(2,1)S(1)} %collective-permute-done.4.refs_4_), channel_id=1, source_target_pairs={{0,4},{1,3},{2,6},{3,1},{4,0},{5,7},{6,2},{7,5},{8,12},{9,11},{10,... | collective-permute-start | bytes 589832 | tf_op jit(solution)/shard_map/ppermute | solution.py:127
  36.0 2.9 %collective-permute-start.15 = (bf16[384,512]{1,0:T(8,128)(2,1)S(1)}, bf16[384,512]{1,0:T(8,128)(2,1)S(1)}, u32[]{:S(2)}, u32[]{:S(2)}) collective-permute-start(bf16[384,512]{1,0:T(8,128)(2,1)S(1)} %get-tuple-element.26), channel_id=1, source_target_pairs={{0,1},{1,0},{2,3},{3,2},{4,5},{5,4},{6,7},{7,6},{8,9},{9,8},{10,11... | collective-permute-start | bytes 1179656 | tf_op jit(solution)/shard_map/ppermute | solution.py:131

commit v7 on v5

--- a/solution.py
+++ b/solution.py
@@ -16,7 +16,7 @@
 
 STEP = 128
 
-OWN_PARTS = 4
+OWN_PARTS = 1
 
 VMEM_LIMIT = 16 * 1024 * 1024
 

time: 41.4 us -> 41.3 us (level)
  no operation moved by 1% of the time
where the time goes in v7:
time: 41.3 us; the launch traced here: 41.2 us
  starting transfers between devices  16.7 us (40%)
  waiting for transfers between devices  12.9 us (31%)
  Pallas kernels  9.52 us (23%)
  other arithmetic  1.91 us (5%)
    ppermute x13, starting transfers between devices, flip(): return lax.ppermute(value, ('fsdp', 'ctx'), pairs)  14.1 us
    ppermute x13, waiting for transfers between devices, flip(): return lax.ppermute(value, ('fsdp', 'ctx'), pairs)  12.3 us
    pallas_call x3, Pallas kernels, partial(): pl.pallas_call(functools.partial(partial_kernel, masks, late, begun), out...  4.85 us
    ppermute x3, starting transfers between devices, swap(): return lax.ppermute(value, 'ctx', [(0, 1), (1, 0)])  2.58 us
    pallas_call x1, Pallas kernels, paired_body(): pl.pallas_call(attention_kernel, out_shape=jax.ShapeDtypeStruct((tokens,...  2.14 us
    neg x1, other arithmetic, paired_body(): sines = jnp.concatenate([-sine, sine], axis=-1)  1.44 us
    pallas_call x1, Pallas kernels, own_columns(): pl.pallas_call(own_kernel, out_shape=jax.ShapeDtypeStruct((weight.shape[0...  0.92 us
  transfers between devices with their start and end apart: 16, of which 10 were waited for; matrix products, arithmetic and copies ran while one was open for 5% of the time, Pallas kernels for 17%

profile of v7, /device:TPU:1, one launch (start us, length us, event | category | flops | bytes accessed | tf_op | source)
XLA Modules:
  0.0 41.2 jit_solution(14563672071944115890)
XLA Ops:
  0.1 0.9 %shard_map.38.refs_2_ = bf16[256,384]{1,0:T(8,128)(2,1)S(1)} custom-call(bf16[256,768]{1,0:T(8,128)(2,1)} %weight_ref.1), custom_call_target="tpu_custom_call" | custom-call | tf_op jit(solution)/shard_map/pallas_call | solution.py:373
  1.0 3.8 %collective-permute-start.2 = (bf16[256,384]{1,0:T(8,128)(2,1)S(1)}, bf16[256,384]{1,0:T(8,128)(2,1)}, u32[]{:S(2)}, u32[]{:S(2)}) collective-permute-start(bf16[256,384]{1,0:T(8,128)(2,1)S(1)} %shard_map.38.refs_2_), channel_id=1, source_target_pairs={{0,16},{1,17},{2,18},{3,19},{4,20},{5,21},{6,22},{7,23},{8,24},{9,... | collective-permute-start | bytes 589832 | tf_op jit(solution)/shard_map/ppermute | solution.py:127
  4.8 1.3 %collective-permute-start.11 = (bf16[256,384]{1,0:T(8,128)(2,1)S(1)}, bf16[256,384]{1,0:T(8,128)(2,1)}, u32[]{:S(2)}, u32[]{:S(2)}) collective-permute-start(bf16[256,384]{1,0:T(8,128)(2,1)S(1)} %shard_map.38.refs_2_), channel_id=1, source_target_pairs={{0,8},{1,9},{2,10},{3,11},{4,12},{5,13},{6,14},{7,15},{8,0},{9,1},... | collective-permute-start | bytes 589832 | tf_op jit(solution)/shard_map/ppermute | solution.py:127
  6.1 1.2 %collective-permute-start.6 = (bf16[256,384]{1,0:T(8,128)(2,1)S(1)}, bf16[256,384]{1,0:T(8,128)(2,1)S(1)}, u32[]{:S(2)}, u32[]{:S(2)}) collective-permute-start(bf16[256,384]{1,0:T(8,128)(2,1)S(1)} %shard_map.38.refs_2_), channel_id=1, source_target_pairs={{0,2},{1,5},{2,0},{3,7},{4,6},{5,1},{6,4},{7,3},{8,10},{9,13},{10,... | collective-permute-start | bytes 589832 | tf_op jit(solution)/shard_map/ppermute | solution.py:127
  7.3 0.8 %collective-permute-start.1 = (s32[1,384]{1,0:T(1,128)}, s32[1,384]{1,0:T(1,128)S(1)}, u32[]{:S(2)}, u32[]{:S(2)}) collective-permute-start(s32[1,384]{1,0:T(1,128)} %docs_ref.1), channel_id=1, source_target_pairs={{0,1},{1,0},{2,3},{3,2},{4,5},{5,4},{6,7},{7,6},{8,9},{9,8},{10,11... | collective-permute-start | bytes 4616 | tf_op jit(solution)/shard_map/ppermute | solution.py:131
  8.3 2.7 %collective-permute-done.6.refs_8_ = bf16[256,384]{1,0:T(8,128)(2,1)S(1)} collective-permute-done((bf16[256,384]{1,0:T(8,128)(2,1)S(1)}, bf16[256,384]{1,0:T(8,128)(2,1)S(1)}, u32[]{:S(2)}, u32[]{:S(2)}) %collective-permute-start.6) | collective-permute-done | bytes 196640 | tf_op jit(solution)/shard_map/ppermute | solution.py:127
  11.1 1.3 %collective-permute-start.7 = (bf16[512,384]{1,0:T(8,128)(2,1)S(1)}, bf16[512,384]{1,0:T(8,128)(2,1)S(1)}, u32[]{:S(2)}, u32[]{:S(2)}) collective-permute-start(bf16[512,384]{1,0:T(8,128)(2,1)S(1)} %pad_maximum_fusion), channel_id=1, source_target_pairs={{0,4},{1,3},{2,6},{3,1},{4,0},{5,7},{6,2},{7,5},{8,12},{9,11},{10,... | collective-permute-start | bytes 1179656 | tf_op jit(solution)/shard_map/ppermute | solution.py:127
  12.3 1.4 %fusion = (f32[2,384,64]{2,1,0:T(8,128)S(1)}, f32[2,384,64]{2,1,0:T(8,128)S(1)}, f32[2,384,64]{2,1,0:T(8,128)S(1)}) fusion(f32[64]{0:T(128)S(1)} %multiply_exponential_fusion, f32[2,384]{1,0:T(2,128)S(1)} %add_convert_fusion), kind=kLoop, calls=%fused_computation.5 | loop fusion | flops 98304 | bytes 593152 | tf_op jit(solution)/shard_map/neg | solution.py:437
  15.2 1.3 %collective-permute-start.9 = (bf16[256,384]{1,0:T(8,128)(2,1)}, bf16[256,384]{1,0:T(8,128)(2,1)S(1)}, u32[]{:S(2)}, u32[]{:S(2)}) collective-permute-start(bf16[256,384]{1,0:T(8,128)(2,1)} %collective-permute-done.2.refs_3_), channel_id=1, source_target_pairs={{0,2},{1,5},{2,0},{3,7},{4,6},{5,1},{6,4},{7,3},{8,10},{9,13},{10,... | collective-permute-start | bytes 589832 | tf_op jit(solution)/shard_map/ppermute | solution.py:127
  16.7 1.3 %collective-permute-done.7.refs_2_ = bf16[512,384]{1,0:T(8,128)(2,1)S(1)} collective-permute-done((bf16[512,384]{1,0:T(8,128)(2,1)S(1)}, bf16[512,384]{1,0:T(8,128)(2,1)S(1)}, u32[]{:S(2)}, u32[]{:S(2)}) %collective-permute-start.7) | collective-permute-done | bytes 393248 | tf_op jit(solution)/shard_map/ppermute | solution.py:127
  18.2 1.8 %collective-permute-done.3.refs_5_ = bf16[256,384]{1,0:T(8,128)(2,1)S(1)} collective-permute-done((bf16[256,384]{1,0:T(8,128)(2,1)}, bf16[256,384]{1,0:T(8,128)(2,1)S(1)}, u32[]{:S(2)}, u32[]{:S(2)}) %collective-permute-start.3) | collective-permute-done | bytes 196640 | tf_op jit(solution)/shard_map/ppermute | solution.py:127
  20.0 1.3 %collective-permute-start.4 = (bf16[256,384]{1,0:T(8,128)(2,1)S(1)}, bf16[256,384]{1,0:T(8,128)(2,1)S(1)}, u32[]{:S(2)}, u32[]{:S(2)}) collective-permute-start(bf16[256,384]{1,0:T(8,128)(2,1)S(1)} %collective-permute-done.3.refs_5_), channel_id=1, source_target_pairs={{0,2},{1,5},{2,0},{3,7},{4,6},{5,1},{6,4},{7,3},{8,10},{9,13},{10,... | collective-permute-start | bytes 589832 | tf_op jit(solution)/shard_map/ppermute | solution.py:127
  21.9 1.2 %collective-permute-start.14 = (bf16[256,384]{1,0:T(8,128)(2,1)}, bf16[256,384]{1,0:T(8,128)(2,1)S(1)}, u32[]{:S(2)}, u32[]{:S(2)}) collective-permute-start(bf16[256,384]{1,0:T(8,128)(2,1)} %collective-permute-done.2.refs_3_), channel_id=1, source_target_pairs={{0,4},{1,3},{2,6},{3,1},{4,0},{5,7},{6,2},{7,5},{8,12},{9,11},{10,... | collective-permute-start | bytes 589832 | tf_op jit(solution)/shard_map/ppermute | solution.py:127
  23.9 2.9 %shard_map.39.refs_5_ = f32[2,384,384]{2,1,0:T(8,128)S(1)} custom-call(bf16[384,4096]{1,0:T(8,128)(2,1)S(1)} %bitcast.5, bf16[384,4096]{1,0:T(8,128)(2,1)S(1)} %get-tuple-element.16.refs_1_, bf16[256,384]{1,0:T(8,128)(2,1)S(1)} %shard_map.38.refs_2_, bf16[256,384]{1,0:T(8,128)(2,1)} %collective-permute-done.2.refs_3_, ...), custom_call_target="tpu_custom_call" | custom-call | flops 1056964608 | bytes 6488064 | tf_op jit(solution)/shard_map/pallas_call | solution.py:402
  26.8 1.3 %collective-permute-start.13 = (bf16[256,384]{1,0:T(8,128)(2,1)S(1)}, bf16[256,384]{1,0:T(8,128)(2,1)S(1)}, u32[]{:S(2)}, u32[]{:S(2)}) collective-permute-start(bf16[256,384]{1,0:T(8,128)(2,1)S(1)} %collective-permute-done.3.refs_5_), channel_id=1, source_target_pairs={{0,4},{1,3},{2,6},{3,1},{4,0},{5,7},{6,2},{7,5},{8,12},{9,11},{10,... | collective-permute-start | bytes 589832 | tf_op jit(solution)/shard_map/ppermute | solution.py:127
  28.3 1.0 %shard_map.40.refs_5_ = f32[2,384,384]{2,1,0:T(8,128)S(1)} custom-call(bf16[384,4096]{1,0:T(8,128)(2,1)S(1)} %bitcast.6, bf16[384,4096]{1,0:T(8,128)(2,1)S(1)} %get-tuple-element.16.refs_1_, bf16[512,384]{1,0:T(8,128)(2,1)S(1)} %collective-permute-done.7.refs_2_, bf16[256,384]{1,0:T(8,128)(2,1)S(1)} %collective-permute-done.14.refs_3_, ...), custom_call_target="tpu_custom_call" | custom-call | flops 603979776 | bytes 4718592 | tf_op jit(solution)/shard_map/pallas_call | solution.py:402
  29.3 1.9 %collective-permute-done.10.refs_3_ = bf16[256,384]{1,0:T(8,128)(2,1)S(1)} collective-permute-done((bf16[256,384]{1,0:T(8,128)(2,1)S(1)}, bf16[256,384]{1,0:T(8,128)(2,1)S(1)}, u32[]{:S(2)}, u32[]{:S(2)}) %collective-permute-start.10) | collective-permute-done | bytes 196640 | tf_op jit(solution)/shard_map/ppermute | solution.py:127
  31.2 2.1 %collective-permute-done.13.refs_4_ = bf16[256,384]{1,0:T(8,128)(2,1)S(1)} collective-permute-done((bf16[256,384]{1,0:T(8,128)(2,1)S(1)}, bf16[256,384]{1,0:T(8,128)(2,1)S(1)}, u32[]{:S(2)}, u32[]{:S(2)}) %collective-permute-start.13) | collective-permute-done | bytes 196640 | tf_op jit(solution)/shard_map/ppermute | solution.py:127
  33.3 1.0 %shard_map.41.refs_3_ = f32[2,384,384]{2,1,0:T(8,128)S(1)} custom-call(bf16[384,4096]{1,0:T(8,128)(2,1)S(1)} %bitcast.7, bf16[384,4096]{1,0:T(8,128)(2,1)S(1)} %get-tuple-element.16.refs_1_, bf16[512,384]{1,0:T(8,128)(2,1)S(1)} %collective-permute-done.8.refs_2_, bf16[256,384]{1,0:T(8,128)(2,1)S(1)} %collective-permute-done.10.refs_3_, ...), custom_call_target="tpu_custom_call" | custom-call | flops 603979776 | bytes 4718592 | tf_op jit(solution)/shard_map/pallas_call | solution.py:402
  34.3 1.1 %collective-permute-done.5.refs_2_ = bf16[256,384]{1,0:T(8,128)(2,1)S(1)} collective-permute-done((bf16[256,384]{1,0:T(8,128)(2,1)S(1)}, bf16[256,384]{1,0:T(8,128)(2,1)S(1)}, u32[]{:S(2)}, u32[]{:S(2)}) %collective-permute-start.5) | collective-permute-done | bytes 196640 | tf_op jit(solution)/shard_map/ppermute | solution.py:127
  36.0 1.7 %collective-permute-start.15 = (bf16[384,512]{1,0:T(8,128)(2,1)S(1)}, bf16[384,512]{1,0:T(8,128)(2,1)S(1)}, u32[]{:S(2)}, u32[]{:S(2)}) collective-permute-start(bf16[384,512]{1,0:T(8,128)(2,1)S(1)} %get-tuple-element.22), channel_id=1, source_target_pairs={{0,1},{1,0},{2,3},{3,2},{4,5},{5,4},{6,7},{7,6},{8,9},{9,8},{10,11... | collective-permute-start | bytes 1179656 | tf_op jit(solution)/shard_map/ppermute | solution.py:131
  37.7 0.7 %shard_map.43 = (bf16[3,256,768]{2,1,0:T(8,128)(2,1)S(1)}, bf16[128,768]{1,0:T(8,128)(2,1)S(1)}) custom-call(bf16[384,512]{1,0:T(8,128)(2,1)S(1)} %get-tuple-element.21.keep_ref, f32[384,1]{1,0:T(8,128)S(1)} %get-tuple-element.23.column_ref, f32[1,768]{1,0:T(1,128)S(1)} %get-tuple-element.24.row_ref), custom_call_target="tpu_custom_call" | custom-call | flops 75497472 | bytes 589824 | tf_op jit(solution)/shard_map/pallas_call | solution.py:468
  38.4 0.6 %collective-permute-done.15.recv_ref = bf16[384,512]{1,0:T(8,128)(2,1)S(1)} collective-permute-done((bf16[384,512]{1,0:T(8,128)(2,1)S(1)}, bf16[384,512]{1,0:T(8,128)(2,1)S(1)}, u32[]{:S(2)}, u32[]{:S(2)}) %collective-permute-start.15) | collective-permute-done | bytes 393248 | tf_op jit(solution)/shard_map/ppermute | solution.py:131
  39.0 2.1 %shard_map.44 = bf16[384,512]{1,0:T(8,128)(2,1)} custom-call(bf16[384,512]{1,0:T(8,128)(2,1)S(1)} %get-tuple-element.21.keep_ref, bf16[384,512]{1,0:T(8,128)(2,1)S(1)} %collective-permute-done.15.recv_ref, bf16[3,256,768]{2,1,0:T(8,128)(2,1)S(1)} %get-tuple-element.25.probs_ref, bf16[128,768]{1,0:T(8,128)(2,1)S(1)} %get-tuple-element.26.keys_ref, ...), custom_call_target="tpu_custom_call" | custom-call | flops 603979776 | bytes 1572864 | tf_op jit(solution)/shard_map/pallas_call | solution.py:483
  (26 shorter events, 4.2 us)
Async XLA Ops:
  0.0 23.2 %collective-permute-start = (bf16[384,4096]{1,0:T(8,128)(2,1)}, bf16[384,4096]{1,0:T(8,128)(2,1)S(1)}, u32[]{:S(2)}, u32[]{:S(2)}) collective-permute-start(bf16[384,4096]{1,0:T(8,128)(2,1)} %bitcast.4), channel_id=1, source_target_pairs={{0,1},{1,0},{2,3},{3,2},{4,5},{5,4},{6,7},{7,6},{8,9},{9,8},{10,11... | collective-permute-start | bytes 9437192 | tf_op jit(solution)/shard_map/ppermute | solution.py:131
  1.0 13.5 %collective-permute-start.2 = (bf16[256,384]{1,0:T(8,128)(2,1)S(1)}, bf16[256,384]{1,0:T(8,128)(2,1)}, u32[]{:S(2)}, u32[]{:S(2)}) collective-permute-start(bf16[256,384]{1,0:T(8,128)(2,1)S(1)} %shard_map.38.refs_2_), channel_id=1, source_target_pairs={{0,16},{1,17},{2,18},{3,19},{4,20},{5,21},{6,22},{7,23},{8,24},{9,... | collective-permute-start | bytes 589832 | tf_op jit(solution)/shard_map/ppermute | solution.py:127
  4.8 11.7 %collective-permute-start.11 = (bf16[256,384]{1,0:T(8,128)(2,1)S(1)}, bf16[256,384]{1,0:T(8,128)(2,1)}, u32[]{:S(2)}, u32[]{:S(2)}) collective-permute-start(bf16[256,384]{1,0:T(8,128)(2,1)S(1)} %shard_map.38.refs_2_), channel_id=1, source_target_pairs={{0,8},{1,9},{2,10},{3,11},{4,12},{5,13},{6,14},{7,15},{8,0},{9,1},... | collective-permute-start | bytes 589832 | tf_op jit(solution)/shard_map/ppermute | solution.py:127
  6.1 4.9 %collective-permute-start.6 = (bf16[256,384]{1,0:T(8,128)(2,1)S(1)}, bf16[256,384]{1,0:T(8,128)(2,1)S(1)}, u32[]{:S(2)}, u32[]{:S(2)}) collective-permute-start(bf16[256,384]{1,0:T(8,128)(2,1)S(1)} %shard_map.38.refs_2_), channel_id=1, source_target_pairs={{0,2},{1,5},{2,0},{3,7},{4,6},{5,1},{6,4},{7,3},{8,10},{9,13},{10,... | collective-permute-start | bytes 589832 | tf_op jit(solution)/shard_map/ppermute | solution.py:127
  7.3 7.8 %collective-permute-start.1 = (s32[1,384]{1,0:T(1,128)}, s32[1,384]{1,0:T(1,128)S(1)}, u32[]{:S(2)}, u32[]{:S(2)}) collective-permute-start(s32[1,384]{1,0:T(1,128)} %docs_ref.1), channel_id=1, source_target_pairs={{0,1},{1,0},{2,3},{3,2},{4,5},{5,4},{6,7},{7,6},{8,9},{9,8},{10,11... | collective-permute-start | bytes 4616 | tf_op jit(solution)/shard_map/ppermute | solution.py:131
  11.1 7.0 %collective-permute-start.7 = (bf16[512,384]{1,0:T(8,128)(2,1)S(1)}, bf16[512,384]{1,0:T(8,128)(2,1)S(1)}, u32[]{:S(2)}, u32[]{:S(2)}) collective-permute-start(bf16[512,384]{1,0:T(8,128)(2,1)S(1)} %pad_maximum_fusion), channel_id=1, source_target_pairs={{0,4},{1,3},{2,6},{3,1},{4,0},{5,7},{6,2},{7,5},{8,12},{9,11},{10,... | collective-permute-start | bytes 1179656 | tf_op jit(solution)/shard_map/ppermute | solution.py:127
  13.8 9.6 %copy-start.1 = (s32[1,384]{1,0:T(1,128)S(1)}, s32[1,384]{1,0:T(1,128)}, u32[]{:S(2)}) copy-start(s32[1,384]{1,0:T(1,128)} %docs_ref.1) | copy-start | bytes 4612
  14.4 5.5 %collective-permute-start.3 = (bf16[256,384]{1,0:T(8,128)(2,1)}, bf16[256,384]{1,0:T(8,128)(2,1)S(1)}, u32[]{:S(2)}, u32[]{:S(2)}) collective-permute-start(bf16[256,384]{1,0:T(8,128)(2,1)} %collective-permute-done.2.refs_3_), channel_id=1, source_target_pairs={{0,8},{1,9},{2,10},{3,11},{4,12},{5,13},{6,14},{7,15},{8,0},{9,1},... | collective-permute-start | bytes 589832 | tf_op jit(solution)/shard_map/ppermute | solution.py:127
  15.2 8.8 %copy-start = (bf16[1,384,4096]{2,1,0:T(8,128)(2,1)S(1)}, bf16[1,384,4096]{2,1,0:T(8,128)(2,1)}, u32[]{:S(2)}) copy-start(bf16[1,384,4096]{2,1,0:T(8,128)(2,1)} %param.3) | copy-start | bytes 9437188
  15.2 6.8 %collective-permute-start.9 = (bf16[256,384]{1,0:T(8,128)(2,1)}, bf16[256,384]{1,0:T(8,128)(2,1)S(1)}, u32[]{:S(2)}, u32[]{:S(2)}) collective-permute-start(bf16[256,384]{1,0:T(8,128)(2,1)} %collective-permute-done.2.refs_3_), channel_id=1, source_target_pairs={{0,2},{1,5},{2,0},{3,7},{4,6},{5,1},{6,4},{7,3},{8,10},{9,13},{10,... | collective-permute-start | bytes 589832 | tf_op jit(solution)/shard_map/ppermute | solution.py:127
  16.5 7.4 %collective-permute-start.12 = (bf16[256,384]{1,0:T(8,128)(2,1)}, bf16[256,384]{1,0:T(8,128)(2,1)S(1)}, u32[]{:S(2)}, u32[]{:S(2)}) collective-permute-start(bf16[256,384]{1,0:T(8,128)(2,1)} %collective-permute-done.11.refs_7_), channel_id=1, source_target_pairs={{0,2},{1,5},{2,0},{3,7},{4,6},{5,1},{6,4},{7,3},{8,10},{9,13},{10,... | collective-permute-start | bytes 589832 | tf_op jit(solution)/shard_map/ppermute | solution.py:127
  18.1 13.1 %collective-permute-start.8 = (bf16[512,384]{1,0:T(8,128)(2,1)S(1)}, bf16[512,384]{1,0:T(8,128)(2,1)S(1)}, u32[]{:S(2)}, u32[]{:S(2)}) collective-permute-start(bf16[512,384]{1,0:T(8,128)(2,1)S(1)} %collective-permute-done.7.refs_2_), channel_id=1, source_target_pairs={{0,8},{1,9},{2,10},{3,11},{4,12},{5,13},{6,14},{7,15},{8,0},{9,1},... | collective-permute-start | bytes 1179656 | tf_op jit(solution)/shard_map/ppermute | solution.py:127
  20.0 8.1 %collective-permute-start.4 = (bf16[256,384]{1,0:T(8,128)(2,1)S(1)}, bf16[256,384]{1,0:T(8,128)(2,1)S(1)}, u32[]{:S(2)}, u32[]{:S(2)}) collective-permute-start(bf16[256,384]{1,0:T(8,128)(2,1)S(1)} %collective-permute-done.3.refs_5_), channel_id=1, source_target_pairs={{0,2},{1,5},{2,0},{3,7},{4,6},{5,1},{6,4},{7,3},{8,10},{9,13},{10,... | collective-permute-start | bytes 589832 | tf_op jit(solution)/shard_map/ppermute | solution.py:127
  21.9 6.4 %collective-permute-start.14 = (bf16[256,384]{1,0:T(8,128)(2,1)}, bf16[256,384]{1,0:T(8,128)(2,1)S(1)}, u32[]{:S(2)}, u32[]{:S(2)}) collective-permute-start(bf16[256,384]{1,0:T(8,128)(2,1)} %collective-permute-done.2.refs_3_), channel_id=1, source_target_pairs={{0,4},{1,3},{2,6},{3,1},{4,0},{5,7},{6,2},{7,5},{8,12},{9,11},{10,... | collective-permute-start | bytes 589832 | tf_op jit(solution)/shard_map/ppermute | solution.py:127
  23.2 8.0 %collective-permute-start.10 = (bf16[256,384]{1,0:T(8,128)(2,1)S(1)}, bf16[256,384]{1,0:T(8,128)(2,1)S(1)}, u32[]{:S(2)}, u32[]{:S(2)}) collective-permute-start(bf16[256,384]{1,0:T(8,128)(2,1)S(1)} %collective-permute-done.9.refs_4_), channel_id=1, source_target_pairs={{0,4},{1,3},{2,6},{3,1},{4,0},{5,7},{6,2},{7,5},{8,12},{9,11},{10,... | collective-permute-start | bytes 589832 | tf_op jit(solution)/shard_map/ppermute | solution.py:127
  26.8 6.5 %collective-permute-start.13 = (bf16[256,384]{1,0:T(8,128)(2,1)S(1)}, bf16[256,384]{1,0:T(8,128)(2,1)S(1)}, u32[]{:S(2)}, u32[]{:S(2)}) collective-permute-start(bf16[256,384]{1,0:T(8,128)(2,1)S(1)} %collective-permute-done.3.refs_5_), channel_id=1, source_target_pairs={{0,4},{1,3},{2,6},{3,1},{4,0},{5,7},{6,2},{7,5},{8,12},{9,11},{10,... | collective-permute-start | bytes 589832 | tf_op jit(solution)/shard_map/ppermute | solution.py:127
  28.1 7.3 %collective-permute-start.5 = (bf16[256,384]{1,0:T(8,128)(2,1)S(1)}, bf16[256,384]{1,0:T(8,128)(2,1)S(1)}, u32[]{:S(2)}, u32[]{:S(2)}) collective-permute-start(bf16[256,384]{1,0:T(8,128)(2,1)S(1)} %collective-permute-done.4.refs_4_), channel_id=1, source_target_pairs={{0,4},{1,3},{2,6},{3,1},{4,0},{5,7},{6,2},{7,5},{8,12},{9,11},{10,... | collective-permute-start | bytes 589832 | tf_op jit(solution)/shard_map/ppermute | solution.py:127
  36.0 3.1 %collective-permute-start.15 = (bf16[384,512]{1,0:T(8,128)(2,1)S(1)}, bf16[384,512]{1,0:T(8,128)(2,1)S(1)}, u32[]{:S(2)}, u32[]{:S(2)}) collective-permute-start(bf16[384,512]{1,0:T(8,128)(2,1)S(1)} %get-tuple-element.22), channel_id=1, source_target_pairs={{0,1},{1,0},{2,3},{3,2},{4,5},{5,4},{6,7},{7,6},{8,9},{9,8},{10,11... | collective-permute-start | bytes 1179656 | tf_op jit(solution)/shard_map/ppermute | solution.py:131
